TPU v7x, 128 devices: a whole 4x4x4 slice. The times are simulated.
128 devices in a mesh: pipe: 16 (over y_lo, x, core), tensor: 8 (over y_hi, z).
Axes of the slice: x: 4, y: 4 (y_hi: 2, y_lo: 2; y = y_hi * 2 + y_lo), z: 4, core: 2. Of those that a mesh axis runs over, the one named last changes fastest.
Arguments:
- forward_in: bfloat16 [16, 128, 4096], P('pipe', 'tensor'), may hold values from -21 to 21
- entering: bfloat16 [128, 4096], P('tensor'), may hold values from -21 to 21
- backward_in: bfloat16 [16, 128, 4096], P('pipe', 'tensor'), may hold values from -1.5 to 1.5
- loss_grad: bfloat16 [128, 4096], P('tensor'), may hold values from -1.5 to 1.5
- stashed: bfloat16 [16, 2, 128, 4096], P('pipe'), may hold values from -21 to 21
- norm_gain: float32 [16, 4096], P('pipe'), may hold values from 0.5 to 1.5
- w_query: bfloat16 [16, 4096, 4096], P('pipe', None, 'tensor'), may hold values from -0.09375 to 0.09375
- key_projection: bfloat16 [16, 4096, 1024], P('pipe', None, 'tensor'), may hold values from -0.09375 to 0.09375
- value_projection: bfloat16 [16, 4096, 1024], P('pipe', None, 'tensor'), may hold values from -0.09375 to 0.09375
- w_out: bfloat16 [16, 4096, 4096], P('pipe', 'tensor'), may hold values from -0.25 to 0.25
Outputs:
- forward_out: bfloat16 [2, 16, 128, 4096], P(None, 'pipe', 'tensor')
- backward_out: bfloat16 [2, 16, 128, 4096], P(None, 'pipe', 'tensor')
- grad_query: bfloat16 [16, 4096, 4096], P('pipe', None, 'tensor')
- key_weight_gradient: bfloat16 [16, 4096, 1024], P('pipe', None, 'tensor')
- value_weight_gradient: bfloat16 [16, 4096, 1024], P('pipe', None, 'tensor')
- grad_out: bfloat16 [16, 4096, 4096], P('pipe', 'tensor')
- grad_gain: float32 [16, 4096], P('pipe')
All inputs are finite; a program needn't handle non-finite values.
Results may differ from a plain program's by a relative error of at most 0.029.
Values may be sent and summed in bfloat16 or wider, within the bound.
No kernel may reach another device: no remote copies, remote signals or barrier semaphores. Data moves between devices by JAX's collectives and lax.ppermute only.
A program may use at most 128 MiB of HBM per device.

v0:
```python
import jax
import jax.numpy as jnp
from jax import lax
from jax.sharding import PartitionSpec as P

HEAD_DIMENSION = 128


EPSILON = 1e-05
ROPE_BASE = 10000.0


def swapped(x, axis, distance):
    return lax.ppermute(x, axis, [(i, i ^ 1 << distance) for i in range(lax.axis_size(axis))])


def shifted(x, axis, by):
    peers = lax.axis_size(axis)
    pairs = [(i, i + by) for i in range(peers) if 0 <= i + by < peers]
    return lax.ppermute(x, axis, pairs)


def rope_tables(token_count, head_size):
    positions = jnp.arange(token_count, dtype=jnp.float32)[:, None]
    exponents = jnp.arange(head_size // 2, dtype=jnp.float32) * (2.0 / head_size)
    angles = positions * (ROPE_BASE ** (-exponents))[None, :]
    angles = jnp.concatenate([angles, angles], axis=1)
    return (jnp.cos(angles), jnp.sin(angles))


def apply_rotary(values, cosine_table, sine_table):
    half_size = values.shape[-1] // 2
    turned = jnp.concatenate([-values[..., half_size:], values[..., :half_size]], axis=-1)
    return values * cosine_table[:, None, :] + turned * sine_table[:, None, :]


def reverse_rotary(gradient, cosine_table, sine_table):
    half_size = gradient.shape[-1] // 2
    scaled = gradient * sine_table[:, None, :]
    turned = jnp.concatenate([scaled[..., half_size:], -scaled[..., :half_size]], axis=-1)
    return gradient * cosine_table[:, None, :] + turned


def own_rows(full_rows, lane_index, shard_rows):
    return lax.dynamic_slice_in_dim(full_rows, lane_index * shard_rows, shard_rows, 0)


def attend(layer_in, gain_row, w_query, key_projection, value_projection, cosine_table, sine_table):
    token_count = layer_in.shape[0]
    head_size = cosine_table.shape[1]
    query_heads = w_query.shape[1] // head_size
    key_heads = key_projection.shape[1] // head_size
    heads_per_group = query_heads // key_heads
    wide_in = layer_in.astype(jnp.float32)
    inverse = lax.rsqrt(jnp.mean(wide_in * wide_in, axis=-1, keepdims=True) + EPSILON)
    normalized_input = (wide_in * inverse * gain_row[None, :]).astype(jnp.bfloat16)
    projected_queries = jnp.dot(
        normalized_input, w_query, preferred_element_type=jnp.float32
    ).reshape(token_count, query_heads, head_size)
    projected_queries = (
        apply_rotary(projected_queries, cosine_table, sine_table)
        .astype(jnp.bfloat16)
        .reshape(token_count, key_heads, heads_per_group, head_size)
    )
    projected_keys = jnp.dot(
        normalized_input, key_projection, preferred_element_type=jnp.float32
    ).reshape(token_count, key_heads, head_size)
    projected_keys = apply_rotary(projected_keys, cosine_table, sine_table).astype(jnp.bfloat16)
    projected_values = (
        jnp.dot(normalized_input, value_projection, preferred_element_type=jnp.float32)
        .astype(jnp.bfloat16)
        .reshape(token_count, key_heads, head_size)
    )
    scores = jnp.einsum(
        "qhgd,khd->hgqk", projected_queries, projected_keys, preferred_element_type=jnp.float32
    ) * head_size ** (-0.5)
    causal = jnp.arange(token_count)[:, None] >= jnp.arange(token_count)[None, :]
    exponent_terms = jnp.where(causal, jnp.exp(scores), 0.0)
    probability = exponent_terms / jnp.sum(exponent_terms, axis=-1, keepdims=True)
    weights = probability.astype(jnp.bfloat16)
    attended = jnp.einsum(
        "hgqk,khd->qhgd", weights, projected_values, preferred_element_type=jnp.float32
    )
    attended = attended.astype(jnp.bfloat16).reshape(token_count, query_heads * head_size)
    return (
        wide_in,
        inverse,
        normalized_input,
        projected_queries,
        projected_keys,
        projected_values,
        probability,
        weights,
        attended,
    )


def section_forward(
    layer_in, gain_row, weights_all, cosine_table, sine_table, lane_index, shard_rows
):
    w_query, key_projection, value_projection, w_out = weights_all
    pieces = attend(
        layer_in, gain_row, w_query, key_projection, value_projection, cosine_table, sine_table
    )
    partial_term = jnp.dot(pieces[8], w_out, preferred_element_type=jnp.float32)
    rounded = lax.optimization_barrier(partial_term.astype(jnp.bfloat16)).astype(jnp.float32)
    summed = lax.psum(rounded.astype(jnp.bfloat16), "tensor").astype(jnp.float32)
    full_out = (pieces[0] + summed).astype(jnp.bfloat16)
    return (own_rows(full_out, lane_index, shard_rows), full_out)


def section_backward(
    stash_in, grad_rows, gain_row, weights_all, cosine_table, sine_table, lane_index, shard_rows
):
    w_query, key_projection, value_projection, w_out = weights_all
    (
        wide_in,
        inverse,
        normalized_input,
        projected_queries,
        projected_keys,
        projected_values,
        probability,
        weights,
        attended,
    ) = attend(
        stash_in, gain_row, w_query, key_projection, value_projection, cosine_table, sine_table
    )
    token_count = stash_in.shape[0]
    head_size = cosine_table.shape[1]
    key_heads = projected_keys.shape[1]
    heads_per_group = projected_queries.shape[2]
    contract_last = (((1,), (1,)), ((), ()))
    contract_first = (((0,), (0,)), ((), ()))
    attended_gradient = lax.dot_general(
        grad_rows, w_out, contract_last, preferred_element_type=jnp.float32
    ).astype(jnp.bfloat16)
    grad_w_out = lax.dot_general(
        attended, grad_rows, contract_first, preferred_element_type=jnp.float32
    )
    group_gradients = attended_gradient.reshape(token_count, key_heads, heads_per_group, head_size)
    value_weight_gradient = jnp.einsum(
        "hgqk,qhgd->khd", weights, group_gradients, preferred_element_type=jnp.float32
    )
    grad_probability = jnp.einsum(
        "qhgd,khd->hgqk", group_gradients, projected_values, preferred_element_type=jnp.float32
    )
    row_terms = jnp.sum(grad_probability * probability, axis=-1, keepdims=True)
    grad_scores = (probability * (grad_probability - row_terms) * head_size ** (-0.5)).astype(
        jnp.bfloat16
    )
    grad_query = jnp.einsum(
        "hgqk,khd->qhgd", grad_scores, projected_keys, preferred_element_type=jnp.float32
    )
    grad_query = grad_query.reshape(token_count, key_heads * heads_per_group, head_size)
    key_weight_gradient = jnp.einsum(
        "hgqk,qhgd->khd", grad_scores, projected_queries, preferred_element_type=jnp.float32
    )
    grad_query = (
        reverse_rotary(grad_query, cosine_table, sine_table)
        .astype(jnp.bfloat16)
        .reshape(token_count, -1)
    )
    key_weight_gradient = (
        reverse_rotary(key_weight_gradient, cosine_table, sine_table)
        .astype(jnp.bfloat16)
        .reshape(token_count, -1)
    )
    value_weight_gradient = value_weight_gradient.astype(jnp.bfloat16).reshape(token_count, -1)
    grad_w_query = lax.dot_general(
        normalized_input, grad_query, contract_first, preferred_element_type=jnp.float32
    )
    grad_w_key = lax.dot_general(
        normalized_input, key_weight_gradient, contract_first, preferred_element_type=jnp.float32
    )
    grad_w_value = lax.dot_general(
        normalized_input, value_weight_gradient, contract_first, preferred_element_type=jnp.float32
    )
    partial_term = lax.dot_general(
        grad_query, w_query, contract_last, preferred_element_type=jnp.float32
    )
    partial_term = partial_term + lax.dot_general(
        key_weight_gradient, key_projection, contract_last, preferred_element_type=jnp.float32
    )
    partial_term = partial_term + lax.dot_general(
        value_weight_gradient, value_projection, contract_last, preferred_element_type=jnp.float32
    )
    rounded = lax.optimization_barrier(partial_term.astype(jnp.bfloat16)).astype(jnp.float32)
    grad_normed = lax.psum(rounded.astype(jnp.bfloat16), "tensor").astype(jnp.float32)
    grad_gain = jnp.sum(grad_normed * wide_in * inverse, axis=0)
    scaled_grad = grad_normed * gain_row[None, :]
    grad_in = (
        grad_rows.astype(jnp.float32)
        + inverse * scaled_grad
        - wide_in * inverse**3 * jnp.mean(scaled_grad * wide_in, axis=-1, keepdims=True)
    )
    full_back = grad_in.astype(jnp.bfloat16)
    own_back = own_rows(full_back, lane_index, shard_rows)
    return (own_back, full_back, (grad_w_query, grad_w_key, grad_w_value, grad_w_out, grad_gain))


def mirror(held):
    frequency_levels = lax.axis_size("pipe").bit_length() - 1
    for bit_index in range(frequency_levels):
        held = swapped(held, "pipe", bit_index)
    return held


def per_device(
    forward_in,
    entering,
    backward_in,
    loss_grad,
    stashed,
    norm_gain,
    w_query,
    key_projection,
    value_projection,
    w_out,
):
    sections = lax.axis_size("pipe")
    section_index = lax.axis_index("pipe")
    lane_index = lax.axis_index("tensor")
    first_in, fresh_rows, first_grad, final_grad = (
        lax.all_gather(forward_in, "tensor", axis=1, tiled=True),
        lax.all_gather(entering, "tensor", axis=0, tiled=True),
        lax.all_gather(backward_in, "tensor", axis=1, tiled=True),
        lax.all_gather(loss_grad, "tensor", axis=0, tiled=True),
    )
    first_in = first_in[0]
    first_grad = first_grad[0]
    token_count = first_in.shape[0]
    shard_rows = forward_in.shape[1]
    gain_row = norm_gain[0]
    weights_all = (w_query[0], key_projection[0], value_projection[0], w_out[0])
    cosine_table, sine_table = rope_tables(token_count, HEAD_DIMENSION)
    saved = mirror(stashed[0])
    first_own, first_full = section_forward(
        first_in, gain_row, weights_all, cosine_table, sine_table, lane_index, shard_rows
    )
    first_back_own, first_back_full, grads_first = section_backward(
        saved[0],
        first_grad,
        gain_row,
        weights_all,
        cosine_table,
        sine_table,
        lane_index,
        shard_rows,
    )
    arriving = shifted(first_full, "pipe", 1)
    returning = shifted(first_back_full, "pipe", -1)
    second_in = jnp.where(section_index == 0, fresh_rows, arriving)
    second_grad = jnp.where(section_index == sections - 1, final_grad, returning)
    second_own, second_full = section_forward(
        second_in, gain_row, weights_all, cosine_table, sine_table, lane_index, shard_rows
    )
    second_back_own, second_back_full, grads_second = section_backward(
        saved[1],
        second_grad,
        gain_row,
        weights_all,
        cosine_table,
        sine_table,
        lane_index,
        shard_rows,
    )
    forward_out = jnp.stack([first_own, second_own])[:, None]
    backward_out = jnp.stack([first_back_own, second_back_own])[:, None]
    grad_query = (grads_first[0] + grads_second[0]).astype(jnp.bfloat16)[None]
    key_weight_gradient = (grads_first[1] + grads_second[1]).astype(jnp.bfloat16)[None]
    value_weight_gradient = (grads_first[2] + grads_second[2]).astype(jnp.bfloat16)[None]
    grad_out = (grads_first[3] + grads_second[3]).astype(jnp.bfloat16)[None]
    grad_gain = (grads_first[4] + grads_second[4])[None]
    return (
        forward_out,
        backward_out,
        grad_query,
        key_weight_gradient,
        value_weight_gradient,
        grad_out,
        grad_gain,
    )


def solution(mesh):
    in_specs = (
        P("pipe", "tensor", None),
        P("tensor", None),
        P("pipe", "tensor", None),
        P("tensor", None),
        P("pipe", None, None, None),
        P("pipe", None),
        P("pipe", None, "tensor"),
        P("pipe", None, "tensor"),
        P("pipe", None, "tensor"),
        P("pipe", "tensor", None),
    )
    out_specs = (
        P(None, "pipe", "tensor", None),
        P(None, "pipe", "tensor", None),
        P("pipe", None, "tensor"),
        P("pipe", None, "tensor"),
        P("pipe", None, "tensor"),
        P("pipe", "tensor", None),
        P("pipe", None),
    )
    return jax.shard_map(
        per_device, mesh=mesh, in_specs=in_specs, out_specs=out_specs, check_vma=False
    )
```

profile of v0, /device:TPU:0, one launch (start us, length us, event | category | flops | bytes accessed | tf_op | source)
XLA Modules:
  0.0 495.2 jit_solution(17137004698345270266)
XLA Ops:
  7.3 4.5 collective-permute-done.1
  13.5 46.2 %collective-permute-done.2 = bf16[2,128,4096]{2,1,0:T(8,128)(2,1)S(1)} collective-permute-done((bf16[2,128,4096]{2,1,0:T(8,128)(2,1)}, bf16[2,128,4096]{2,1,0:T(8,128)(2,1)S(1)}, u32[]{:S(2)}, u32[]{:S(2)}) %collective-permute-start.2) | collective-permute-done | bytes 2097184 | tf_op jit(solution)/shard_map/ppermute | solution.py:14
  59.7 3.1 collective-permute-start.3
  62.9 6.3 %copy.71 = bf16[512,4096]{1,0:T(8,128)(2,1)} copy(bf16[512,4096]{0,1:T(8,128)(2,1)} %bitcast.385) | data formatting | bytes 8388608 | tf_op jit(solution)/shard_map/dot_general | solution.py:57
  69.2 39.0 %collective-permute-done.3 = bf16[2,128,4096]{2,1,0:T(8,128)(2,1)} collective-permute-done((bf16[2,128,4096]{2,1,0:T(8,128)(2,1)S(1)}, bf16[2,128,4096]{2,1,0:T(8,128)(2,1)}, u32[]{:S(2)}, u32[]{:S(2)}) %collective-permute-start.3) | collective-permute-done | bytes 2097184 | tf_op jit(solution)/shard_map/ppermute | solution.py:14
  108.2 1.7 collective-permute-start.4
  110.0 4.0 fusion.51
  116.4 2.2 fusion.101
  118.6 3.7 fusion.93
  122.3 32.1 %collective-permute-done.4 = bf16[2,128,4096]{2,1,0:T(8,128)(2,1)S(1)} collective-permute-done((bf16[2,128,4096]{2,1,0:T(8,128)(2,1)}, bf16[2,128,4096]{2,1,0:T(8,128)(2,1)S(1)}, u32[]{:S(2)}, u32[]{:S(2)}) %collective-permute-start.4) | collective-permute-done | bytes 2097184 | tf_op jit(solution)/shard_map/ppermute | solution.py:14
  156.6 2.0 convolution_convert_fusion.5
  158.6 4.1 convolution_convert_fusion.1
  175.0 4.7 fusion.81
  179.6 1.9 fusion.79
  181.5 1.9 fusion.84
  183.4 4.5 fusion.88
  188.0 78.8 %all-reduce.7.cloned.1.call-done = (bf16[128,4096]{1,0:T(8,128)(2,1)}, bf16[128,4096]{1,0:T(8,128)(2,1)}) async-done(((bf16[128,4096]{1,0:T(8,128)(2,1)}, bf16[128,4096]{1,0:T(8,128)(2,1)}), (bf16[128,4096]{1,0:T(8,128)(2,1)}, bf16[128,4096]{1,0:T(8,128)(2,1)})) %all-reduce.7.cloned.1.call-update) | async-done | bytes 2097168 | tf_op jit(solution)/shard_map/psum | solution.py:107
  266.8 2.8 fusion.31
  269.6 2.5 collective-permute-start
  275.9 1.9 fusion.27
  283.8 33.8 %all-gather.7.cloned.1.call-done = bf16[128,4096]{1,0:T(8,128)(2,1)} async-done(((bf16[16,4096]{1,0:T(8,128)(2,1)}), bf16[128,4096]{1,0:T(8,128)(2,1)}) %all-gather.7.cloned.1.call-update) | async-done | bytes 1048592 | tf_op jit(solution)/shard_map/all_gather | solution.py:226
  317.6 1.8 multiply_reduce_fusion.2
  320.8 2.0 fusion.91
  322.8 42.2 %all-gather.11.cloned.1.call-done = bf16[128,4096]{1,0:T(8,128)(2,1)} async-done(((bf16[16,4096]{1,0:T(8,128)(2,1)}), bf16[128,4096]{1,0:T(8,128)(2,1)}) %all-gather.11.cloned.1.call-update) | async-done | bytes 1048592 | tf_op jit(solution)/shard_map/all_gather | solution.py:228
  367.3 4.4 fusion.54
  380.1 2.0 convolution_convert_fusion.4
  382.2 4.0 convolution_convert_fusion
  393.3 2.8 convert_element_type.310
  399.3 6.8 %fusion.1 = bf16[1,512,4096]{2,1,0:T(8,128)(2,1)} fusion(f32[512,4096]{1,0:T(8,128)} %fusion.88, bf16[128,512]{0,1:T(8,128)(2,1)S(1)} %bitcast.419, bf16[128,4096]{1,0:T(8,128)(2,1)S(1)} %copy-done.4), kind=kOutput, calls=%fused_computation.3 | convolution fusion | flops 541065216 | bytes 13762560 | tf_op jit(solution)/shard_map/dot_general | solution.py:138
  406.2 3.5 fusion
  409.6 73.2 %all-reduce.5.cloned.1.call-done = (bf16[128,4096]{1,0:T(8,128)(2,1)}, bf16[128,4096]{1,0:T(8,128)(2,1)}) async-done(((bf16[128,4096]{1,0:T(8,128)(2,1)}, bf16[128,4096]{1,0:T(8,128)(2,1)}), (bf16[128,4096]{1,0:T(8,128)(2,1)}, bf16[128,4096]{1,0:T(8,128)(2,1)})) %all-reduce.5.cloned.1.call-update) | async-done | bytes 2097168 | tf_op jit(solution)/shard_map/psum | solution.py:107
  482.8 2.2 fusion.29
  (192 shorter events, 53.8 us)
Async XLA Ops:
  7.2 149.4 %copy-start = (bf16[1,4096,128]{2,1,0:T(8,128)(2,1)S(1)}, bf16[1,4096,128]{2,1,0:T(8,128)(2,1)}, u32[]{:S(2)}) copy-start(bf16[1,4096,128]{2,1,0:T(8,128)(2,1)} %param.18) | copy-start | bytes 3145732
  7.2 102.8 %all-gather.9.cloned.1.call-start = ((), (), s32[]{:S(2)}) async-start(), calls=%async_computation.2 | async-start | bytes 1179648 | tf_op jit(solution)/shard_map/all_gather | solution.py:227
  7.2 4.6 collective-permute-start.1
  11.8 47.9 %collective-permute-start.2 = (bf16[2,128,4096]{2,1,0:T(8,128)(2,1)}, bf16[2,128,4096]{2,1,0:T(8,128)(2,1)S(1)}, u32[]{:S(2)}, u32[]{:S(2)}) collective-permute-start(bf16[2,128,4096]{2,1,0:T(8,128)(2,1)} %collective-permute-done.1), channel_id=1, source_target_pairs={{0,16},{8,24},{16,0},{24,8},{32,48},{40,56},{48,32},{56,40},{64,80... | collective-permute-start | bytes 6291464 | tf_op jit(solution)/shard_map/ppermute | solution.py:14
  13.4 101.4 %all-gather.5.cloned.1.call-start = ((), (), s32[]{:S(2)}) async-start(), calls=%async_computation | async-start | bytes 1179648 | tf_op jit(solution)/shard_map/all_gather | solution.py:225
  59.7 48.5 %collective-permute-start.3 = (bf16[2,128,4096]{2,1,0:T(8,128)(2,1)S(1)}, bf16[2,128,4096]{2,1,0:T(8,128)(2,1)}, u32[]{:S(2)}, u32[]{:S(2)}) collective-permute-start(bf16[2,128,4096]{2,1,0:T(8,128)(2,1)S(1)} %collective-permute-done.2), channel_id=1, source_target_pairs={{0,32},{8,40},{16,48},{24,56},{32,0},{40,8},{48,16},{56,24},{64,96... | collective-permute-start | bytes 6291464 | tf_op jit(solution)/shard_map/ppermute | solution.py:14
  62.8 204.0 %all-reduce.7.cloned.1.call-start = ((), (), s32[]{:S(2)}) async-start(), calls=%async_computation.5 | async-start | bytes 4194304 | tf_op jit(solution)/shard_map/psum | solution.py:107
  108.2 46.2 %collective-permute-start.4 = (bf16[2,128,4096]{2,1,0:T(8,128)(2,1)}, bf16[2,128,4096]{2,1,0:T(8,128)(2,1)S(1)}, u32[]{:S(2)}, u32[]{:S(2)}) collective-permute-start(bf16[2,128,4096]{2,1,0:T(8,128)(2,1)} %collective-permute-done.3), channel_id=1, source_target_pairs={{0,64},{8,72},{16,80},{24,88},{32,96},{40,104},{48,112},{56,120},{... | collective-permute-start | bytes 6291464 | tf_op jit(solution)/shard_map/ppermute | solution.py:14
  110.0 6.5 %copy-start.20 = (f32[1,4096]{1,0:T(1,128)S(1)}, f32[1,4096]{1,0:T(1,128)}, u32[]{:S(2)}) copy-start(f32[1,4096]{1,0:T(1,128)} %param.15) | copy-start | bytes 49156
  118.6 36.1 %copy-start.9 = (bf16[1,4096,128]{2,1,0:T(8,128)(2,1)S(1)}, bf16[1,4096,128]{2,1,0:T(8,128)(2,1)}, u32[]{:S(2)}) copy-start(bf16[1,4096,128]{2,1,0:T(8,128)(2,1)} %param.17) | copy-start | bytes 3145732
  164.6 4.8 copy-start.29
  170.8 146.8 %all-gather.7.cloned.1.call-start = ((), (), s32[]{:S(2)}) async-start(), calls=%async_computation.1 | async-start | bytes 1179648 | tf_op jit(solution)/shard_map/all_gather | solution.py:226
  171.4 193.6 %all-gather.11.cloned.1.call-start = ((), (), s32[]{:S(2)}) async-start(), calls=%async_computation.3 | async-start | bytes 1179648 | tf_op jit(solution)/shard_map/all_gather | solution.py:228
  172.0 310.8 %all-reduce.5.cloned.1.call-start = ((), (), s32[]{:S(2)}) async-start(), calls=%async_computation.4 | async-start | bytes 4194304 | tf_op jit(solution)/shard_map/psum | solution.py:107
  266.8 5.3 %copy-start.16 = (bf16[128,4096]{1,0:T(8,128)(2,1)S(1)}, bf16[128,4096]{1,0:T(8,128)(2,1)}, u32[]{:S(2)}) copy-start(bf16[128,4096]{1,0:T(8,128)(2,1)} %get-tuple-element.15) | copy-start | bytes 3145732
  269.6 4.2 copy-start.11
  269.6 48.0 %collective-permute-start = (bf16[128,4096]{1,0:T(8,128)(2,1)}, bf16[128,4096]{1,0:T(8,128)(2,1)}, u32[]{:S(2)}, u32[]{:S(2)}) collective-permute-start(bf16[128,4096]{1,0:T(8,128)(2,1)} %fusion.31), channel_id=1, source_target_pairs={{0,8},{8,16},{16,24},{24,32},{32,40},{40,48},{48,56},{56,64},{64,7... | collective-permute-start | bytes 3145736 | tf_op jit(solution)/shard_map/ppermute | solution.py:20
  273.8 7.0 %copy-start.37 = (f32[128]{0:T(128)}, f32[128]{0:T(128)S(1)}, u32[]{:S(2)}) copy-start(f32[128]{0:T(128)S(1)} %get-tuple-element.47) | copy-start | bytes 1540
  277.8 87.2 %collective-permute-start.5 = (bf16[128,4096]{1,0:T(8,128)(2,1)}, bf16[128,4096]{1,0:T(8,128)(2,1)}, u32[]{:S(2)}, u32[]{:S(2)}) collective-permute-start(bf16[128,4096]{1,0:T(8,128)(2,1)} %fusion.27), channel_id=1, source_target_pairs={{8,0},{16,8},{24,16},{32,24},{40,32},{48,40},{56,48},{64,56},{72,6... | collective-permute-start | bytes 3145736 | tf_op jit(solution)/shard_map/ppermute | solution.py:20
  281.3 92.1 %copy-start.43 = (bf16[128,128,1]{1,0,2:T(8,128)(2,1)}, bf16[128,128,1]{1,0,2:T(8,128)(2,1)S(1)}, u32[]{:S(2)}) copy-start(bf16[128,128,1]{1,0,2:T(8,128)(2,1)S(1)} %fusion.66) | copy-start | bytes 98308
  282.3 92.5 %copy-start.35 = (f32[4,128]{1,0:T(4,128)}, f32[4,128]{1,0:T(4,128)S(1)}, u32[]{:S(2)}) copy-start(f32[4,128]{1,0:T(4,128)S(1)} %get-tuple-element.64) | copy-start | bytes 6148
  373.4 4.2 copy-start.22
  373.4 4.2 copy-start.33
  373.4 5.7 %copy-start.25 = (f32[128,4,128]{0,2,1:T(8,128)S(1)}, f32[128,4,128]{0,2,1:T(8,128)}, u32[]{:S(2)}) copy-start(f32[128,4,128]{0,2,1:T(8,128)} %fusion.91) | copy-start | bytes 786436
  373.4 5.7 %copy-start.27 = (f32[128,128]{0,1:T(8,128)S(1)}, f32[128,128]{0,1:T(8,128)}, u32[]{:S(2)}) copy-start(f32[128,128]{0,1:T(8,128)} %fusion.99) | copy-start | bytes 196612
  382.1 4.1 copy-start.21
  382.2 4.1 copy-start.24
  382.2 4.1 copy-start.2
  391.1 5.0 %copy-start.8 = (f32[4096,128]{1,0:T(8,128)S(1)}, f32[4096,128]{1,0:T(8,128)}, u32[]{:S(2)}) copy-start(f32[4096,128]{1,0:T(8,128)} %fusion.79) | copy-start | bytes 6291460
  391.1 5.0 %copy-start.38 = (f32[128]{0:T(128)S(1)}, f32[128]{0:T(128)}, u32[]{:S(2)}) copy-start(f32[128]{0:T(128)} %copy-done.37) | copy-start | bytes 1540
  397.7 8.4 %slice-start = ((s8[8388608]{0:T(1024)(128)(4,1)}), s8[4194304]{0:T(1024)(128)(4,1)S(1)}, s32[]{:S(2)}) async-start(s8[8388608]{0:T(1024)(128)(4,1)} %bitcast.383), calls=%async_computation.6 | async-start | bytes 8388608
  399.3 6.9 %slice-start.1 = ((s8[8388608]{0:T(1024)(128)(4,1)}), s8[4194304]{0:T(1024)(128)(4,1)S(1)}, s32[]{:S(2)}) async-start(s8[8388608]{0:T(1024)(128)(4,1)} %bitcast.383), calls=%async_computation.7 | async-start | bytes 8388608
  (28 other events, 56.2 us)
Sparse Core Ops, SparseCore 0:
  13.5 48.4 all-gather.8
  64.4 45.5 all-gather.4
  171.0 95.7 all-reduce.6
  269.0 48.5 all-gather.6
  319.8 45.1 all-gather.10
  390.5 92.2 all-reduce.4
where the time goes:
time: 496 us; the launch traced here: 495 us
  waiting for transfers between devices  351 us (71%)
  matrix products  79 us (16%)
  other arithmetic  23.9 us (5%)
  local copies, waits for them, and re-layouts  15.8 us (3%)
  between operations  14.8 us (3%)
  starting transfers between devices  10.9 us (2%)
    psum x2, waiting for transfers between devices, section_forward(): lax.psum(rounded.astype(jnp.bfloat16), 'tensor').astype(jnp.float32)  152 us
    ppermute x4, waiting for transfers between devices, swapped(): lax.ppermute(x, axis, [(i, i ^ 1 << distance) for i in range(lax.axis_siz...  122 us
    all_gather x1, waiting for transfers between devices, per_device(): lax.all_gather(loss_grad, 'tensor', axis=0, tiled=True)  42.2 us
    all_gather x1, waiting for transfers between devices, per_device(): lax.all_gather(entering, 'tensor', axis=0, tiled=True)  33.8 us
    dot_general x2, matrix products, section_backward(): lax.dot_general(attended, grad_rows, contract_first, preferred_element_ty...  11.4 us
  transfers between devices with their start and end apart: 12, of which 8 were waited for; matrix products, arithmetic and copies ran while one was open for 14% of the time, Pallas kernels for 0%

commit v1 on v0

v1 whole, which is shorter than its diff:
```python
import jax
import jax.numpy as jnp
from jax import lax
from jax.sharding import PartitionSpec as P

HEAD_DIMENSION = 128


EPSILON = 1e-05
ROPE_BASE = 10000.0


def shifted(x, axis, by):
    peers = lax.axis_size(axis)
    pairs = [(i, i + by) for i in range(peers) if 0 <= i + by < peers]
    return lax.ppermute(x, axis, pairs)


def rope_tables(token_count, head_size):
    positions = jnp.arange(token_count, dtype=jnp.float32)[:, None]
    exponents = jnp.arange(head_size // 2, dtype=jnp.float32) * (2.0 / head_size)
    angles = positions * (ROPE_BASE ** (-exponents))[None, :]
    angles = jnp.concatenate([angles, angles], axis=1)
    return (jnp.cos(angles), jnp.sin(angles))


def apply_rotary(values, cosine_table, sine_table):
    half_size = values.shape[-1] // 2
    turned = jnp.concatenate([-values[..., half_size:], values[..., :half_size]], axis=-1)
    return values * cosine_table[:, None, :] + turned * sine_table[:, None, :]


def reverse_rotary(gradient, cosine_table, sine_table):
    half_size = gradient.shape[-1] // 2
    scaled = gradient * sine_table[:, None, :]
    turned = jnp.concatenate([scaled[..., half_size:], -scaled[..., :half_size]], axis=-1)
    return gradient * cosine_table[:, None, :] + turned


def own_rows(full_rows, lane_index, shard_rows):
    return lax.dynamic_slice_in_dim(full_rows, lane_index * shard_rows, shard_rows, 0)


def attend(layer_in, gain_row, w_query, key_projection, value_projection, cosine_table, sine_table):
    token_count = layer_in.shape[0]
    head_size = cosine_table.shape[1]
    query_heads = w_query.shape[1] // head_size
    key_heads = key_projection.shape[1] // head_size
    heads_per_group = query_heads // key_heads
    wide_in = layer_in.astype(jnp.float32)
    inverse = lax.rsqrt(jnp.mean(wide_in * wide_in, axis=-1, keepdims=True) + EPSILON)
    normalized_input = (wide_in * inverse * gain_row[None, :]).astype(jnp.bfloat16)
    projected_queries = jnp.dot(
        normalized_input, w_query, preferred_element_type=jnp.float32
    ).reshape(token_count, query_heads, head_size)
    projected_queries = (
        apply_rotary(projected_queries, cosine_table, sine_table)
        .astype(jnp.bfloat16)
        .reshape(token_count, key_heads, heads_per_group, head_size)
    )
    projected_keys = jnp.dot(
        normalized_input, key_projection, preferred_element_type=jnp.float32
    ).reshape(token_count, key_heads, head_size)
    projected_keys = apply_rotary(projected_keys, cosine_table, sine_table).astype(jnp.bfloat16)
    projected_values = (
        jnp.dot(normalized_input, value_projection, preferred_element_type=jnp.float32)
        .astype(jnp.bfloat16)
        .reshape(token_count, key_heads, head_size)
    )
    scores = jnp.einsum(
        "qhgd,khd->hgqk", projected_queries, projected_keys, preferred_element_type=jnp.float32
    ) * head_size ** (-0.5)
    causal = jnp.arange(token_count)[:, None] >= jnp.arange(token_count)[None, :]
    exponent_terms = jnp.where(causal, jnp.exp(scores), 0.0)
    probability = exponent_terms / jnp.sum(exponent_terms, axis=-1, keepdims=True)
    weights = probability.astype(jnp.bfloat16)
    attended = jnp.einsum(
        "hgqk,khd->qhgd", weights, projected_values, preferred_element_type=jnp.float32
    )
    attended = attended.astype(jnp.bfloat16).reshape(token_count, query_heads * head_size)
    return (
        wide_in,
        inverse,
        normalized_input,
        projected_queries,
        projected_keys,
        projected_values,
        probability,
        weights,
        attended,
    )


def gathered(rows):
    peers = lax.axis_size("tensor")
    copies = jnp.broadcast_to(rows[None], (peers,) + rows.shape)
    return lax.all_to_all(copies, "tensor", 0, 0).reshape(peers * rows.shape[0], rows.shape[1])


def scattered_sum(term):
    peers = lax.axis_size("tensor")
    parts = lax.all_to_all(term.reshape(peers, -1, term.shape[1]), "tensor", 0, 0)
    return jnp.sum(parts.astype(jnp.float32), axis=0)


def section_forward(layer_in, own_in, gain_row, weights_all, cosine_table, sine_table):
    w_query, key_projection, value_projection, w_out = weights_all
    pieces = attend(
        layer_in, gain_row, w_query, key_projection, value_projection, cosine_table, sine_table
    )
    partial_term = jnp.dot(pieces[8], w_out, preferred_element_type=jnp.float32)
    summed = scattered_sum(partial_term.astype(jnp.bfloat16))
    return (own_in.astype(jnp.float32) + summed).astype(jnp.bfloat16)


def section_backward(
    pieces, own_stash, grad_rows, own_grad, gain_row, weights_all, cosine_table, sine_table
):
    w_query, key_projection, value_projection, w_out = weights_all
    (
        wide_in,
        inverse,
        normalized_input,
        projected_queries,
        projected_keys,
        projected_values,
        probability,
        weights,
        attended,
    ) = pieces
    token_count = wide_in.shape[0]
    head_size = cosine_table.shape[1]
    key_heads = projected_keys.shape[1]
    heads_per_group = projected_queries.shape[2]
    contract_last = (((1,), (1,)), ((), ()))
    attended_gradient = lax.dot_general(
        grad_rows, w_out, contract_last, preferred_element_type=jnp.float32
    ).astype(jnp.bfloat16)
    group_gradients = attended_gradient.reshape(token_count, key_heads, heads_per_group, head_size)
    value_grad = jnp.einsum(
        "hgqk,qhgd->khd", weights, group_gradients, preferred_element_type=jnp.float32
    )
    grad_probability = jnp.einsum(
        "qhgd,khd->hgqk", group_gradients, projected_values, preferred_element_type=jnp.float32
    )
    row_terms = jnp.sum(grad_probability * probability, axis=-1, keepdims=True)
    grad_scores = (probability * (grad_probability - row_terms) * head_size ** (-0.5)).astype(
        jnp.bfloat16
    )
    query_grad = jnp.einsum(
        "hgqk,khd->qhgd", grad_scores, projected_keys, preferred_element_type=jnp.float32
    )
    query_grad = query_grad.reshape(token_count, key_heads * heads_per_group, head_size)
    key_grad = jnp.einsum(
        "hgqk,qhgd->khd", grad_scores, projected_queries, preferred_element_type=jnp.float32
    )
    query_grad = (
        reverse_rotary(query_grad, cosine_table, sine_table)
        .astype(jnp.bfloat16)
        .reshape(token_count, -1)
    )
    key_grad = (
        reverse_rotary(key_grad, cosine_table, sine_table)
        .astype(jnp.bfloat16)
        .reshape(token_count, -1)
    )
    value_grad = value_grad.astype(jnp.bfloat16).reshape(token_count, -1)
    partial_term = lax.dot_general(
        query_grad, w_query, contract_last, preferred_element_type=jnp.float32
    )
    partial_term = partial_term + lax.dot_general(
        key_grad, key_projection, contract_last, preferred_element_type=jnp.float32
    )
    partial_term = partial_term + lax.dot_general(
        value_grad, value_projection, contract_last, preferred_element_type=jnp.float32
    )
    rounded = partial_term.astype(jnp.bfloat16)
    gain_part = jnp.sum(rounded.astype(jnp.float32) * wide_in * inverse, axis=0)
    grad_normed = scattered_sum(rounded)
    own_wide = own_stash.astype(jnp.float32)
    own_inverse = lax.rsqrt(jnp.mean(own_wide * own_wide, axis=-1, keepdims=True) + EPSILON)
    scaled_grad = grad_normed * gain_row[None, :]
    grad_in = (
        own_grad.astype(jnp.float32)
        + own_inverse * scaled_grad
        - own_wide * own_inverse**3 * jnp.mean(scaled_grad * own_wide, axis=-1, keepdims=True)
    )
    return (
        grad_in.astype(jnp.bfloat16),
        gain_part,
        (normalized_input, query_grad, key_grad, value_grad, attended),
    )


def mirrored(rows):
    sections = lax.axis_size("pipe")
    peers = lax.axis_size("tensor")
    half = rows.shape[0] // 2
    near, far = [], []
    for section in range(sections):
        for lane in range(peers):
            here = section * peers + lane
            there = (sections - 1 - section) * peers
            near.append((here, there + lane))
            far.append((here, there + (lane ^ peers // 2)))
    return jnp.concatenate(
        [
            lax.ppermute(rows[:half], ("pipe", "tensor"), near),
            lax.ppermute(rows[half:], ("pipe", "tensor"), far),
        ]
    )


def per_device(
    forward_in,
    entering,
    backward_in,
    loss_grad,
    stashed,
    norm_gain,
    w_query,
    key_projection,
    value_projection,
    w_out,
):
    sections = lax.axis_size("pipe")
    section_index = lax.axis_index("pipe")
    lane_index = lax.axis_index("tensor")
    shard_rows = forward_in.shape[1]
    token_count = stashed.shape[2]
    gain_row = norm_gain[0]
    weights_all = (w_query[0], key_projection[0], value_projection[0], w_out[0])
    cosine_table, sine_table = rope_tables(token_count, HEAD_DIMENSION)
    contract_first = (((0,), (0,)), ((), ()))

    def recompute(rows):
        return attend(rows, gain_row, *weights_all[:3], cosine_table, sine_table)

    def weight_gradient(left, right):
        both = lax.dot_general(
            jnp.concatenate(left),
            jnp.concatenate(right),
            contract_first,
            preferred_element_type=jnp.float32,
        )
        return both.astype(jnp.bfloat16)[None]

    saved = (mirrored(stashed[0, 0]), mirrored(stashed[0, 1]))
    own_saved = [own_rows(rows, lane_index, shard_rows) for rows in saved]
    first_in = gathered(forward_in[0])
    first_grad = gathered(backward_in[0])
    first_own = section_forward(
        first_in, forward_in[0], gain_row, weights_all, cosine_table, sine_table
    )
    second_own_in = jnp.where(section_index == 0, entering, shifted(first_own, "pipe", 1))
    second_in = gathered(second_own_in)
    first_back, first_gain, first_terms = section_backward(
        recompute(saved[0]),
        own_saved[0],
        first_grad,
        backward_in[0],
        gain_row,
        weights_all,
        cosine_table,
        sine_table,
    )
    second_own_grad = jnp.where(
        section_index == sections - 1, loss_grad, shifted(first_back, "pipe", -1)
    )
    second_grad = gathered(second_own_grad)
    second_own = section_forward(
        second_in, second_own_in, gain_row, weights_all, cosine_table, sine_table
    )
    second_back, second_gain, second_terms = section_backward(
        recompute(saved[1]),
        own_saved[1],
        second_grad,
        second_own_grad,
        gain_row,
        weights_all,
        cosine_table,
        sine_table,
    )
    forward_out = jnp.stack([first_own, second_own])[:, None]
    backward_out = jnp.stack([first_back, second_back])[:, None]
    normed = (first_terms[0], second_terms[0])
    grad_query = weight_gradient(normed, (first_terms[1], second_terms[1]))
    key_weight_gradient = weight_gradient(normed, (first_terms[2], second_terms[2]))
    value_weight_gradient = weight_gradient(normed, (first_terms[3], second_terms[3]))
    grad_out = weight_gradient(
        (first_terms[4], second_terms[4]), (first_grad, second_grad)
    )
    gain_parts = gathered((first_gain + second_gain)[None])
    grad_gain = jnp.sum(gain_parts, axis=0)[None]
    return (
        forward_out,
        backward_out,
        grad_query,
        key_weight_gradient,
        value_weight_gradient,
        grad_out,
        grad_gain,
    )


def solution(mesh):
    in_specs = (
        P("pipe", "tensor", None),
        P("tensor", None),
        P("pipe", "tensor", None),
        P("tensor", None),
        P("pipe", None, None, None),
        P("pipe", None),
        P("pipe", None, "tensor"),
        P("pipe", None, "tensor"),
        P("pipe", None, "tensor"),
        P("pipe", "tensor", None),
    )
    out_specs = (
        P(None, "pipe", "tensor", None),
        P(None, "pipe", "tensor", None),
        P("pipe", None, "tensor"),
        P("pipe", None, "tensor"),
        P("pipe", None, "tensor"),
        P("pipe", "tensor", None),
        P("pipe", None),
    )
    return jax.shard_map(
        per_device, mesh=mesh, in_specs=in_specs, out_specs=out_specs, check_vma=False
    )
```

time: 496 us -> 286 us (0.58)
  waiting for transfers between devices: 351 us -> 96 us
  starting transfers between devices: 10.9 us -> 61.8 us
  between operations: 14.8 us -> 1.62 us
  other arithmetic: 23.9 us -> 33.7 us
  matrix products: 79 us -> 70.5 us
    psum x2 -> x0, waiting for transfers between devices: 152 us -> none  [section_forward(): lax.psum(rounded.astype(jnp.bfloat16), 'tensor').astype(jnp.float32)]
    ppermute x4, waiting for transfers between devices: 122 us -> 36.5 us  [the longest x2 28.9 us: mirrored(): lax.ppermute(rows[half:], ('pipe', 'tensor'), far)]
    all_gather x4 -> x0, waiting for transfers between devices: 76 us -> none  [the longest x1 42.2 us: per_device(): lax.all_gather(loss_grad, 'tensor', axis=0, tiled=True)]
    all_to_all x0 -> x9, waiting for transfers between devices: none -> 59.5 us  [the longest x4 30.7 us: scattered_sum(): lax.all_to_all(term.reshape(peers, -1, term.shape[1]), 'tensor', 0, 0)]
    all_to_all x0 -> x9, starting transfers between devices: none -> 50 us  [the longest x5 26.8 us: gathered(): lax.all_to_all(copies, 'tensor', 0, 0)]
    dot_general x14 -> x10, matrix products: 33.3 us -> 19.3 us  [the longest x4 11.6 us: weight_gradient(): lax.dot_general(jnp.concatenate(left), jnp.concatenate(right), contract_f...]
    broadcast_in_dim x0 -> x5, local copies, waits for them, and re-layouts: none -> 5.9 us  [gathered(): copies = jnp.broadcast_to(rows[None], (peers,) + rows.shape)]
  transfers between devices with their start and end apart: 12 -> 15, of which waited for: 8 -> 9; matrix products, arithmetic and copies ran while one was open for 14% -> 28% of each run, Pallas kernels for 0% -> 0%
where the time goes in v1:
time: 286 us; the launch traced here: 284 us
  waiting for transfers between devices  96 us (34%)
  matrix products  70.5 us (25%)
  starting transfers between devices  61.8 us (22%)
  other arithmetic  33.7 us (12%)
  local copies, waits for them, and re-layouts  20.3 us (7%)
    all_to_all x4, waiting for transfers between devices, scattered_sum(): lax.all_to_all(term.reshape(peers, -1, term.shape[1]), 'tensor', 0, 0)  30.7 us
    ppermute x2, waiting for transfers between devices, mirrored(): lax.ppermute(rows[half:], ('pipe', 'tensor'), far)  28.9 us
    all_to_all x5, waiting for transfers between devices, gathered(): lax.all_to_all(copies, 'tensor', 0, 0)  28.8 us
    all_to_all x5, starting transfers between devices, gathered(): lax.all_to_all(copies, 'tensor', 0, 0)  26.8 us
    all_to_all x4, starting transfers between devices, scattered_sum(): lax.all_to_all(term.reshape(peers, -1, term.shape[1]), 'tensor', 0, 0)  23.2 us
    dot_general x4, matrix products, weight_gradient(): lax.dot_general(jnp.concatenate(left), jnp.concatenate(right), contract_f...  11.6 us
    dot_general x4, matrix products, attend(): jnp.dot(normalized_input, w_query, preferred_element_type=jnp.float32)  10.3 us
    dot_general x2, matrix products, section_backward(): lax.dot_general(grad_rows, w_out, contract_last, preferred_element_type=j...  8.15 us
  transfers between devices with their start and end apart: 15, of which 9 were waited for; matrix products, arithmetic and copies ran while one was open for 28% of the time, Pallas kernels for 0%

profile of v1, /device:TPU:0, one launch (start us, length us, event | category | flops | bytes accessed | tf_op | source)
XLA Modules:
  0.0 283.9 jit_solution(16093941406093742141)
XLA Ops:
  0.7 3.0 %slice_bitcast_fusion.2 = (bf16[64,4096]{1,0:T(8,128)(2,1)}, bf16[64,4096]{1,0:T(8,128)(2,1)}, bf16[64,4096]{1,0:T(8,128)(2,1)}, bf16[64,4096]{1,0:T(8,128)(2,1)}) fusion(bf16[1,2,128,4096]{3,2,1,0:T(8,128)(2,1)} %param.14), kind=kLoop, calls=%fused_computation.124 | loop fusion | bytes 4194304 | tf_op jit(solution)/shard_map/slice | solution.py:209
  3.6 3.3 %collective-permute-start.1 = (bf16[64,4096]{1,0:T(8,128)(2,1)}, bf16[64,4096]{1,0:T(8,128)(2,1)S(1)}, u32[]{:S(2)}, u32[]{:S(2)}) collective-permute-start(bf16[64,4096]{1,0:T(8,128)(2,1)} %get-tuple-element.33), channel_id=1, source_target_pairs={{0,120},{1,121},{2,122},{3,123},{4,124},{5,125},{6,126},{7,127},{8... | collective-permute-start | bytes 1572872 | tf_op jit(solution)/shard_map/ppermute | solution.py:208
  6.9 2.4 collective-permute-start.2
  13.3 7.8 %all-to-all-start.4 = ((bf16[8,16,4096]{2,1,0:T(8,128)(2,1)}), bf16[8,16,4096]{2,1,0:T(8,128)(2,1)}, u32[]{:S(2)}, u32[]{:S(2)}) async-start(bf16[8,16,4096]{2,1,0:T(8,128)(2,1)} %broadcast_in_dim.52), calls=%async_computation.4 | async-start | bytes 2097152 | tf_op jit(solution)/shard_map/all_to_all | solution.py:97
  21.1 6.3 %copy.129 = bf16[512,4096]{1,0:T(8,128)(2,1)} copy(bf16[512,4096]{0,1:T(8,128)(2,1)} %bitcast.383) | data formatting | bytes 8388608 | tf_op jit(solution)/shard_map/dot_general | solution.py:53
  28.2 10.8 %collective-permute-done.2 = bf16[64,4096]{1,0:T(8,128)(2,1)S(1)} collective-permute-done((bf16[64,4096]{1,0:T(8,128)(2,1)}, bf16[64,4096]{1,0:T(8,128)(2,1)S(1)}, u32[]{:S(2)}, u32[]{:S(2)}) %collective-permute-start.2) | collective-permute-done | bytes 524320 | tf_op jit(solution)/shard_map/ppermute | solution.py:209
  39.3 7.6 %collective-permute-done.4 = bf16[64,4096]{1,0:T(8,128)(2,1)S(1)} collective-permute-done((bf16[64,4096]{1,0:T(8,128)(2,1)}, bf16[64,4096]{1,0:T(8,128)(2,1)S(1)}, u32[]{:S(2)}, u32[]{:S(2)}) %collective-permute-start.4) | collective-permute-done | bytes 524320 | tf_op jit(solution)/shard_map/ppermute | solution.py:208
  47.0 18.1 %collective-permute-done.5 = bf16[64,4096]{1,0:T(8,128)(2,1)S(1)} collective-permute-done((bf16[64,4096]{1,0:T(8,128)(2,1)}, bf16[64,4096]{1,0:T(8,128)(2,1)S(1)}, u32[]{:S(2)}, u32[]{:S(2)}) %collective-permute-start.5) | collective-permute-done | bytes 524320 | tf_op jit(solution)/shard_map/ppermute | solution.py:209
  77.0 5.4 %all-to-all-start = ((bf16[8,16,4096]{2,1,0:T(8,128)(2,1)}), bf16[8,16,4096]{2,1,0:T(8,128)(2,1)}, u32[]{:S(2)}, u32[]{:S(2)}) async-start(bf16[8,16,4096]{2,1,0:T(8,128)(2,1)} %broadcast_in_dim.47), calls=%async_computation | async-start | bytes 2097152 | tf_op jit(solution)/shard_map/all_to_all | solution.py:97
  84.6 4.1 %fusion.56 = bf16[16,4,8,128]{3,2,1,0:T(8,128)(2,1)S(1)} fusion(bf16[128,4096]{1,0:T(8,128)(2,1)} %bitcast.50, bf16[1,512,4096]{2,1,0:T(8,128)(2,1)} %param.19), kind=kOutput, calls=%fused_computation.85 | convolution fusion | flops 536936448 | bytes 5373952 | tf_op jit(solution)/shard_map/dot_general | solution.py:136
  90.9 7.4 %all-to-all-done = bf16[8,16,4096]{2,1,0:T(8,128)(2,1)} async-done(((bf16[8,16,4096]{2,1,0:T(8,128)(2,1)}), bf16[8,16,4096]{2,1,0:T(8,128)(2,1)}, u32[]{:S(2)}, u32[]{:S(2)}) %all-to-all-start) | async-done | bytes 1048608 | tf_op jit(solution)/shard_map/all_to_all | solution.py:97
  101.4 3.9 %fusion.205 = f32[128,4,128]{0,2,1:T(8,128)S(1)} fusion(bf16[128,4096,1]{1,0,2:T(8,128)(2,1)S(1)} %bitcast.384, bf16[4,128,4096]{2,1,0:T(8,128)(2,1)} %bitcast.379), kind=kOutput, calls=%fused_computation.308 | convolution fusion | flops 536870912 | bytes 5505024 | tf_op jit(solution)/shard_map/dot_general | solution.py:53
  113.8 4.3 %all-to-all-start.5 = ((bf16[8,16,4096]{2,1,0:T(8,128)(2,1)}), bf16[8,16,4096]{2,1,0:T(8,128)(2,1)}, u32[]{:S(2)}, u32[]{:S(2)}) async-start(bf16[8,16,4096]{2,1,0:T(8,128)(2,1)} %bitcast.393), calls=%async_computation.5 | async-start | bytes 2097152 | tf_op jit(solution)/shard_map/all_to_all | solution.py:102
  118.9 2.5 fusion.201
  123.4 3.9 %convolution_convert_fusion.5 = bf16[128,4096]{1,0:T(8,128)(2,1)} fusion(bf16[128,512]{0,1:T(8,128)(2,1)S(1)} %bitcast.411, bf16[1,512,4096]{2,1,0:T(8,128)(2,1)} %param.19), kind=kOutput, calls=%fused_computation.13 | convolution fusion | flops 537395200 | bytes 5373952 | tf_op jit(solution)/shard_map/dot_general | solution.py:111
  127.3 6.8 %all-to-all-done.5 = bf16[8,16,4096]{2,1,0:T(8,128)(2,1)} async-done(((bf16[8,16,4096]{2,1,0:T(8,128)(2,1)}), bf16[8,16,4096]{2,1,0:T(8,128)(2,1)}, u32[]{:S(2)}, u32[]{:S(2)}) %all-to-all-start.5) | async-done | bytes 1048608 | tf_op jit(solution)/shard_map/all_to_all | solution.py:102
  134.1 4.2 %all-to-all-start.1 = ((bf16[8,16,4096]{2,1,0:T(8,128)(2,1)}), bf16[8,16,4096]{2,1,0:T(8,128)(2,1)}, u32[]{:S(2)}, u32[]{:S(2)}) async-start(bf16[8,16,4096]{2,1,0:T(8,128)(2,1)} %bitcast.392), calls=%async_computation.1 | async-start | bytes 2097152 | tf_op jit(solution)/shard_map/all_to_all | solution.py:102
  143.9 10.5 %all-to-all-done.1 = bf16[8,16,4096]{2,1,0:T(8,128)(2,1)} async-done(((bf16[8,16,4096]{2,1,0:T(8,128)(2,1)}), bf16[8,16,4096]{2,1,0:T(8,128)(2,1)}, u32[]{:S(2)}, u32[]{:S(2)}) %all-to-all-start.1) | async-done | bytes 1048608 | tf_op jit(solution)/shard_map/all_to_all | solution.py:102
  161.9 4.9 %all-to-all-start.6 = ((bf16[8,16,4096]{2,1,0:T(8,128)(2,1)}), bf16[8,16,4096]{2,1,0:T(8,128)(2,1)}, u32[]{:S(2)}, u32[]{:S(2)}) async-start(bf16[8,16,4096]{2,1,0:T(8,128)(2,1)} %broadcast_in_dim.53), calls=%async_computation.6 | async-start | bytes 2097152 | tf_op jit(solution)/shard_map/all_to_all | solution.py:97
  170.2 12.5 %all-to-all-done.6 = bf16[8,16,4096]{2,1,0:T(8,128)(2,1)} async-done(((bf16[8,16,4096]{2,1,0:T(8,128)(2,1)}), bf16[8,16,4096]{2,1,0:T(8,128)(2,1)}, u32[]{:S(2)}, u32[]{:S(2)}) %all-to-all-start.6) | async-done | bytes 1048608 | tf_op jit(solution)/shard_map/all_to_all | solution.py:97
  184.7 4.6 %all-to-all-start.2 = ((bf16[8,16,4096]{2,1,0:T(8,128)(2,1)}), bf16[8,16,4096]{2,1,0:T(8,128)(2,1)}, u32[]{:S(2)}, u32[]{:S(2)}) async-start(bf16[8,16,4096]{2,1,0:T(8,128)(2,1)} %broadcast_in_dim.50), calls=%async_computation.2 | async-start | bytes 2097152 | tf_op jit(solution)/shard_map/all_to_all | solution.py:97
  189.4 4.1 %fusion.53 = bf16[16,4,8,128]{3,2,1,0:T(8,128)(2,1)S(1)} fusion(bf16[128,4096]{1,0:T(8,128)(2,1)} %bitcast.85, bf16[1,512,4096]{2,1,0:T(8,128)(2,1)} %param.19), kind=kOutput, calls=%fused_computation.84 | convolution fusion | flops 536936448 | bytes 5373952 | tf_op jit(solution)/shard_map/dot_general | solution.py:136
  196.5 8.9 %all-to-all-done.2 = bf16[8,16,4096]{2,1,0:T(8,128)(2,1)} async-done(((bf16[8,16,4096]{2,1,0:T(8,128)(2,1)}), bf16[8,16,4096]{2,1,0:T(8,128)(2,1)}, u32[]{:S(2)}, u32[]{:S(2)}) %all-to-all-start.2) | async-done | bytes 1048608 | tf_op jit(solution)/shard_map/all_to_all | solution.py:97
  208.4 3.9 %fusion.206 = f32[128,4,128]{0,2,1:T(8,128)S(1)} fusion(bf16[128,4096,1]{1,0,2:T(8,128)(2,1)S(1)} %bitcast.387, bf16[4,128,4096]{2,1,0:T(8,128)(2,1)} %bitcast.380), kind=kOutput, calls=%fused_computation.309 | convolution fusion | flops 536870912 | bytes 5505024 | tf_op jit(solution)/shard_map/dot_general | solution.py:53
  220.4 4.3 %all-to-all-start.8 = ((f32[8,1,4096]{2,1,0:T(1,128)}), f32[8,1,4096]{2,1,0:T(1,128)}, u32[]{:S(2)}, u32[]{:S(2)}) async-start(f32[8,1,4096]{2,1,0:T(1,128)} %broadcast_in_dim.59), calls=%async_computation.8 | async-start | bytes 262144 | tf_op jit(solution)/shard_map/all_to_all | solution.py:97
  224.7 2.7 fusion.202
  229.6 4.0 %convolution_convert_fusion.4 = bf16[128,4096]{1,0:T(8,128)(2,1)} fusion(bf16[128,512]{0,1:T(8,128)(2,1)} %bitcast.412, bf16[1,512,4096]{2,1,0:T(8,128)(2,1)} %param.19), kind=kOutput, calls=%fused_computation.12 | convolution fusion | flops 537395200 | bytes 5373952 | tf_op jit(solution)/shard_map/dot_general | solution.py:111
  233.6 7.4 %all-to-all-start.3 = ((bf16[8,16,4096]{2,1,0:T(8,128)(2,1)}), bf16[8,16,4096]{2,1,0:T(8,128)(2,1)}, u32[]{:S(2)}, u32[]{:S(2)}) async-start(bf16[8,16,4096]{2,1,0:T(8,128)(2,1)} %bitcast.391), calls=%async_computation.3 | async-start | bytes 2097152 | tf_op jit(solution)/shard_map/all_to_all | solution.py:102
  247.3 4.8 %fusion.1 = bf16[1,512,4096]{2,1,0:T(8,128)(2,1)} fusion(bf16[128,4096]{1,0:T(8,128)(2,1)} %bitcast.85, bf16[128,4096]{1,0:T(8,128)(2,1)} %bitcast.50, bf16[128,512]{0,1:T(8,128)(2,1)S(1)} %bitcast.410, bf16[128,512]{0,1:T(8,128)(2,1)S(1)} %bitcast.409), kind=kOutput, calls=%fused_computation.3 | convolution fusion | flops 1080557568 | bytes 6553600 | tf_op jit(solution)/shard_map/dot_general | solution.py:240
  252.2 3.3 %fusion = bf16[1,4096,512]{2,1,0:T(8,128)(2,1)} fusion(bf16[128,4096]{1,0:T(8,128)(2,1)S(1)} %copy-done.6, bf16[128,4096]{1,0:T(8,128)(2,1)S(1)} %get-tuple-element.72, bf16[128,512]{0,1:T(8,128)(2,1)S(1)} %get-tuple-element.55, bf16[128,512]{0,1:T(8,128)(2,1)S(1)} %get-tuple-element.54), kind=kOutput, calls=%fused_computation.2 | convolution fusion | flops 1080557568 | bytes 6553600 | tf_op jit(solution)/shard_map/dot_general | solution.py:240
  257.1 7.2 %all-to-all-start.7 = ((bf16[8,16,4096]{2,1,0:T(8,128)(2,1)}), bf16[8,16,4096]{2,1,0:T(8,128)(2,1)S(1)}, u32[]{:S(2)}, u32[]{:S(2)}) async-start(bf16[8,16,4096]{2,1,0:T(8,128)(2,1)} %bitcast.390), calls=%async_computation.7 | async-start | bytes 2097152 | tf_op jit(solution)/shard_map/all_to_all | solution.py:102
  265.8 13.4 %all-to-all-done.7 = bf16[8,16,4096]{2,1,0:T(8,128)(2,1)S(1)} async-done(((bf16[8,16,4096]{2,1,0:T(8,128)(2,1)}), bf16[8,16,4096]{2,1,0:T(8,128)(2,1)S(1)}, u32[]{:S(2)}, u32[]{:S(2)}) %all-to-all-start.7) | async-done | bytes 1048608 | tf_op jit(solution)/shard_map/all_to_all | solution.py:102
  (235 shorter events, 84.1 us)
Async XLA Ops:
  0.6 71.3 %copy-start = (bf16[1,4096,128]{2,1,0:T(8,128)(2,1)S(1)}, bf16[1,4096,128]{2,1,0:T(8,128)(2,1)}, u32[]{:S(2)}) copy-start(bf16[1,4096,128]{2,1,0:T(8,128)(2,1)} %param.18) | copy-start | bytes 3145732
  0.6 11.6 %copy-start.35 = (bf16[1,16,4096]{2,1,0:T(8,128)(2,1)S(1)}, bf16[1,16,4096]{2,1,0:T(8,128)(2,1)}, u32[]{:S(2)}) copy-start(bf16[1,16,4096]{2,1,0:T(8,128)(2,1)} %param.12) | copy-start | bytes 393220
  3.6 24.5 %collective-permute-start.1 = (bf16[64,4096]{1,0:T(8,128)(2,1)}, bf16[64,4096]{1,0:T(8,128)(2,1)S(1)}, u32[]{:S(2)}, u32[]{:S(2)}) collective-permute-start(bf16[64,4096]{1,0:T(8,128)(2,1)} %get-tuple-element.33), channel_id=1, source_target_pairs={{0,120},{1,121},{2,122},{3,123},{4,124},{5,125},{6,126},{7,127},{8... | collective-permute-start | bytes 1572872 | tf_op jit(solution)/shard_map/ppermute | solution.py:208
  6.9 32.0 %collective-permute-start.2 = (bf16[64,4096]{1,0:T(8,128)(2,1)}, bf16[64,4096]{1,0:T(8,128)(2,1)S(1)}, u32[]{:S(2)}, u32[]{:S(2)}) collective-permute-start(bf16[64,4096]{1,0:T(8,128)(2,1)} %get-tuple-element.32), channel_id=1, source_target_pairs={{0,124},{1,125},{2,126},{3,127},{4,120},{5,121},{6,122},{7,123},{8... | collective-permute-start | bytes 1572872 | tf_op jit(solution)/shard_map/ppermute | solution.py:209
  9.3 37.6 %collective-permute-start.4 = (bf16[64,4096]{1,0:T(8,128)(2,1)}, bf16[64,4096]{1,0:T(8,128)(2,1)S(1)}, u32[]{:S(2)}, u32[]{:S(2)}) collective-permute-start(bf16[64,4096]{1,0:T(8,128)(2,1)} %get-tuple-element.35), channel_id=1, source_target_pairs={{0,120},{1,121},{2,122},{3,123},{4,124},{5,125},{6,126},{7,127},{8... | collective-permute-start | bytes 1572872 | tf_op jit(solution)/shard_map/ppermute | solution.py:208
  11.6 53.5 %collective-permute-start.5 = (bf16[64,4096]{1,0:T(8,128)(2,1)}, bf16[64,4096]{1,0:T(8,128)(2,1)S(1)}, u32[]{:S(2)}, u32[]{:S(2)}) collective-permute-start(bf16[64,4096]{1,0:T(8,128)(2,1)} %get-tuple-element.34), channel_id=1, source_target_pairs={{0,124},{1,125},{2,126},{3,127},{4,120},{5,121},{6,122},{7,123},{8... | collective-permute-start | bytes 1572872 | tf_op jit(solution)/shard_map/ppermute | solution.py:209
  13.3 62.6 %all-to-all-start.4 = ((bf16[8,16,4096]{2,1,0:T(8,128)(2,1)}), bf16[8,16,4096]{2,1,0:T(8,128)(2,1)}, u32[]{:S(2)}, u32[]{:S(2)}) async-start(bf16[8,16,4096]{2,1,0:T(8,128)(2,1)} %broadcast_in_dim.52), calls=%async_computation.4 | async-start | bytes 2097152 | tf_op jit(solution)/shard_map/all_to_all | solution.py:97
  28.1 46.2 %copy-start.38 = (pred[128,128]{0,1:T(8,128)(4,1)}, pred[128,128]{0,1:T(8,128)(4,1)S(1)}, u32[]{:S(2)}) copy-start(pred[128,128]{0,1:T(8,128)(4,1)S(1)} %iota_compare_fusion) | copy-start | bytes 49156
  39.0 26.4 %copy-start.7 = (bf16[128,4096]{1,0:T(8,128)(2,1)}, bf16[128,4096]{1,0:T(8,128)(2,1)S(1)}, u32[]{:S(2)}) copy-start(bf16[128,4096]{1,0:T(8,128)(2,1)S(1)} %constant_dynamic-update-slice_fusion) | copy-start | bytes 3145732
  39.0 26.4 %copy-start.33 = (f32[1,4096]{1,0:T(1,128)S(1)}, f32[1,4096]{1,0:T(1,128)}, u32[]{:S(2)}) copy-start(f32[1,4096]{1,0:T(1,128)} %param.15) | copy-start | bytes 49156
  39.3 26.8 %copy-start.64 = (f32[128]{0:T(128)}, f32[128]{0:T(128)S(1)}, u32[]{:S(2)}) copy-start(f32[128]{0:T(128)S(1)} %add_rsqrt_fusion.4) | copy-start | bytes 1540
  72.8 17.3 %copy-start.59 = (f32[4,128]{1,0:T(4,128)}, f32[4,128]{1,0:T(4,128)S(1)}, u32[]{:S(2)}) copy-start(f32[4,128]{1,0:T(4,128)S(1)} %get-tuple-element.84) | copy-start | bytes 6148
  77.0 21.3 %all-to-all-start = ((bf16[8,16,4096]{2,1,0:T(8,128)(2,1)}), bf16[8,16,4096]{2,1,0:T(8,128)(2,1)}, u32[]{:S(2)}, u32[]{:S(2)}) async-start(bf16[8,16,4096]{2,1,0:T(8,128)(2,1)} %broadcast_in_dim.47), calls=%async_computation | async-start | bytes 2097152 | tf_op jit(solution)/shard_map/all_to_all | solution.py:97
  113.8 20.3 %all-to-all-start.5 = ((bf16[8,16,4096]{2,1,0:T(8,128)(2,1)}), bf16[8,16,4096]{2,1,0:T(8,128)(2,1)}, u32[]{:S(2)}, u32[]{:S(2)}) async-start(bf16[8,16,4096]{2,1,0:T(8,128)(2,1)} %bitcast.393), calls=%async_computation.5 | async-start | bytes 2097152 | tf_op jit(solution)/shard_map/all_to_all | solution.py:102
  127.3 13.6 %copy-start.36 = (bf16[1,16,4096]{2,1,0:T(8,128)(2,1)S(1)}, bf16[1,16,4096]{2,1,0:T(8,128)(2,1)}, u32[]{:S(2)}) copy-start(bf16[1,16,4096]{2,1,0:T(8,128)(2,1)} %param.12) | copy-start | bytes 393220
  134.1 20.2 %all-to-all-start.1 = ((bf16[8,16,4096]{2,1,0:T(8,128)(2,1)}), bf16[8,16,4096]{2,1,0:T(8,128)(2,1)}, u32[]{:S(2)}, u32[]{:S(2)}) async-start(bf16[8,16,4096]{2,1,0:T(8,128)(2,1)} %bitcast.392), calls=%async_computation.1 | async-start | bytes 2097152 | tf_op jit(solution)/shard_map/all_to_all | solution.py:102
  142.6 16.7 %collective-permute-start.3 = (bf16[16,4096]{1,0:T(8,128)(2,1)}, bf16[16,4096]{1,0:T(8,128)(2,1)}, u32[]{:S(2)}, u32[]{:S(2)}) collective-permute-start(bf16[16,4096]{1,0:T(8,128)(2,1)} %fusion.94), channel_id=1, source_target_pairs={{8,0},{16,8},{24,16},{32,24},{40,32},{48,40},{56,48},{64,56},{72,6... | collective-permute-start | bytes 393224 | tf_op jit(solution)/shard_map/ppermute | solution.py:16
  157.3 11.3 %collective-permute-start = (bf16[16,4096]{1,0:T(8,128)(2,1)}, bf16[16,4096]{1,0:T(8,128)(2,1)}, u32[]{:S(2)}, u32[]{:S(2)}) collective-permute-start(bf16[16,4096]{1,0:T(8,128)(2,1)} %add_convert_fusion.1), channel_id=1, source_target_pairs={{0,8},{8,16},{16,24},{24,32},{32,40},{40,48},{48,56},{56,64},{64,7... | collective-permute-start | bytes 393224 | tf_op jit(solution)/shard_map/ppermute | solution.py:16
  161.9 20.8 %all-to-all-start.6 = ((bf16[8,16,4096]{2,1,0:T(8,128)(2,1)}), bf16[8,16,4096]{2,1,0:T(8,128)(2,1)}, u32[]{:S(2)}, u32[]{:S(2)}) async-start(bf16[8,16,4096]{2,1,0:T(8,128)(2,1)} %broadcast_in_dim.53), calls=%async_computation.6 | async-start | bytes 2097152 | tf_op jit(solution)/shard_map/all_to_all | solution.py:97
  184.7 20.6 %all-to-all-start.2 = ((bf16[8,16,4096]{2,1,0:T(8,128)(2,1)}), bf16[8,16,4096]{2,1,0:T(8,128)(2,1)}, u32[]{:S(2)}, u32[]{:S(2)}) async-start(bf16[8,16,4096]{2,1,0:T(8,128)(2,1)} %broadcast_in_dim.50), calls=%async_computation.2 | async-start | bytes 2097152 | tf_op jit(solution)/shard_map/all_to_all | solution.py:97
  208.4 5.9 %copy-start.25 = (f32[128,4,128]{0,2,1:T(8,128)S(1)}, f32[128,4,128]{0,2,1:T(8,128)}, u32[]{:S(2)}) copy-start(f32[128,4,128]{0,2,1:T(8,128)} %get-tuple-element.96) | copy-start | bytes 786436
  208.4 5.9 %copy-start.15 = (f32[128,4,128]{2,0,1:T(8,128)S(1)}, f32[128,4,128]{2,0,1:T(8,128)}, u32[]{:S(2)}) copy-start(f32[128,4,128]{2,0,1:T(8,128)} %get-tuple-element.97) | copy-start | bytes 786436
  218.1 9.2 %copy-start.13 = (bf16[8,16,4096]{2,1,0:T(8,128)(2,1)S(1)}, bf16[8,16,4096]{2,1,0:T(8,128)(2,1)}, u32[]{:S(2)}) copy-start(bf16[8,16,4096]{2,1,0:T(8,128)(2,1)} %copy-done.12) | copy-start | bytes 3145732
  220.4 13.2 %all-to-all-start.8 = ((f32[8,1,4096]{2,1,0:T(1,128)}), f32[8,1,4096]{2,1,0:T(1,128)}, u32[]{:S(2)}, u32[]{:S(2)}) async-start(f32[8,1,4096]{2,1,0:T(1,128)} %broadcast_in_dim.59), calls=%async_computation.8 | async-start | bytes 262144 | tf_op jit(solution)/shard_map/all_to_all | solution.py:97
  233.6 10.2 %copy-start.6 = (bf16[128,4096]{1,0:T(8,128)(2,1)S(1)}, bf16[128,4096]{1,0:T(8,128)(2,1)}, u32[]{:S(2)}) copy-start(bf16[128,4096]{1,0:T(8,128)(2,1)} %copy-done.5) | copy-start | bytes 3145732
  233.6 10.2 %copy-start.47 = (bf16[128,128]{0,1:T(8,128)(2,1)S(1)}, bf16[128,128]{0,1:T(8,128)(2,1)}, u32[]{:S(2)}) copy-start(bf16[128,128]{0,1:T(8,128)(2,1)} %copy-done.46) | copy-start | bytes 98308
  233.6 10.2 %copy-start.49 = (bf16[128,128]{0,1:T(8,128)(2,1)S(1)}, bf16[128,128]{0,1:T(8,128)(2,1)}, u32[]{:S(2)}) copy-start(bf16[128,128]{0,1:T(8,128)(2,1)} %copy-done.48) | copy-start | bytes 98308
  233.6 23.5 %all-to-all-start.3 = ((bf16[8,16,4096]{2,1,0:T(8,128)(2,1)}), bf16[8,16,4096]{2,1,0:T(8,128)(2,1)}, u32[]{:S(2)}, u32[]{:S(2)}) async-start(bf16[8,16,4096]{2,1,0:T(8,128)(2,1)} %bitcast.391), calls=%async_computation.3 | async-start | bytes 2097152 | tf_op jit(solution)/shard_map/all_to_all | solution.py:102
  255.5 10.3 %copy-start.19 = (bf16[16,4096]{1,0:T(8,128)(2,1)S(1)}, bf16[16,4096]{1,0:T(8,128)(2,1)}, u32[]{:S(2)}) copy-start(bf16[16,4096]{1,0:T(8,128)(2,1)} %broadcast_select_fusion.1) | copy-start | bytes 393220
  257.1 22.1 %all-to-all-start.7 = ((bf16[8,16,4096]{2,1,0:T(8,128)(2,1)}), bf16[8,16,4096]{2,1,0:T(8,128)(2,1)S(1)}, u32[]{:S(2)}, u32[]{:S(2)}) async-start(bf16[8,16,4096]{2,1,0:T(8,128)(2,1)} %bitcast.390), calls=%async_computation.7 | async-start | bytes 2097152 | tf_op jit(solution)/shard_map/all_to_all | solution.py:102
  264.3 16.1 %copy-start.37 = (bf16[1,16,4096]{2,1,0:T(8,128)(2,1)S(1)}, bf16[1,16,4096]{2,1,0:T(8,128)(2,1)}, u32[]{:S(2)}) copy-start(bf16[1,16,4096]{2,1,0:T(8,128)(2,1)} %fusion.123) | copy-start | bytes 393220
  264.3 16.9 %copy-start.18 = (bf16[16,4096]{1,0:T(8,128)(2,1)S(1)}, bf16[16,4096]{1,0:T(8,128)(2,1)}, u32[]{:S(2)}) copy-start(bf16[16,4096]{1,0:T(8,128)(2,1)} %copy-done.17) | copy-start | bytes 393220
  (49 other events, 101.5 us)

commit v2 on v0

v2 whole, which is shorter than its diff:
```python
import functools

import jax
import jax.numpy as jnp
import numpy as np
from jax import lax
from jax.experimental import pallas as pl
from jax.experimental.pallas import tpu as pltpu
from jax.sharding import PartitionSpec as P

HEAD = 128
EPSILON = 1e-05
ROPE_BASE = 10000.0
CHUNK = 512
VMEM_BYTES = 24 * 1024 * 1024
SHARD = 16
RING = 4
WHOLE = pl.BlockSpec(memory_space=pltpu.VMEM)

NN = (((1,), (0,)), ((), ()))
NT = (((1,), (1,)), ((), ()))
TN = (((0,), (0,)), ((), ()))


def dot(left, right, dims):
    return lax.dot_general(left, right, dims, preferred_element_type=jnp.float32)


def row_tables(token_count):
    lane = lax.axis_index("tensor")
    flip, ahead = np.meshgrid(np.arange(2), np.arange(RING), indexing="ij")
    blocks = ((lane // RING) ^ flip) * RING + (lane + ahead) % RING
    rows = blocks.reshape(-1, 1) * SHARD + np.arange(token_count // blocks.size)
    positions = rows.reshape(-1).astype(jnp.float32)
    exponents = np.arange(HEAD // 2, dtype=np.float32) * np.float32(2.0 / HEAD)
    angles = positions[:, None] * (np.float32(ROPE_BASE) ** (-exponents))[None, :]
    cosine, sine = jnp.cos(angles), jnp.sin(angles)
    return (
        jnp.concatenate([cosine, cosine], axis=1),
        jnp.concatenate([-sine, sine], axis=1),
        (positions[:, None] >= positions[None, :]).astype(jnp.float32),
    )


def rotated(values, cosine, signed_sine):
    return values * cosine + pltpu.roll(values, HEAD // 2, 1) * signed_sine


def rotated_back(values, cosine, signed_sine):
    return values * cosine - pltpu.roll(values, HEAD // 2, 1) * signed_sine


def stacked_heads(wide):
    return jnp.concatenate(
        [wide[:, first : first + HEAD] for first in range(0, wide.shape[1], HEAD)], axis=0
    )


def side_by_side(stacked, tokens):
    return jnp.concatenate(
        [stacked[first : first + tokens] for first in range(0, stacked.shape[0], tokens)], axis=1
    )


def columns(refs, part):
    if len(refs) == 2:
        return jnp.concatenate([ref[:, part] for ref in refs], axis=0)
    pieces = [ref[:SHARD, part] for ref in refs] + [ref[SHARD:, part] for ref in refs]
    return jnp.concatenate(pieces, axis=0)


def attend(x_ref, gain_ref, wq_ref, wk_ref, wv_ref, tables, normed_ref=None):
    cos_ref, sin_ref, mask_ref = tables
    tokens, width = cos_ref.shape[0], wq_ref.shape[0]
    squares = jnp.zeros((tokens, HEAD), jnp.float32)
    for first in range(0, width, HEAD):
        block = columns(x_ref, slice(first, first + HEAD)).astype(jnp.float32)
        squares = squares + block * block
    inverse = lax.rsqrt(jnp.sum(squares, axis=1, keepdims=True) * (1.0 / width) + EPSILON)
    queries = jnp.zeros((tokens, wq_ref.shape[1]), jnp.float32)
    pair = jnp.zeros((tokens, 2 * HEAD), jnp.float32)
    for first in range(0, width, CHUNK):
        part = slice(first, first + CHUNK)
        normed = (
            columns(x_ref, part).astype(jnp.float32) * inverse * gain_ref[:, part]
        ).astype(jnp.bfloat16)
        if normed_ref is not None:
            normed_ref[:, part] = normed
        queries = queries + dot(normed, wq_ref[part, :], NN)
        both = jnp.concatenate([wk_ref[part, :], wv_ref[part, :]], axis=1)
        pair = pair + dot(normed, both, NN)
    cosine, sine = cos_ref[...], sin_ref[...]
    query = jnp.concatenate(
        [
            rotated(queries[:, first : first + HEAD], cosine, sine).astype(jnp.bfloat16)
            for first in range(0, queries.shape[1], HEAD)
        ],
        axis=0,
    )
    key = rotated(pair[:, :HEAD], cosine, sine).astype(jnp.bfloat16)
    value = pair[:, HEAD:].astype(jnp.bfloat16)
    scores = dot(query, key, NT) * HEAD ** (-0.5)
    causal = jnp.concatenate([mask_ref[...]] * (scores.shape[0] // tokens), axis=0) > 0.0
    terms = jnp.where(causal, jnp.exp(scores), 0.0)
    probability = terms / jnp.sum(terms, axis=1, keepdims=True)
    attended = dot(probability.astype(jnp.bfloat16), value, NN).astype(jnp.bfloat16)
    return inverse, query, key, value, probability, side_by_side(attended, tokens)


def forward_kernel(*refs):
    x_refs, (gain_ref, wq_ref, wk_ref, wv_ref, wo_ref) = refs[:RING], refs[RING : RING + 5]
    tables, (near_ref, far_ref) = refs[RING + 5 : RING + 8], refs[RING + 8 :]
    half = near_ref.shape[0]
    attended = attend(x_refs, gain_ref, wq_ref, wk_ref, wv_ref, tables)[5]
    for first in range(0, wo_ref.shape[1], CHUNK):
        part = slice(first, first + CHUNK)
        term = dot(attended, wo_ref[:, part], NN).astype(jnp.bfloat16)
        near_ref[:, part] = term[:half]
        far_ref[:, part] = term[half:]


def recompute_kernel(*refs):
    x_refs, (gain_ref, wq_ref, wk_ref, wv_ref) = refs[:RING], refs[RING : RING + 4]
    tables, outs = refs[RING + 4 : RING + 7], refs[RING + 7 :]
    (
        normed_ref,
        inverse_ref,
        query_ref,
        key_ref,
        value_ref,
        probability_ref,
        attended_ref,
    ) = outs
    inverse, query, key, value, probability, attended = attend(
        x_refs, gain_ref, wq_ref, wk_ref, wv_ref, tables, normed_ref
    )
    inverse_ref[...] = jnp.broadcast_to(inverse, inverse_ref.shape)
    query_ref[...] = query
    key_ref[...] = key
    value_ref[...] = value
    probability_ref[...] = probability
    attended_ref[...] = attended


def backward_kernel(*refs):
    grad_refs, x_refs, refs = refs[:2], refs[2 : 2 + RING], refs[2 + RING :]
    inverse_ref, query_ref, key_ref, value_ref, probability_ref = refs[:5]
    wq_ref, wk_ref, wv_ref, wo_ref = refs[5:9]
    (cos_ref, sin_ref), rest = refs[9:11], refs[11:]
    term_refs, rest = rest[-4 - RING : -4], rest[: -4 - RING] + rest[-4:]
    gain_out_ref, query_grad_ref, key_grad_ref, value_grad_ref = rest[-4:]
    earlier_gain_ref = rest[0] if len(rest) > 4 else None
    tokens, width = cos_ref.shape[0], wq_ref.shape[0]
    grad_attended = jnp.zeros((tokens, wo_ref.shape[0]), jnp.float32)
    for first in range(0, width, CHUNK):
        part = slice(first, first + CHUNK)
        grad_attended = grad_attended + dot(columns(grad_refs, part), wo_ref[:, part], NT)
    grads = stacked_heads(grad_attended.astype(jnp.bfloat16))
    probability = probability_ref[...]
    key, value, query = key_ref[...], value_ref[...], query_ref[...]
    grad_probability = dot(grads, value, NT)
    row_terms = jnp.sum(grad_probability * probability, axis=1, keepdims=True)
    grad_scores = (
        probability * (grad_probability - row_terms) * HEAD ** (-0.5)
    ).astype(jnp.bfloat16)
    cosine, sine = cos_ref[...], sin_ref[...]
    raw = dot(grad_scores, key, NN)
    query_grad = jnp.concatenate(
        [
            rotated_back(raw[first : first + tokens], cosine, sine).astype(jnp.bfloat16)
            for first in range(0, raw.shape[0], tokens)
        ],
        axis=1,
    )
    key_grad = rotated_back(dot(grad_scores, query, TN), cosine, sine).astype(jnp.bfloat16)
    value_grad = dot(probability.astype(jnp.bfloat16), grads, TN).astype(jnp.bfloat16)
    query_grad_ref[...] = query_grad
    key_grad_ref[...] = key_grad
    value_grad_ref[...] = value_grad
    pair_grad = jnp.concatenate([key_grad, value_grad], axis=1)
    inverse = inverse_ref[:, :1]
    gains = []
    for first in range(0, width, CHUNK):
        part = slice(first, first + CHUNK)
        both = jnp.concatenate([wk_ref[part, :], wv_ref[part, :]], axis=1)
        term = dot(query_grad, wq_ref[part, :], NT) + dot(pair_grad, both, NT)
        term = term.astype(jnp.bfloat16)
        for ahead, term_ref in enumerate(term_refs):
            for flip in range(2):
                start = (flip * RING + ahead) * SHARD
                rows = slice(flip * SHARD, flip * SHARD + SHARD)
                term_ref[rows, part] = term[start : start + SHARD]
        gains.append(
            jnp.sum(
                term.astype(jnp.float32) * columns(x_refs, part).astype(jnp.float32) * inverse,
                axis=0,
                keepdims=True,
            )
        )
    gain = jnp.concatenate(gains, axis=0)
    if earlier_gain_ref is not None:
        gain = gain + earlier_gain_ref[...]
    gain_out_ref[...] = gain


def wide(value):
    return value.astype(jnp.float32)


def parts_of(width):
    return [slice(first, first + CHUNK) for first in range(0, width, CHUNK)]


def halve_forward_kernel(near_ref, arrived_ref, own_ref, *send_refs):
    for part in parts_of(own_ref.shape[1]):
        total = wide(near_ref[:, part]) + wide(arrived_ref[:, part])
        own_ref[:, part] = total[:SHARD]
        for ahead, ref in enumerate(send_refs, 1):
            ref[:, part] = total[ahead * SHARD : ahead * SHARD + SHARD].astype(jnp.bfloat16)


def finish_forward_kernel(x_ref, own_ref, one_ref, two_ref, three_ref, *rest):
    out_ref = rest[-1]
    if len(rest) > 1:
        out_ref[0] = rest[0][...]
        out_ref = out_ref.at[1]
    for part in parts_of(x_ref.shape[1]):
        total = own_ref[:, part] + wide(one_ref[:, part])
        total = total + wide(two_ref[:, part]) + wide(three_ref[:, part])
        out_ref[:, part] = (wide(x_ref[:SHARD, part]) + total).astype(jnp.bfloat16)


def quarter_backward_kernel(kept_ref, one_ref, two_ref, three_ref, own_ref, send_ref):
    for part in parts_of(own_ref.shape[1]):
        total = wide(kept_ref[:, part]) + wide(one_ref[:, part])
        total = total + wide(two_ref[:, part]) + wide(three_ref[:, part])
        own_ref[:, part] = total[:SHARD]
        send_ref[:, part] = total[SHARD:].astype(jnp.bfloat16)


def finish_backward_kernel(own_ref, arrived_ref, x_ref, grad_ref, gain_ref, *rest):
    out_ref = rest[-1]
    if len(rest) > 1:
        out_ref[0] = rest[0][...]
        out_ref = out_ref.at[1]
    width = own_ref.shape[1]
    squares = jnp.zeros((SHARD, 1), jnp.float32)
    crosses = jnp.zeros((SHARD, 1), jnp.float32)
    scaled = []
    for part in parts_of(width):
        own = wide(x_ref[:SHARD, part])
        scaled.append((own_ref[:, part] + wide(arrived_ref[:, part])) * gain_ref[:, part])
        squares = squares + jnp.sum(own * own, axis=1, keepdims=True)
        crosses = crosses + jnp.sum(scaled[-1] * own, axis=1, keepdims=True)
    inverse = lax.rsqrt(squares * (1.0 / width) + EPSILON)
    factor = inverse * inverse * inverse * (crosses * (1.0 / width))
    for part, scaled_part in zip(parts_of(width), scaled):
        out_ref[:, part] = (
            wide(grad_ref[:SHARD, part])
            + inverse * scaled_part
            - wide(x_ref[:SHARD, part]) * factor
        ).astype(jnp.bfloat16)


def weight_gradient_kernel(
    normed_a,
    normed_b,
    grad_a_near,
    grad_a_far,
    grad_b_near,
    grad_b_far,
    att_a,
    att_b,
    qg_a,
    qg_b,
    kg_a,
    kg_b,
    vg_a,
    vg_b,
    gq_ref,
    gk_ref,
    gv_ref,
    go_ref,
):
    def over(top, bottom):
        return jnp.concatenate([top[...], bottom[...]], axis=0)

    part = pl.ds(pl.multiple_of(pl.program_id(0) * CHUNK, CHUNK), CHUNK)
    normed = jnp.concatenate([normed_a[:, part], normed_b[:, part]], axis=0)
    grad = jnp.concatenate(
        [ref[:, part] for ref in (grad_a_near, grad_a_far, grad_b_near, grad_b_far)], axis=0
    )
    gq_ref[...] = dot(normed, over(qg_a, qg_b), TN).astype(jnp.bfloat16)
    pair = jnp.concatenate([over(kg_a, kg_b), over(vg_a, vg_b)], axis=1)
    both = dot(normed, pair, TN).astype(jnp.bfloat16)
    gk_ref[...] = both[:, :HEAD]
    gv_ref[...] = both[:, HEAD:]
    go_ref[...] = dot(over(att_a, att_b), grad, TN).astype(jnp.bfloat16)


def estimate(flops, moved):
    return pl.CostEstimate(flops=int(flops), bytes_accessed=int(moved), transcendentals=0)


def call(kernel, out_shape, operands, flops, moved, **extra):
    return pl.pallas_call(
        kernel,
        out_shape=out_shape,
        in_specs=[extra.get("specs", {}).get(index, WHOLE) for index in range(len(operands))],
        out_specs=jax.tree.map(lambda _: WHOLE, out_shape),
        compiler_params=pltpu.CompilerParams(vmem_limit_bytes=VMEM_BYTES),
        cost_estimate=estimate(flops, moved),
        name=extra["name"],
    )(*operands)


def shaped(shape, dtype=jnp.bfloat16):
    return jax.ShapeDtypeStruct(shape, dtype)


def forward_term(pieces, gain, weights, tables):
    tokens, width = tables[0].shape[0], pieces[0].shape[1]
    size = sum(w.size for w in weights)
    return call(
        forward_kernel,
        (shaped((tokens // 2, width)), shaped((tokens // 2, width))),
        (*pieces, gain, *weights, *tables),
        4 * tokens * size,
        2 * size,
        name="layer_term",
    )


def recomputed(pieces, gain, weights, tables):
    tokens, width = tables[0].shape[0], pieces[0].shape[1]
    wq, wk, wv, _ = weights
    size = wq.size + wk.size + wv.size
    stacked = tokens * wq.shape[1] // HEAD
    return call(
        recompute_kernel,
        (
            shaped((tokens, width)),
            shaped((tokens, HEAD), jnp.float32),
            shaped((stacked, HEAD)),
            shaped((tokens, HEAD)),
            shaped((tokens, HEAD)),
            shaped((stacked, HEAD), jnp.float32),
            shaped((tokens, wq.shape[1])),
        ),
        (*pieces, gain, wq, wk, wv, *tables),
        4 * tokens * size,
        2 * size,
        name="recompute",
    )


def backward_term(grads, pieces, saved, weights, tables, *earlier_gain):
    tokens, width = tables[0].shape[0], grads[0].shape[1]
    size = sum(w.size for w in weights)
    out = call(
        backward_kernel,
        (shaped((tokens // RING, width)),) * RING
        + (
            shaped((width // CHUNK, CHUNK), jnp.float32),
            shaped((tokens, weights[0].shape[1])),
            shaped((tokens, HEAD)),
            shaped((tokens, HEAD)),
        ),
        (*grads, *pieces, *saved[1:6], *weights, *tables[:2], *earlier_gain),
        4 * tokens * size,
        2 * size,
        name="layer_gradient_term",
    )
    return out[:RING], out[RING:]


def small(kernel, out_shape, *operands):
    size = sum(x.size for x in operands)
    return call(kernel, out_shape, operands, size, 2 * size, name=kernel.__name__)


def weight_gradients(normed, grads, attended, query_grads, key_grads, value_grads):
    tokens, width = normed[0].shape
    heads = attended[0].shape[1]
    size = width * (2 * heads + 2 * HEAD)
    return pl.pallas_call(
        weight_gradient_kernel,
        grid=(width // CHUNK,),
        out_shape=(
            shaped((width, heads)),
            shaped((width, HEAD)),
            shaped((width, HEAD)),
            shaped((heads, width)),
        ),
        in_specs=[WHOLE] * 14,
        out_specs=(
            pl.BlockSpec((CHUNK, heads), lambda i: (i, 0)),
            pl.BlockSpec((CHUNK, HEAD), lambda i: (i, 0)),
            pl.BlockSpec((CHUNK, HEAD), lambda i: (i, 0)),
            pl.BlockSpec((heads, CHUNK), lambda i: (0, i)),
        ),
        compiler_params=pltpu.CompilerParams(vmem_limit_bytes=VMEM_BYTES),
        cost_estimate=estimate(4 * tokens * size, 2 * size),
        name="weight_gradients",
    )(*normed, *grads[0], *grads[1], *attended, *query_grads, *key_grads, *value_grads)


def moved(x, route, sections=None):
    count, lanes = lax.axis_size("pipe"), lax.axis_size("tensor")
    pairs = []
    for section in range(count) if sections is None else sections:
        for lane in range(lanes):
            to_section, to_lane = route(section, lane)
            if 0 <= to_section < count:
                pairs.append((section * lanes + lane, to_section * lanes + to_lane))
    return lax.ppermute(x, ("pipe", "tensor"), pairs)


def around(lane, by):
    return lane // RING * RING + (lane + by) % RING


def across(x, sections=None):
    return moved(x, lambda section, lane: (section, lane ^ RING), sections)


def from_ahead(x, sections=None):
    return [
        moved(x, lambda section, lane, by=by: (section, around(lane, -by)), sections)
        for by in range(1, RING)
    ]


def to_ahead(xs):
    return [
        moved(x, lambda section, lane, by=by: (section, around(lane, by)))
        for by, x in enumerate(xs, 1)
    ]


def forward_reduced(near, far, x, *first):
    width = near.shape[1]
    piece = shaped((SHARD, width))
    own, *sent = small(
        halve_forward_kernel,
        (shaped((SHARD, width), jnp.float32),) + (piece,) * (RING - 1),
        near,
        across(far),
    )
    out = shaped((2,) * len(first) + (SHARD, width))
    return small(finish_forward_kernel, out, x, own, *to_ahead(sent), *first)


def backward_reduced(terms, x, grad, gain, *first):
    width = terms[0].shape[1]
    own, sent = small(
        quarter_backward_kernel,
        (shaped((SHARD, width), jnp.float32), shaped((SHARD, width))),
        terms[0],
        *to_ahead(terms[1:]),
    )
    out = shaped((2,) * len(first) + (SHARD, width))
    return small(finish_backward_kernel, out, own, across(sent), x, grad, gain, *first)


def saved_pieces(rows, lane):
    blocks = [
        lax.dynamic_slice_in_dim(rows, block * SHARD, SHARD, 0) for block in (lane, lane ^ RING)
    ]
    mine = moved(
        jnp.concatenate(blocks),
        lambda section, lane: (lax.axis_size("pipe") - 1 - section, lane),
    )
    return (mine, *from_ahead(mine))


def summed_gain(gain):
    pair = gain + across(gain)
    return sum(from_ahead(pair), pair)


def per_device(
    forward_in,
    entering,
    backward_in,
    loss_grad,
    stashed,
    norm_gain,
    w_query,
    key_projection,
    value_projection,
    w_out,
):
    sections = lax.axis_size("pipe")
    section_index = lax.axis_index("pipe")
    lane = lax.axis_index("tensor")
    tables = row_tables(stashed.shape[2])
    weights = (w_query[0], key_projection[0], value_projection[0], w_out[0])
    gain = norm_gain

    own_in, own_grad = forward_in[0], backward_in[0]
    in_pair = jnp.concatenate([own_in, across(own_in)])
    in_pieces = (in_pair, *from_ahead(in_pair))
    grad_near = jnp.concatenate([own_grad, *from_ahead(own_grad)])
    first_grads = (grad_near, across(grad_near))
    pieces = [saved_pieces(stashed[0, tick], lane) for tick in range(2)]
    enter_pair = jnp.concatenate([entering, across(entering, [0])])
    last = sections - 1
    loss_near = jnp.concatenate([loss_grad, *from_ahead(loss_grad, [last])])

    first_terms = forward_term(in_pieces, gain, weights, tables)
    saved = [recomputed(rows, gain, weights, tables) for rows in pieces]
    first_back_terms, first_grad_parts = backward_term(
        first_grads, pieces[0], saved[0], weights, tables
    )
    first_out = forward_reduced(*first_terms, own_in)
    next_in = jnp.concatenate(
        [
            moved(first_out, lambda section, lane: (section + 1, lane)),
            moved(first_out, lambda section, lane: (section + 1, lane ^ RING)),
        ]
    )
    next_pair = jnp.where(section_index == 0, enter_pair, next_in)
    next_pieces = (next_pair, *from_ahead(next_pair))

    first_back = backward_reduced(first_back_terms, pieces[0][0], own_grad, gain)
    next_grad = jnp.concatenate(
        [
            moved(first_back, lambda section, lane, by=by: (section - 1, around(lane, -by)))
            for by in range(RING)
        ]
    )
    next_near = jnp.where(section_index == last, loss_near, next_grad)
    second_grads = (next_near, across(next_near))

    second_terms = forward_term(next_pieces, gain, weights, tables)
    second_back_terms, second_grad_parts = backward_term(
        second_grads, pieces[1], saved[1], weights, tables, first_grad_parts[0]
    )
    forward_out = forward_reduced(*second_terms, next_pair, first_out)
    backward_out = backward_reduced(
        second_back_terms, pieces[1][0], next_near, gain, first_back
    )
    grad_gain = summed_gain(second_grad_parts[0])
    grad_query, key_weight_gradient, value_weight_gradient, grad_out = weight_gradients(
        (saved[0][0], saved[1][0]),
        (first_grads, second_grads),
        (saved[0][6], saved[1][6]),
        (first_grad_parts[1], second_grad_parts[1]),
        (first_grad_parts[2], second_grad_parts[2]),
        (first_grad_parts[3], second_grad_parts[3]),
    )
    return (
        forward_out[:, None],
        backward_out[:, None],
        grad_query[None],
        key_weight_gradient[None],
        value_weight_gradient[None],
        grad_out[None],
        grad_gain.reshape(1, -1),
    )


def solution(mesh):
    in_specs = (
        P("pipe", "tensor", None),
        P("tensor", None),
        P("pipe", "tensor", None),
        P("tensor", None),
        P("pipe", None, None, None),
        P("pipe", None),
        P("pipe", None, "tensor"),
        P("pipe", None, "tensor"),
        P("pipe", None, "tensor"),
        P("pipe", "tensor", None),
    )
    out_specs = (
        P(None, "pipe", "tensor", None),
        P(None, "pipe", "tensor", None),
        P("pipe", None, "tensor"),
        P("pipe", None, "tensor"),
        P("pipe", None, "tensor"),
        P("pipe", "tensor", None),
        P("pipe", None),
    )
    return jax.shard_map(
        per_device, mesh=mesh, in_specs=in_specs, out_specs=out_specs, check_vma=False
    )
```

time: 496 us -> 169 us (0.34)
  waiting for transfers between devices: 351 us -> 32 us
  matrix products: 79 us -> 0 us
  starting transfers between devices: 10.9 us -> 85 us
  Pallas kernels: 0 us -> 26.4 us
  other arithmetic: 23.9 us -> 5.3 us
  between operations: 14.8 us -> 1.19 us
    psum x2 -> x0, waiting for transfers between devices: 152 us -> none  [section_forward(): lax.psum(rounded.astype(jnp.bfloat16), 'tensor').astype(jnp.float32)]
    ppermute x6 -> x50, waiting for transfers between devices: 122 us -> 32 us  [moved(): return lax.ppermute(x, ('pipe', 'tensor'), pairs)]
    dot_general x44 -> x0, matrix products: 79 us -> none  [the longest x2 11.4 us: section_backward(): lax.dot_general(attended, grad_rows, contract_first, preferred_element_ty...]
    all_gather x4 -> x0, waiting for transfers between devices: 76 us -> none  [the longest x1 42.2 us: per_device(): lax.all_gather(loss_grad, 'tensor', axis=0, tiled=True)]
    ppermute x6 -> x50, starting transfers between devices: 10.4 us -> 85 us  [moved(): return lax.ppermute(x, ('pipe', 'tensor'), pairs)]
    pallas_call x0 -> x15, Pallas kernels: none -> 26.4 us  [the longest x14 19.9 us: call(): pl.pallas_call(kernel, out_shape=out_shape, in_specs=[extra.get('specs',...]
    convert_element_type x12 -> x2, other arithmetic: 10.3 us -> 0.16 us  [the longest x1 0.08 us: row_tables(): (positions[:, None] >= positions[None, :]).astype(jnp.float32)]
    unnamed x96 -> x65, local copies, waits for them, and re-layouts: 3.35 us -> 13.2 us
  transfers between devices with their start and end apart: 12 -> 50, of which waited for: 8 -> 15; matrix products, arithmetic and copies ran while one was open for 14% -> 7% of each run, Pallas kernels for 0% -> 15%
where the time goes in v2:
time: 169 us; the launch traced here: 168 us
  starting transfers between devices  85 us (50%)
  waiting for transfers between devices  32 us (19%)
  Pallas kernels  26.4 us (16%)
  local copies, waits for them, and re-layouts  18.3 us (11%)
  other arithmetic  5.3 us (3%)
    ppermute x50, starting transfers between devices, moved(): return lax.ppermute(x, ('pipe', 'tensor'), pairs)  85 us
    ppermute x50, waiting for transfers between devices, moved(): return lax.ppermute(x, ('pipe', 'tensor'), pairs)  32 us
    pallas_call x14, Pallas kernels, call(): pl.pallas_call(kernel, out_shape=out_shape, in_specs=[extra.get('specs',...  19.9 us
    unnamed x65, local copies, waits for them, and re-layouts  13.2 us
    pallas_call x1, Pallas kernels, weight_gradients(): pl.pallas_call(weight_gradient_kernel, grid=(width // CHUNK,), out_shape=...  6.46 us
  transfers between devices with their start and end apart: 50, of which 15 were waited for; matrix products, arithmetic and copies ran while one was open for 7% of the time, Pallas kernels for 15%

profile of v2, /device:TPU:0, one launch (start us, length us, event | category | flops | bytes accessed | tf_op | source)
XLA Modules:
  0.0 168.1 jit_solution(5142495275337256160)
XLA Ops:
  0.7 2.1 %collective-permute-start.23 = (bf16[16,4096]{1,0:T(8,128)(2,1)}, bf16[16,4096]{1,0:T(8,128)(2,1)S(1)}, u32[]{:S(2)}, u32[]{:S(2)}) collective-permute-start(bf16[16,4096]{1,0:T(8,128)(2,1)} %bitcast.53), channel_id=1, source_target_pairs={{0,1},{1,2},{2,3},{3,0},{4,5},{5,6},{6,7},{7,4},{8,9},{9,10},{10,1... | collective-permute-start | bytes 393224 | tf_op jit(solution)/shard_map/ppermute | solution.py:416
  2.8 3.6 %collective-permute-start.22 = (bf16[16,4096]{1,0:T(8,128)(2,1)}, bf16[16,4096]{1,0:T(8,128)(2,1)S(1)}, u32[]{:S(2)}, u32[]{:S(2)}) collective-permute-start(bf16[16,4096]{1,0:T(8,128)(2,1)} %bitcast.54), channel_id=1, source_target_pairs={{0,2},{1,3},{2,0},{3,1},{4,6},{5,7},{6,4},{7,5},{8,10},{9,11},{10,... | collective-permute-start | bytes 393224 | tf_op jit(solution)/shard_map/ppermute | solution.py:416
  7.4 3.2 %collective-permute-start.1 = (bf16[16,4096]{1,0:T(8,128)(2,1)}, bf16[16,4096]{1,0:T(8,128)(2,1)S(1)}, u32[]{:S(2)}, u32[]{:S(2)}) collective-permute-start(bf16[16,4096]{1,0:T(8,128)(2,1)} %bitcast.50), channel_id=1, source_target_pairs={{0,4},{1,5},{2,6},{3,7},{4,0},{5,1},{6,2},{7,3},{8,12},{9,13},{10,... | collective-permute-start | bytes 393224 | tf_op jit(solution)/shard_map/ppermute | solution.py:416
  10.6 3.1 %fusion.5 = (bf16[1,1,128,4096]{3,2,1,0:T(8,128)(2,1)}, bf16[1,1,128,4096]{3,2,1,0:T(8,128)(2,1)}) fusion(bf16[1,2,128,4096]{3,2,1,0:T(8,128)(2,1)} %param.18), kind=kLoop, calls=%fused_computation.26 | loop fusion | bytes 4194304 | tf_op jit(solution)/shard_map/slice | solution.py:506
  19.8 2.0 %collective-permute-start.2 = (bf16[32,4096]{1,0:T(8,128)(2,1)S(1)}, bf16[32,4096]{1,0:T(8,128)(2,1)S(1)}, u32[]{:S(2)}, u32[]{:S(2)}) collective-permute-start(bf16[32,4096]{1,0:T(8,128)(2,1)S(1)} %pad_maximum_fusion.1.refs_0_), channel_id=1, source_target_pairs={{0,3},{1,0},{2,1},{3,2},{4,7},{5,4},{6,5},{7,6},{8,11},{9,8},{10,9... | collective-permute-start | bytes 786440 | tf_op jit(solution)/shard_map/ppermute | solution.py:416
  22.8 1.9 %collective-permute-start.24 = (bf16[64,4096]{1,0:T(8,128)(2,1)S(1)}, bf16[64,4096]{1,0:T(8,128)(2,1)S(1)}, u32[]{:S(2)}, u32[]{:S(2)}) collective-permute-start(bf16[64,4096]{1,0:T(8,128)(2,1)S(1)} %pad_maximum_fusion.refs_0_.grad_a_near), channel_id=1, source_target_pairs={{0,4},{1,5},{2,6},{3,7},{4,0},{5,1},{6,2},{7,3},{8,12},{9,13},{10,... | collective-permute-start | bytes 1572872 | tf_op jit(solution)/shard_map/ppermute | solution.py:416
  27.6 5.7 %collective-permute-done.4.refs_3_ = bf16[32,4096]{1,0:T(8,128)(2,1)S(1)} collective-permute-done((bf16[32,4096]{1,0:T(8,128)(2,1)S(1)}, bf16[32,4096]{1,0:T(8,128)(2,1)S(1)}, u32[]{:S(2)}, u32[]{:S(2)}) %collective-permute-start.4) | collective-permute-done | bytes 262176 | tf_op jit(solution)/shard_map/ppermute | solution.py:416
  34.5 2.2 %copy-done = bf16[1,4096,512]{2,1,0:T(8,128)(2,1)S(1)} copy-done((bf16[1,4096,512]{2,1,0:T(8,128)(2,1)S(1)}, bf16[1,4096,512]{2,1,0:T(8,128)(2,1)}, u32[]{:S(2)}) %copy-start) | copy-done | bytes 4194328
  36.7 2.2 %copy-done.4 = bf16[1,512,4096]{2,1,0:T(8,128)(2,1)S(1)} copy-done((bf16[1,512,4096]{2,1,0:T(8,128)(2,1)S(1)}, bf16[1,512,4096]{2,1,0:T(8,128)(2,1)}, u32[]{:S(2)}) %copy-start.4) | copy-done | bytes 4194328
  38.9 2.8 %layer_term.2 = (bf16[64,4096]{1,0:T(8,128)(2,1)S(1)}, bf16[64,4096]{1,0:T(8,128)(2,1)S(1)}) custom-call(bf16[32,4096]{1,0:T(8,128)(2,1)S(1)} %pad_maximum_fusion.1.refs_0_, bf16[32,4096]{1,0:T(8,128)(2,1)S(1)} %collective-permute-done.2.refs_1_, bf16[32,4096]{1,0:T(8,128)(2,1)S(1)} %collective-permute-done.3.refs_2_, ...), custom_call_target="tpu_custom_call" | custom-call | flops 2684354560 | bytes 10485760 | tf_op jit(solution)/shard_map/layer_term/pallas_call | solution.py:306
  41.7 1.9 %collective-permute-start.5 = (bf16[64,4096]{1,0:T(8,128)(2,1)S(1)}, bf16[64,4096]{1,0:T(8,128)(2,1)S(1)}, u32[]{:S(2)}, u32[]{:S(2)}) collective-permute-start(bf16[64,4096]{1,0:T(8,128)(2,1)S(1)} %get-tuple-element.58), channel_id=1, source_target_pairs={{0,4},{1,5},{2,6},{3,7},{4,0},{5,1},{6,2},{7,3},{8,12},{9,13},{10,... | collective-permute-start | bytes 1572872 | tf_op jit(solution)/shard_map/ppermute | solution.py:416
  47.7 4.2 %layer_gradient_term.2 = (bf16[32,4096]{1,0:T(8,128)(2,1)S(1)}, bf16[32,4096]{1,0:T(8,128)(2,1)S(1)}, bf16[32,4096]{1,0:T(8,128)(2,1)S(1)}, bf16[32,4096]{1,0:T(...) custom-call(bf16[64,4096]{1,0:T(8,128)(2,1)S(1)} %pad_maximum_fusion, ...), custom_call_target="tpu_custom_call" | custom-call | flops 2684354560 | bytes 10485760 | tf_op jit(solution)/shard_map/layer_gradient_term/pallas_call | solution.py:306
  54.1 3.6 %collective-permute-start.30 = (bf16[32,4096]{1,0:T(8,128)(2,1)S(1)}, bf16[32,4096]{1,0:T(8,128)(2,1)S(1)}, u32[]{:S(2)}, u32[]{:S(2)}) collective-permute-start(bf16[32,4096]{1,0:T(8,128)(2,1)S(1)} %get-tuple-element.76), channel_id=1, source_target_pairs={{0,2},{1,3},{2,0},{3,1},{4,6},{5,7},{6,4},{7,5},{8,10},{9,11},{10,... | collective-permute-start | bytes 786440 | tf_op jit(solution)/shard_map/ppermute | solution.py:416
  57.9 2.0 %collective-permute-start.6 = (bf16[16,4096]{1,0:T(8,128)(2,1)S(1)}, bf16[16,4096]{1,0:T(8,128)(2,1)S(1)}, u32[]{:S(2)}, u32[]{:S(2)}) collective-permute-start(bf16[16,4096]{1,0:T(8,128)(2,1)S(1)} %get-tuple-element.60), channel_id=1, source_target_pairs={{0,1},{1,2},{2,3},{3,0},{4,5},{5,6},{6,7},{7,4},{8,9},{9,10},{10,1... | collective-permute-start | bytes 393224 | tf_op jit(solution)/shard_map/ppermute | solution.py:416
  59.8 2.8 %collective-permute-start.7 = (bf16[16,4096]{1,0:T(8,128)(2,1)S(1)}, bf16[16,4096]{1,0:T(8,128)(2,1)S(1)}, u32[]{:S(2)}, u32[]{:S(2)}) collective-permute-start(bf16[16,4096]{1,0:T(8,128)(2,1)S(1)} %get-tuple-element.61), channel_id=1, source_target_pairs={{0,2},{1,3},{2,0},{3,1},{4,6},{5,7},{6,4},{7,5},{8,10},{9,11},{10,... | collective-permute-start | bytes 393224 | tf_op jit(solution)/shard_map/ppermute | solution.py:416
  63.4 1.9 %collective-permute-start.8 = (bf16[16,4096]{1,0:T(8,128)(2,1)S(1)}, bf16[16,4096]{1,0:T(8,128)(2,1)S(1)}, u32[]{:S(2)}, u32[]{:S(2)}) collective-permute-start(bf16[16,4096]{1,0:T(8,128)(2,1)S(1)} %get-tuple-element.62), channel_id=1, source_target_pairs={{0,3},{1,0},{2,1},{3,2},{4,7},{5,4},{6,5},{7,6},{8,11},{9,8},{10,9... | collective-permute-start | bytes 393224 | tf_op jit(solution)/shard_map/ppermute | solution.py:416
  65.3 5.1 %collective-permute-done.30.two_ref = bf16[32,4096]{1,0:T(8,128)(2,1)S(1)} collective-permute-done((bf16[32,4096]{1,0:T(8,128)(2,1)S(1)}, bf16[32,4096]{1,0:T(8,128)(2,1)S(1)}, u32[]{:S(2)}, u32[]{:S(2)}) %collective-permute-start.30) | collective-permute-done | bytes 262176 | tf_op jit(solution)/shard_map/ppermute | solution.py:416
  75.2 3.7 %collective-permute-start = (bf16[16,4096]{1,0:T(8,128)(2,1)}, bf16[16,4096]{1,0:T(8,128)(2,1)}, u32[]{:S(2)}, u32[]{:S(2)}) collective-permute-start(bf16[16,4096]{1,0:T(8,128)(2,1)} %param.15), channel_id=1, source_target_pairs={{0,4},{1,5},{2,6},{3,7},{4,0},{5,1},{6,2},{7,3}} | collective-permute-start | bytes 393224 | tf_op jit(solution)/shard_map/ppermute | solution.py:416
  79.0 1.9 %collective-permute-start.10 = (bf16[16,4096]{1,0:T(8,128)(2,1)S(1)}, bf16[16,4096]{1,0:T(8,128)(2,1)}, u32[]{:S(2)}, u32[]{:S(2)}) collective-permute-start(bf16[16,4096]{1,0:T(8,128)(2,1)S(1)} %finish_forward_kernel.2.rest_0_), channel_id=1, source_target_pairs={{0,12},{1,13},{2,14},{3,15},{4,8},{5,9},{6,10},{7,11},{8,20},{9,21... | collective-permute-start | bytes 393224 | tf_op jit(solution)/shard_map/ppermute | solution.py:416
  81.6 1.9 %collective-permute-start.9 = (bf16[16,4096]{1,0:T(8,128)(2,1)S(1)}, bf16[16,4096]{1,0:T(8,128)(2,1)}, u32[]{:S(2)}, u32[]{:S(2)}) collective-permute-start(bf16[16,4096]{1,0:T(8,128)(2,1)S(1)} %finish_forward_kernel.2.rest_0_), channel_id=1, source_target_pairs={{0,8},{1,9},{2,10},{3,11},{4,12},{5,13},{6,14},{7,15},{8,16},{9,17... | collective-permute-start | bytes 393224 | tf_op jit(solution)/shard_map/ppermute | solution.py:416
  93.4 10.7 %collective-permute-start.38 = (bf16[32,4096]{1,0:T(8,128)(2,1)}, bf16[32,4096]{1,0:T(8,128)(2,1)S(1)}, u32[]{:S(2)}, u32[]{:S(2)}) collective-permute-start(bf16[32,4096]{1,0:T(8,128)(2,1)} %pad_maximum_fusion.3), channel_id=1, source_target_pairs={{0,120},{1,121},{2,122},{3,123},{4,124},{5,125},{6,126},{7,127},{8... | collective-permute-start | bytes 786440 | tf_op jit(solution)/shard_map/ppermute | solution.py:416
  112.4 7.6 %collective-permute-done.13.refs_3_ = bf16[32,4096]{1,0:T(8,128)(2,1)S(1)} collective-permute-done((bf16[32,4096]{1,0:T(8,128)(2,1)S(1)}, bf16[32,4096]{1,0:T(8,128)(2,1)S(1)}, u32[]{:S(2)}, u32[]{:S(2)}) %collective-permute-start.13) | collective-permute-done | bytes 262176 | tf_op jit(solution)/shard_map/ppermute | solution.py:416
  121.1 2.2 %copy-done.2 = bf16[1,4096,512]{2,1,0:T(8,128)(2,1)S(1)} copy-done((bf16[1,4096,512]{2,1,0:T(8,128)(2,1)S(1)}, bf16[1,4096,512]{2,1,0:T(8,128)(2,1)}, u32[]{:S(2)}) %copy-start.2) | copy-done | bytes 4194328
  123.3 2.2 %copy-done.6 = bf16[1,512,4096]{2,1,0:T(8,128)(2,1)S(1)} copy-done((bf16[1,512,4096]{2,1,0:T(8,128)(2,1)S(1)}, bf16[1,512,4096]{2,1,0:T(8,128)(2,1)}, u32[]{:S(2)}) %copy-start.6) | copy-done | bytes 4194328
  125.5 2.8 %layer_term.3 = (bf16[64,4096]{1,0:T(8,128)(2,1)S(1)}, bf16[64,4096]{1,0:T(8,128)(2,1)S(1)}) custom-call(bf16[32,4096]{1,0:T(8,128)(2,1)S(1)} %maximum_select_fusion.1.refs_0_.x_ref, bf16[32,4096]{1,0:T(8,128)(2,1)S(1)} %collective-permute-done.11.refs_1_, bf16[32,4096]{1,0:T(8,128)(2,1)S(1)} %collective-permute-done.12.refs_2_, ...), custom_call_target="tpu_custom_call" | custom-call | flops 2684354560 | bytes 10485760 | tf_op jit(solution)/shard_map/layer_term/pallas_call | solution.py:306
  133.0 4.2 %layer_gradient_term.3 = (bf16[32,4096]{1,0:T(8,128)(2,1)S(1)}, bf16[32,4096]{1,0:T(8,128)(2,1)S(1)}, bf16[32,4096]{1,0:T(8,128)(2,1)S(1)}, bf16[32,4096]{1,0:T(...) custom-call(bf16[64,4096]{1,0:T(8,128)(2,1)S(1)} %maximum_select_fus, ...), custom_call_target="tpu_custom_call" | custom-call | flops 2684354560 | bytes 10485760 | tf_op jit(solution)/shard_map/layer_gradient_term/pallas_call | solution.py:306
  137.8 2.0 %collective-permute-start.46 = (f32[8,512]{1,0:T(8,128)S(1)}, f32[8,512]{1,0:T(8,128)S(1)}, u32[]{:S(2)}, u32[]{:S(2)}) collective-permute-start(f32[8,512]{1,0:T(8,128)S(1)} %get-tuple-element.106), channel_id=1, source_target_pairs={{0,4},{1,5},{2,6},{3,7},{4,0},{5,1},{6,2},{7,3},{8,12},{9,13},{10,... | collective-permute-start | bytes 49160 | tf_op jit(solution)/shard_map/ppermute | solution.py:416
  139.9 2.8 %collective-permute-start.43 = (bf16[32,4096]{1,0:T(8,128)(2,1)S(1)}, bf16[32,4096]{1,0:T(8,128)(2,1)S(1)}, u32[]{:S(2)}, u32[]{:S(2)}) collective-permute-start(bf16[32,4096]{1,0:T(8,128)(2,1)S(1)} %get-tuple-element.88), channel_id=1, source_target_pairs={{0,2},{1,3},{2,0},{3,1},{4,6},{5,7},{6,4},{7,5},{8,10},{9,11},{10,... | collective-permute-start | bytes 786440 | tf_op jit(solution)/shard_map/ppermute | solution.py:416
  144.8 3.5 %collective-permute-start.48 = (f32[8,512]{1,0:T(8,128)S(1)}, f32[8,512]{1,0:T(8,128)S(1)}, u32[]{:S(2)}, u32[]{:S(2)}) collective-permute-start(f32[8,512]{1,0:T(8,128)S(1)} %add.68), channel_id=1, source_target_pairs={{0,2},{1,3},{2,0},{3,1},{4,6},{5,7},{6,4},{7,5},{8,10},{9,11},{10,... | collective-permute-start | bytes 49160 | tf_op jit(solution)/shard_map/ppermute | solution.py:416
  149.3 6.5 %weight_gradients.1 = (bf16[4096,512]{1,0:T(8,128)(2,1)}, bf16[4096,128]{1,0:T(8,128)(2,1)}, bf16[4096,128]{1,0:T(8,128)(2,1)}, bf16[512,4096]{1,0:T(8,128)(2,1)}) custom-call(bf16[128,4096]{1,0:T(8,128)(2,1)S(1)} %copy-done.20, bf16[128,4096]{1,0:T(8,128)(2,1)S(1)} %get-tuple-element.93.normed_b, bf16[64,4096]{1,0:T(8,128)(2,1)S(1)} %pad_maximum_fusion.refs_0_.grad_a_near, ...), custom_call_target="tpu_custom_call" | custom-call | flops 2684354560 | bytes 10485760 | tf_op jit(solution)/shard_map/weight_gradients/pallas_call | solution.py:386
  157.6 2.4 %collective-permute-start.17 = (bf16[16,4096]{1,0:T(8,128)(2,1)S(1)}, bf16[16,4096]{1,0:T(8,128)(2,1)S(1)}, u32[]{:S(2)}, u32[]{:S(2)}) collective-permute-start(bf16[16,4096]{1,0:T(8,128)(2,1)S(1)} %get-tuple-element.68), channel_id=1, source_target_pairs={{0,3},{1,0},{2,1},{3,2},{4,7},{5,4},{6,5},{7,6},{8,11},{9,8},{10,9... | collective-permute-start | bytes 393224 | tf_op jit(solution)/shard_map/ppermute | solution.py:416
  161.5 4.9 %collective-permute-done.45.arrived_ref = bf16[16,4096]{1,0:T(8,128)(2,1)S(1)} collective-permute-done((bf16[16,4096]{1,0:T(8,128)(2,1)S(1)}, bf16[16,4096]{1,0:T(8,128)(2,1)S(1)}, u32[]{:S(2)}, u32[]{:S(2)}) %collective-permute-start.45) | collective-permute-done | bytes 131104 | tf_op jit(solution)/shard_map/ppermute | solution.py:416
  (165 shorter events, 57.3 us)
Async XLA Ops:
  0.7 18.4 %collective-permute-start.23 = (bf16[16,4096]{1,0:T(8,128)(2,1)}, bf16[16,4096]{1,0:T(8,128)(2,1)S(1)}, u32[]{:S(2)}, u32[]{:S(2)}) collective-permute-start(bf16[16,4096]{1,0:T(8,128)(2,1)} %bitcast.53), channel_id=1, source_target_pairs={{0,1},{1,2},{2,3},{3,0},{4,5},{5,6},{6,7},{7,4},{8,9},{9,10},{10,1... | collective-permute-start | bytes 393224 | tf_op jit(solution)/shard_map/ppermute | solution.py:416
  2.8 17.0 %collective-permute-start.22 = (bf16[16,4096]{1,0:T(8,128)(2,1)}, bf16[16,4096]{1,0:T(8,128)(2,1)S(1)}, u32[]{:S(2)}, u32[]{:S(2)}) collective-permute-start(bf16[16,4096]{1,0:T(8,128)(2,1)} %bitcast.54), channel_id=1, source_target_pairs={{0,2},{1,3},{2,0},{3,1},{4,6},{5,7},{6,4},{7,5},{8,10},{9,11},{10,... | collective-permute-start | bytes 393224 | tf_op jit(solution)/shard_map/ppermute | solution.py:416
  6.4 15.5 %collective-permute-start.21 = (bf16[16,4096]{1,0:T(8,128)(2,1)}, bf16[16,4096]{1,0:T(8,128)(2,1)}, u32[]{:S(2)}, u32[]{:S(2)}) collective-permute-start(bf16[16,4096]{1,0:T(8,128)(2,1)} %bitcast.55), channel_id=1, source_target_pairs={{0,3},{1,0},{2,1},{3,2},{4,7},{5,4},{6,5},{7,6},{8,11},{9,8},{10,9... | collective-permute-start | bytes 393224 | tf_op jit(solution)/shard_map/ppermute | solution.py:416
  18.0 15.3 %collective-permute-start.4 = (bf16[32,4096]{1,0:T(8,128)(2,1)S(1)}, bf16[32,4096]{1,0:T(8,128)(2,1)S(1)}, u32[]{:S(2)}, u32[]{:S(2)}) collective-permute-start(bf16[32,4096]{1,0:T(8,128)(2,1)S(1)} %pad_maximum_fusion.1.refs_0_), channel_id=1, source_target_pairs={{0,1},{1,2},{2,3},{3,0},{4,5},{5,6},{6,7},{7,4},{8,9},{9,10},{10,1... | collective-permute-start | bytes 786440 | tf_op jit(solution)/shard_map/ppermute | solution.py:416
  19.1 14.2 %collective-permute-start.3 = (bf16[32,4096]{1,0:T(8,128)(2,1)S(1)}, bf16[32,4096]{1,0:T(8,128)(2,1)S(1)}, u32[]{:S(2)}, u32[]{:S(2)}) collective-permute-start(bf16[32,4096]{1,0:T(8,128)(2,1)S(1)} %pad_maximum_fusion.1.refs_0_), channel_id=1, source_target_pairs={{0,2},{1,3},{2,0},{3,1},{4,6},{5,7},{6,4},{7,5},{8,10},{9,11},{10,... | collective-permute-start | bytes 786440 | tf_op jit(solution)/shard_map/ppermute | solution.py:416
  19.8 14.7 %collective-permute-start.2 = (bf16[32,4096]{1,0:T(8,128)(2,1)S(1)}, bf16[32,4096]{1,0:T(8,128)(2,1)S(1)}, u32[]{:S(2)}, u32[]{:S(2)}) collective-permute-start(bf16[32,4096]{1,0:T(8,128)(2,1)S(1)} %pad_maximum_fusion.1.refs_0_), channel_id=1, source_target_pairs={{0,3},{1,0},{2,1},{3,2},{4,7},{5,4},{6,5},{7,6},{8,11},{9,8},{10,9... | collective-permute-start | bytes 786440 | tf_op jit(solution)/shard_map/ppermute | solution.py:416
  22.8 24.9 %collective-permute-start.24 = (bf16[64,4096]{1,0:T(8,128)(2,1)S(1)}, bf16[64,4096]{1,0:T(8,128)(2,1)S(1)}, u32[]{:S(2)}, u32[]{:S(2)}) collective-permute-start(bf16[64,4096]{1,0:T(8,128)(2,1)S(1)} %pad_maximum_fusion.refs_0_.grad_a_near), channel_id=1, source_target_pairs={{0,4},{1,5},{2,6},{3,7},{4,0},{5,1},{6,2},{7,3},{8,12},{9,13},{10,... | collective-permute-start | bytes 1572872 | tf_op jit(solution)/shard_map/ppermute | solution.py:416
  26.5 18.0 %collective-permute-start.28 = (bf16[32,4096]{1,0:T(8,128)(2,1)S(1)}, bf16[32,4096]{1,0:T(8,128)(2,1)S(1)}, u32[]{:S(2)}, u32[]{:S(2)}) collective-permute-start(bf16[32,4096]{1,0:T(8,128)(2,1)S(1)} %collective-permute-done.25.refs_0_.refs_2_.x_ref), channel_id=1, source_target_pairs={{0,1},{1,2},{2,3},{3,0},{4,5},{5,6},{6,7},{7,4},{8,9},{9,10},{10,1... | collective-permute-start | bytes 786440 | tf_op jit(solution)/shard_map/ppermute | solution.py:416
  41.7 16.1 %collective-permute-start.5 = (bf16[64,4096]{1,0:T(8,128)(2,1)S(1)}, bf16[64,4096]{1,0:T(8,128)(2,1)S(1)}, u32[]{:S(2)}, u32[]{:S(2)}) collective-permute-start(bf16[64,4096]{1,0:T(8,128)(2,1)S(1)} %get-tuple-element.58), channel_id=1, source_target_pairs={{0,4},{1,5},{2,6},{3,7},{4,0},{5,1},{6,2},{7,3},{8,12},{9,13},{10,... | collective-permute-start | bytes 1572872 | tf_op jit(solution)/shard_map/ppermute | solution.py:416
  54.1 16.3 %collective-permute-start.30 = (bf16[32,4096]{1,0:T(8,128)(2,1)S(1)}, bf16[32,4096]{1,0:T(8,128)(2,1)S(1)}, u32[]{:S(2)}, u32[]{:S(2)}) collective-permute-start(bf16[32,4096]{1,0:T(8,128)(2,1)S(1)} %get-tuple-element.76), channel_id=1, source_target_pairs={{0,2},{1,3},{2,0},{3,1},{4,6},{5,7},{6,4},{7,5},{8,10},{9,11},{10,... | collective-permute-start | bytes 786440 | tf_op jit(solution)/shard_map/ppermute | solution.py:416
  57.6 12.8 %collective-permute-start.31 = (bf16[32,4096]{1,0:T(8,128)(2,1)S(1)}, bf16[32,4096]{1,0:T(8,128)(2,1)S(1)}, u32[]{:S(2)}, u32[]{:S(2)}) collective-permute-start(bf16[32,4096]{1,0:T(8,128)(2,1)S(1)} %get-tuple-element.77), channel_id=1, source_target_pairs={{0,3},{1,0},{2,1},{3,2},{4,7},{5,4},{6,5},{7,6},{8,11},{9,8},{10,9... | collective-permute-start | bytes 786440 | tf_op jit(solution)/shard_map/ppermute | solution.py:416
  57.9 15.9 %collective-permute-start.6 = (bf16[16,4096]{1,0:T(8,128)(2,1)S(1)}, bf16[16,4096]{1,0:T(8,128)(2,1)S(1)}, u32[]{:S(2)}, u32[]{:S(2)}) collective-permute-start(bf16[16,4096]{1,0:T(8,128)(2,1)S(1)} %get-tuple-element.60), channel_id=1, source_target_pairs={{0,1},{1,2},{2,3},{3,0},{4,5},{5,6},{6,7},{7,4},{8,9},{9,10},{10,1... | collective-permute-start | bytes 393224 | tf_op jit(solution)/shard_map/ppermute | solution.py:416
  59.8 15.4 %collective-permute-start.7 = (bf16[16,4096]{1,0:T(8,128)(2,1)S(1)}, bf16[16,4096]{1,0:T(8,128)(2,1)S(1)}, u32[]{:S(2)}, u32[]{:S(2)}) collective-permute-start(bf16[16,4096]{1,0:T(8,128)(2,1)S(1)} %get-tuple-element.61), channel_id=1, source_target_pairs={{0,2},{1,3},{2,0},{3,1},{4,6},{5,7},{6,4},{7,5},{8,10},{9,11},{10,... | collective-permute-start | bytes 393224 | tf_op jit(solution)/shard_map/ppermute | solution.py:416
  63.4 15.6 %collective-permute-start.8 = (bf16[16,4096]{1,0:T(8,128)(2,1)S(1)}, bf16[16,4096]{1,0:T(8,128)(2,1)S(1)}, u32[]{:S(2)}, u32[]{:S(2)}) collective-permute-start(bf16[16,4096]{1,0:T(8,128)(2,1)S(1)} %get-tuple-element.62), channel_id=1, source_target_pairs={{0,3},{1,0},{2,1},{3,2},{4,7},{5,4},{6,5},{7,6},{8,11},{9,8},{10,9... | collective-permute-start | bytes 393224 | tf_op jit(solution)/shard_map/ppermute | solution.py:416
  72.5 14.6 %collective-permute-start.19 = (bf16[16,4096]{1,0:T(8,128)(2,1)}, bf16[16,4096]{1,0:T(8,128)(2,1)}, u32[]{:S(2)}, u32[]{:S(2)}) collective-permute-start(bf16[16,4096]{1,0:T(8,128)(2,1)} %param.17), channel_id=1, source_target_pairs={{120,122},{121,123},{122,120},{123,121},{124,126},{125,127},{126,1... | collective-permute-start | bytes 393224 | tf_op jit(solution)/shard_map/ppermute | solution.py:416
  73.8 14.6 %collective-permute-start.18 = (bf16[16,4096]{1,0:T(8,128)(2,1)}, bf16[16,4096]{1,0:T(8,128)(2,1)}, u32[]{:S(2)}, u32[]{:S(2)}) collective-permute-start(bf16[16,4096]{1,0:T(8,128)(2,1)} %param.17), channel_id=1, source_target_pairs={{120,123},{121,120},{122,121},{123,122},{124,127},{125,124},{126,1... | collective-permute-start | bytes 393224 | tf_op jit(solution)/shard_map/ppermute | solution.py:416
  87.0 17.2 %collective-permute-start.36 = (bf16[16,4096]{1,0:T(8,128)(2,1)S(1)}, bf16[16,4096]{1,0:T(8,128)(2,1)S(1)}, u32[]{:S(2)}, u32[]{:S(2)}) collective-permute-start(bf16[16,4096]{1,0:T(8,128)(2,1)S(1)} %finish_backward_kernel.2.rest_0_), channel_id=1, source_target_pairs={{8,1},{9,2},{10,3},{11,0},{12,5},{13,6},{14,7},{15,4},{16,9},{17,1... | collective-permute-start | bytes 393224 | tf_op jit(solution)/shard_map/ppermute | solution.py:416
  88.4 16.9 %collective-permute-start.35 = (bf16[16,4096]{1,0:T(8,128)(2,1)S(1)}, bf16[16,4096]{1,0:T(8,128)(2,1)S(1)}, u32[]{:S(2)}, u32[]{:S(2)}) collective-permute-start(bf16[16,4096]{1,0:T(8,128)(2,1)S(1)} %finish_backward_kernel.2.rest_0_), channel_id=1, source_target_pairs={{8,2},{9,3},{10,0},{11,1},{12,6},{13,7},{14,4},{15,5},{16,10},{17,... | collective-permute-start | bytes 393224 | tf_op jit(solution)/shard_map/ppermute | solution.py:416
  89.7 17.0 %collective-permute-start.34 = (bf16[16,4096]{1,0:T(8,128)(2,1)S(1)}, bf16[16,4096]{1,0:T(8,128)(2,1)S(1)}, u32[]{:S(2)}, u32[]{:S(2)}) collective-permute-start(bf16[16,4096]{1,0:T(8,128)(2,1)S(1)} %finish_backward_kernel.2.rest_0_), channel_id=1, source_target_pairs={{8,3},{9,0},{10,1},{11,2},{12,7},{13,4},{14,5},{15,6},{16,11},{17,... | collective-permute-start | bytes 393224 | tf_op jit(solution)/shard_map/ppermute | solution.py:416
  91.0 17.0 %collective-permute-start.33 = (bf16[16,4096]{1,0:T(8,128)(2,1)S(1)}, bf16[16,4096]{1,0:T(8,128)(2,1)S(1)}, u32[]{:S(2)}, u32[]{:S(2)}) collective-permute-start(bf16[16,4096]{1,0:T(8,128)(2,1)S(1)} %finish_backward_kernel.2.rest_0_), channel_id=1, source_target_pairs={{8,0},{9,1},{10,2},{11,3},{12,4},{13,5},{14,6},{15,7},{16,8},{17,9... | collective-permute-start | bytes 393224 | tf_op jit(solution)/shard_map/ppermute | solution.py:416
  93.4 17.7 %collective-permute-start.38 = (bf16[32,4096]{1,0:T(8,128)(2,1)}, bf16[32,4096]{1,0:T(8,128)(2,1)S(1)}, u32[]{:S(2)}, u32[]{:S(2)}) collective-permute-start(bf16[32,4096]{1,0:T(8,128)(2,1)} %pad_maximum_fusion.3), channel_id=1, source_target_pairs={{0,120},{1,121},{2,122},{3,123},{4,124},{5,125},{6,126},{7,127},{8... | collective-permute-start | bytes 786440 | tf_op jit(solution)/shard_map/ppermute | solution.py:416
  104.2 15.8 %collective-permute-start.13 = (bf16[32,4096]{1,0:T(8,128)(2,1)S(1)}, bf16[32,4096]{1,0:T(8,128)(2,1)S(1)}, u32[]{:S(2)}, u32[]{:S(2)}) collective-permute-start(bf16[32,4096]{1,0:T(8,128)(2,1)S(1)} %maximum_select_fusion.1.refs_0_.x_ref), channel_id=1, source_target_pairs={{0,1},{1,2},{2,3},{3,0},{4,5},{5,6},{6,7},{7,4},{8,9},{9,10},{10,1... | collective-permute-start | bytes 786440 | tf_op jit(solution)/shard_map/ppermute | solution.py:416
  105.2 14.8 %collective-permute-start.12 = (bf16[32,4096]{1,0:T(8,128)(2,1)S(1)}, bf16[32,4096]{1,0:T(8,128)(2,1)S(1)}, u32[]{:S(2)}, u32[]{:S(2)}) collective-permute-start(bf16[32,4096]{1,0:T(8,128)(2,1)S(1)} %maximum_select_fusion.1.refs_0_.x_ref), channel_id=1, source_target_pairs={{0,2},{1,3},{2,0},{3,1},{4,6},{5,7},{6,4},{7,5},{8,10},{9,11},{10,... | collective-permute-start | bytes 786440 | tf_op jit(solution)/shard_map/ppermute | solution.py:416
  106.7 14.5 %collective-permute-start.11 = (bf16[32,4096]{1,0:T(8,128)(2,1)S(1)}, bf16[32,4096]{1,0:T(8,128)(2,1)S(1)}, u32[]{:S(2)}, u32[]{:S(2)}) collective-permute-start(bf16[32,4096]{1,0:T(8,128)(2,1)S(1)} %maximum_select_fusion.1.refs_0_.x_ref), channel_id=1, source_target_pairs={{0,3},{1,0},{2,1},{3,2},{4,7},{5,4},{6,5},{7,6},{8,11},{9,8},{10,9... | collective-permute-start | bytes 786440 | tf_op jit(solution)/shard_map/ppermute | solution.py:416
  109.1 23.8 %collective-permute-start.37 = (bf16[64,4096]{1,0:T(8,128)(2,1)S(1)}, bf16[64,4096]{1,0:T(8,128)(2,1)S(1)}, u32[]{:S(2)}, u32[]{:S(2)}) collective-permute-start(bf16[64,4096]{1,0:T(8,128)(2,1)S(1)} %maximum_select_fusion.refs_0_.grad_ref.grad_b_near), channel_id=1, source_target_pairs={{0,4},{1,5},{2,6},{3,7},{4,0},{5,1},{6,2},{7,3},{8,12},{9,13},{10,... | collective-permute-start | bytes 1572872 | tf_op jit(solution)/shard_map/ppermute | solution.py:416
  111.2 19.3 %collective-permute-start.41 = (bf16[32,4096]{1,0:T(8,128)(2,1)S(1)}, bf16[32,4096]{1,0:T(8,128)(2,1)S(1)}, u32[]{:S(2)}, u32[]{:S(2)}) collective-permute-start(bf16[32,4096]{1,0:T(8,128)(2,1)S(1)} %collective-permute-done.38.refs_0_.refs_2_.x_ref), channel_id=1, source_target_pairs={{0,1},{1,2},{2,3},{3,0},{4,5},{5,6},{6,7},{7,4},{8,9},{9,10},{10,1... | collective-permute-start | bytes 786440 | tf_op jit(solution)/shard_map/ppermute | solution.py:416
  128.3 16.5 %collective-permute-start.14 = (bf16[64,4096]{1,0:T(8,128)(2,1)S(1)}, bf16[64,4096]{1,0:T(8,128)(2,1)S(1)}, u32[]{:S(2)}, u32[]{:S(2)}) collective-permute-start(bf16[64,4096]{1,0:T(8,128)(2,1)S(1)} %get-tuple-element.64), channel_id=1, source_target_pairs={{0,4},{1,5},{2,6},{3,7},{4,0},{5,1},{6,2},{7,3},{8,12},{9,13},{10,... | collective-permute-start | bytes 1572872 | tf_op jit(solution)/shard_map/ppermute | solution.py:416
  139.9 16.0 %collective-permute-start.43 = (bf16[32,4096]{1,0:T(8,128)(2,1)S(1)}, bf16[32,4096]{1,0:T(8,128)(2,1)S(1)}, u32[]{:S(2)}, u32[]{:S(2)}) collective-permute-start(bf16[32,4096]{1,0:T(8,128)(2,1)S(1)} %get-tuple-element.88), channel_id=1, source_target_pairs={{0,2},{1,3},{2,0},{3,1},{4,6},{5,7},{6,4},{7,5},{8,10},{9,11},{10,... | collective-permute-start | bytes 786440 | tf_op jit(solution)/shard_map/ppermute | solution.py:416
  142.7 14.3 %collective-permute-start.44 = (bf16[32,4096]{1,0:T(8,128)(2,1)S(1)}, bf16[32,4096]{1,0:T(8,128)(2,1)S(1)}, u32[]{:S(2)}, u32[]{:S(2)}) collective-permute-start(bf16[32,4096]{1,0:T(8,128)(2,1)S(1)} %get-tuple-element.89), channel_id=1, source_target_pairs={{0,3},{1,0},{2,1},{3,2},{4,7},{5,4},{6,5},{7,6},{8,11},{9,8},{10,9... | collective-permute-start | bytes 786440 | tf_op jit(solution)/shard_map/ppermute | solution.py:416
  143.3 14.2 %collective-permute-start.49 = (f32[8,512]{1,0:T(8,128)S(1)}, f32[8,512]{1,0:T(8,128)S(1)}, u32[]{:S(2)}, u32[]{:S(2)}) collective-permute-start(f32[8,512]{1,0:T(8,128)S(1)} %add.68), channel_id=1, source_target_pairs={{0,1},{1,2},{2,3},{3,0},{4,5},{5,6},{6,7},{7,4},{8,9},{9,10},{10,1... | collective-permute-start | bytes 49160 | tf_op jit(solution)/shard_map/ppermute | solution.py:416
  144.8 15.2 %collective-permute-start.48 = (f32[8,512]{1,0:T(8,128)S(1)}, f32[8,512]{1,0:T(8,128)S(1)}, u32[]{:S(2)}, u32[]{:S(2)}) collective-permute-start(f32[8,512]{1,0:T(8,128)S(1)} %add.68), channel_id=1, source_target_pairs={{0,2},{1,3},{2,0},{3,1},{4,6},{5,7},{6,4},{7,5},{8,10},{9,11},{10,... | collective-permute-start | bytes 49160 | tf_op jit(solution)/shard_map/ppermute | solution.py:416
  148.3 12.6 %collective-permute-start.47 = (f32[8,512]{1,0:T(8,128)S(1)}, f32[8,512]{1,0:T(8,128)S(1)}, u32[]{:S(2)}, u32[]{:S(2)}) collective-permute-start(f32[8,512]{1,0:T(8,128)S(1)} %add.68), channel_id=1, source_target_pairs={{0,3},{1,0},{2,1},{3,2},{4,7},{5,4},{6,5},{7,6},{8,11},{9,8},{10,9... | collective-permute-start | bytes 49160 | tf_op jit(solution)/shard_map/ppermute | solution.py:416
  (50 other events, 607.8 us)

commit v3 on v2

v3 whole, which is shorter than its diff:
```python
import functools

import jax
import jax.numpy as jnp
import numpy as np
from jax import lax
from jax.experimental import pallas as pl
from jax.experimental.pallas import tpu as pltpu
from jax.sharding import PartitionSpec as P

HEAD = 128
EPSILON = 1e-05
ROPE_BASE = 10000.0
CHUNK = 512
LAYER_BYTES = 18 * 1024 * 1024
GRADIENT_BYTES = 14 * 1024 * 1024
SMALL_BYTES = 5 * 1024 * 1024
SETUP_BYTES = 56 * 1024 * 1024
SHARD = 16
RING = 4
WHOLE = pl.BlockSpec(memory_space=pltpu.VMEM)
SCALAR = pl.BlockSpec(memory_space=pltpu.SMEM)
AWAY = pl.BlockSpec(memory_space=pltpu.HBM)
ANYWHERE = pl.BlockSpec(memory_space=pl.ANY)

NN = (((1,), (0,)), ((), ()))
NT = (((1,), (1,)), ((), ()))
TN = (((0,), (0,)), ((), ()))


def dot(left, right, dims):
    return lax.dot_general(left, right, dims, preferred_element_type=jnp.float32)


def rope_tables(token_count):
    positions = np.arange(token_count, dtype=np.float32)[:, None]
    exponents = np.arange(HEAD // 2, dtype=np.float32) * np.float32(2.0 / HEAD)
    angles = positions * (np.float32(ROPE_BASE) ** (-exponents))[None, :]
    cosine, sine = np.cos(angles), np.sin(angles)
    return jnp.asarray(np.concatenate([cosine, cosine, -sine, sine], axis=1), jnp.float32)


def rotated(values, cosine, signed_sine):
    return values * cosine + pltpu.roll(values, HEAD // 2, 1) * signed_sine


def rotated_back(values, cosine, signed_sine):
    return values * cosine - pltpu.roll(values, HEAD // 2, 1) * signed_sine


def stacked_heads(wide):
    return jnp.concatenate(
        [wide[:, first : first + HEAD] for first in range(0, wide.shape[1], HEAD)], axis=0
    )


def side_by_side(stacked, tokens):
    return jnp.concatenate(
        [stacked[first : first + tokens] for first in range(0, stacked.shape[0], tokens)], axis=1
    )


def columns(refs, part):
    if len(refs) == 1:
        return refs[0][:, part]
    if len(refs) == 2:
        return jnp.concatenate([ref[:, part] for ref in refs], axis=0)
    pieces = [
        ref[first : first + SHARD, part] for first in (0, SHARD) for ref in refs
    ]
    return jnp.concatenate(pieces, axis=0)


def dynamic_rows(index):
    return pl.ds(pl.multiple_of(index * SHARD, SHARD), SHARD)


def attend(x_ref, gain_ref, wq_ref, wk_ref, wv_ref, tables, normed_ref=None):
    cos_ref, sin_ref, mask_ref = tables
    tokens, width = cos_ref.shape[0], wq_ref.shape[0]
    squares = jnp.zeros((tokens, HEAD), jnp.float32)
    for first in range(0, width, HEAD):
        block = columns(x_ref, slice(first, first + HEAD)).astype(jnp.float32)
        squares = squares + block * block
    inverse = lax.rsqrt(jnp.sum(squares, axis=1, keepdims=True) * (1.0 / width) + EPSILON)
    queries = jnp.zeros((tokens, wq_ref.shape[1]), jnp.float32)
    pair = jnp.zeros((tokens, 2 * HEAD), jnp.float32)
    for first in range(0, width, CHUNK):
        part = slice(first, first + CHUNK)
        normed = (
            columns(x_ref, part).astype(jnp.float32) * inverse * gain_ref[:, part]
        ).astype(jnp.bfloat16)
        if normed_ref is not None:
            normed_ref[:, part] = normed
        queries = queries + dot(normed, wq_ref[part, :], NN)
        both = jnp.concatenate([wk_ref[part, :], wv_ref[part, :]], axis=1)
        pair = pair + dot(normed, both, NN)
    cosine, sine = cos_ref[...], sin_ref[...]
    query = jnp.concatenate(
        [
            rotated(queries[:, first : first + HEAD], cosine, sine).astype(jnp.bfloat16)
            for first in range(0, queries.shape[1], HEAD)
        ],
        axis=0,
    )
    key = rotated(pair[:, :HEAD], cosine, sine).astype(jnp.bfloat16)
    value = pair[:, HEAD:].astype(jnp.bfloat16)
    scores = dot(query, key, NT) * HEAD ** (-0.5)
    causal = jnp.concatenate([mask_ref[...]] * (scores.shape[0] // tokens), axis=0) > 0.0
    terms = jnp.where(causal, jnp.exp(scores), 0.0)
    probability = terms / jnp.sum(terms, axis=1, keepdims=True)
    attended = dot(probability.astype(jnp.bfloat16), value, NN).astype(jnp.bfloat16)
    return inverse, query, key, value, probability, side_by_side(attended, tokens)


def forward_kernel(*refs):
    x_refs, (gain_ref, *projections, wo) = refs[:RING], refs[RING : RING + 5]
    tables, refs = refs[RING + 5 : RING + 8], refs[RING + 8 :]
    near_ref, far_ref = refs[-2:]
    half = near_ref.shape[0]
    attended = attend(x_refs, gain_ref, *projections, tables)[5]
    for first in range(0, wo.shape[1], CHUNK):
        part = slice(first, first + CHUNK)
        term = dot(attended, wo[:, part], NN).astype(jnp.bfloat16)
        near_ref[:, part] = term[:half]
        far_ref[:, part] = term[half:]


def recompute_kernel(first_row, *refs):
    saved_refs, (gain_ref, *projections), tables = refs[:RING], refs[RING : RING + 4], refs[8:11]
    outs = refs[-8:]
    x_ref, normed_ref, inverse_ref, query_ref, key_ref = outs[:5]
    value_ref, probability_ref, attended_ref = outs[5:]
    for flip in range(2):
        for ahead, ref in enumerate(saved_refs):
            first = (flip * RING + ahead) * SHARD
            source = flip * SHARD + (first_row if ahead else 0)
            x_ref[first : first + SHARD] = ref[source : source + SHARD, :]
    inverse, query, key, value, probability, attended = attend(
        (x_ref,), gain_ref, *projections, tables, normed_ref
    )
    inverse_ref[...] = jnp.broadcast_to(inverse, inverse_ref.shape)
    query_ref[...] = query
    key_ref[...] = key
    value_ref[...] = value
    probability_ref[...] = probability
    attended_ref[...] = attended


def backward_kernel(*refs):
    grad_refs, x_refs, refs = refs[:2], refs[2:3], refs[3:]
    inverse_ref, query_ref, key_ref, value_ref, probability_ref = refs[:5]
    (wq, wk, wv, wo), (cos_ref, sin_ref), rest = refs[5:9], refs[9:11], refs[11:]
    term_refs, rest = rest[-4 - RING : -4], rest[: -4 - RING] + rest[-4:]
    gain_out_ref, query_grad_ref, key_grad_ref, value_grad_ref = rest[-4:]
    earlier_gain_ref = rest[0] if len(rest) > 4 else None
    tokens, width = cos_ref.shape[0], wq.shape[0]
    grad_attended = jnp.zeros((tokens, wo.shape[0]), jnp.float32)
    for first in range(0, width, CHUNK):
        part = slice(first, first + CHUNK)
        grad_attended = grad_attended + dot(columns(grad_refs, part), wo[:, part], NT)
    grads = stacked_heads(grad_attended.astype(jnp.bfloat16))
    probability = probability_ref[...]
    key, value, query = key_ref[...], value_ref[...], query_ref[...]
    grad_probability = dot(grads, value, NT)
    row_terms = jnp.sum(grad_probability * probability, axis=1, keepdims=True)
    grad_scores = (
        probability * (grad_probability - row_terms) * HEAD ** (-0.5)
    ).astype(jnp.bfloat16)
    cosine, sine = cos_ref[...], sin_ref[...]
    raw = dot(grad_scores, key, NN)
    query_grad = jnp.concatenate(
        [
            rotated_back(raw[first : first + tokens], cosine, sine).astype(jnp.bfloat16)
            for first in range(0, raw.shape[0], tokens)
        ],
        axis=1,
    )
    key_grad = rotated_back(dot(grad_scores, query, TN), cosine, sine).astype(jnp.bfloat16)
    value_grad = dot(probability.astype(jnp.bfloat16), grads, TN).astype(jnp.bfloat16)
    query_grad_ref[...] = query_grad
    key_grad_ref[...] = key_grad
    value_grad_ref[...] = value_grad
    pair_grad = jnp.concatenate([key_grad, value_grad], axis=1)
    inverse = inverse_ref[:, :1]
    gains = []
    for first in range(0, width, CHUNK):
        part = slice(first, first + CHUNK)
        both = jnp.concatenate([wk[part, :], wv[part, :]], axis=1)
        term = dot(query_grad, wq[part, :], NT) + dot(pair_grad, both, NT)
        term = term.astype(jnp.bfloat16)
        for ahead, term_ref in enumerate(term_refs):
            for flip in range(2):
                start = (flip * RING + ahead) * SHARD
                rows = slice(flip * SHARD, flip * SHARD + SHARD)
                term_ref[rows, part] = term[start : start + SHARD]
        gains.append(
            jnp.sum(
                term.astype(jnp.float32) * columns(x_refs, part).astype(jnp.float32) * inverse,
                axis=0,
                keepdims=True,
            )
        )
    gain = jnp.concatenate(gains, axis=0)
    if earlier_gain_ref is None:
        gain_out_ref[...] = gain
        return
    gain = gain + earlier_gain_ref[...]
    gain_out_ref[...] = gain
    block = two_parts(gain)
    middle = block.shape[1] // 2
    block = jnp.concatenate(
        [
            block[rows, cols]
            for rows in (slice(0, 8), slice(8, 16))
            for cols in (slice(0, middle), slice(middle, 2 * middle))
        ],
        axis=0,
    ).astype(jnp.bfloat16)
    for term_ref in term_refs[1:]:
        term_ref[:, width:] = block


def two_parts(gain):
    high = wide(gain.astype(jnp.bfloat16))
    return jnp.concatenate([high, gain - high], axis=0)


def wide(value):
    return value.astype(jnp.float32)


def parts_of(width):
    return [slice(first, first + CHUNK) for first in range(0, width, CHUNK)]


def halved(near_ref, arrived_ref, own_ref, send_refs):
    for part in parts_of(own_ref.shape[1]):
        total = wide(near_ref[:, part]) + wide(arrived_ref[:, part])
        own_ref[:, part] = total[:SHARD]
        for ahead, ref in enumerate(send_refs, 1):
            ref[:SHARD, part] = total[ahead * SHARD : ahead * SHARD + SHARD].astype(jnp.bfloat16)


def halve_first_kernel(near_ref, arrived_ref, rider_ref, own_ref, *send_refs):
    halved(near_ref, arrived_ref, own_ref, send_refs)
    for ref in send_refs:
        ref[SHARD:] = rider_ref[...]


def halve_last_kernel(near_ref, arrived_ref, _, own_ref, *send_refs):
    halved(near_ref, arrived_ref, own_ref, send_refs)


def hand_on(section, edge, edge_ref, send_ref, out_ref):
    @pl.when(section == edge)
    def _():
        send_ref[...] = edge_ref[...]

    @pl.when(section != edge)
    def _():
        send_ref[...] = out_ref[...]


def finish_forward_kernel(x_ref, own_ref, one_ref, two_ref, three_ref, *rest):
    if len(rest) > 2:
        out_ref = rest[2]
    else:
        out_ref = rest[1].at[1]
        rest[1][0] = rest[0][...]
    for part in parts_of(x_ref.shape[1]):
        total = own_ref[:, part] + wide(one_ref[:SHARD, part])
        total = total + wide(two_ref[:SHARD, part]) + wide(three_ref[:SHARD, part])
        out_ref[:, part] = (wide(x_ref[:SHARD, part]) + total).astype(jnp.bfloat16)
    if len(rest) > 2:
        hand_on(rest[0][1], rest[0][2], rest[1], rest[3], out_ref)


def quartered(kept_ref, ring_refs, own_ref, send_ref):
    width = own_ref.shape[1]
    for part in parts_of(width):
        total = wide(kept_ref[:, part])
        for ref in ring_refs:
            total = total + wide(ref[:, part])
        own_ref[:, part] = total[:SHARD]
        send_ref[:, part] = total[SHARD:].astype(jnp.bfloat16)


def quarter_first_kernel(kept_ref, one_ref, two_ref, three_ref, own_ref, send_ref):
    quartered(kept_ref, (one_ref, two_ref, three_ref), own_ref, send_ref)


def quarter_last_kernel(kept_ref, one_ref, two_ref, three_ref, gain_ref, *rest):
    own_ref, send_ref, gain_out_ref = rest[-3:]
    ring_refs = (one_ref, two_ref, three_ref)
    quartered(kept_ref, ring_refs, own_ref, send_ref)
    width = own_ref.shape[1]
    gain = gain_ref[...]
    for ref in ring_refs:
        tail = wide(ref[:, width:])
        tail = tail[:SHARD] + tail[SHARD:]
        gain = gain + jnp.concatenate([tail[:8], tail[8:]], axis=1)
    gain_out_ref[...] = gain
    send_ref[:, width:] = two_parts(gain).astype(jnp.bfloat16)


def input_gradient(own_ref, arrived_ref, x_ref, grad_ref, gain_ref, out_ref):
    width = own_ref.shape[1]
    squares = jnp.zeros((SHARD, 1), jnp.float32)
    crosses = jnp.zeros((SHARD, 1), jnp.float32)
    scaled = []
    for part in parts_of(width):
        own = wide(x_ref[:SHARD, part])
        scaled.append((own_ref[:, part] + wide(arrived_ref[:, part])) * gain_ref[:, part])
        squares = squares + jnp.sum(own * own, axis=1, keepdims=True)
        crosses = crosses + jnp.sum(scaled[-1] * own, axis=1, keepdims=True)
    inverse = lax.rsqrt(squares * (1.0 / width) + EPSILON)
    factor = inverse * inverse * inverse * (crosses * (1.0 / width))
    for part, scaled_part in zip(parts_of(width), scaled):
        out_ref[:, part] = (
            wide(grad_ref[:SHARD, part])
            + inverse * scaled_part
            - wide(x_ref[:SHARD, part]) * factor
        ).astype(jnp.bfloat16)


def finish_backward_kernel(*refs):
    refs, (place_ref, edge_ref, out_ref, send_ref) = refs[:5], refs[5:]
    input_gradient(*refs, out_ref)
    hand_on(place_ref[1], 0, edge_ref, send_ref, out_ref)


def finish_last_backward_kernel(*refs):
    refs, (gain_ref, first_ref, out_ref, gain_out_ref) = refs[:5], refs[5:]
    out_ref[0] = first_ref[...]
    input_gradient(*refs, out_ref.at[1])
    width = refs[0].shape[1]
    tail = wide(refs[1][:, width:])
    gain = gain_ref[...] + tail[:8] + tail[8:]
    for index, part in enumerate(parts_of(width)):
        gain_out_ref[:, part] = gain[index : index + 1]


def join_kernel(sizes, *refs):
    outs = refs[len(refs) - len(sizes) :]
    taken = 0
    for size, out in zip(sizes, outs):
        first = 0
        for ref in refs[taken : taken + size]:
            out[first : first + ref.shape[0]] = ref[...]
            first += ref.shape[0]
        taken += size


def place_of(row, lane):
    block = lax.shift_right_logical(row, 4)
    pair = lax.shift_right_logical(lane, 2) ^ lax.shift_right_logical(block, 2)
    ring = (lane + block) & (RING - 1)
    return (pair * RING + ring) * SHARD + (row & (SHARD - 1))


def sent_rows_kernel(place_ref, stashed_ref, *refs):
    outs, sems = refs[:-1], refs[-1]
    copies = [
        pltpu.make_async_copy(
            stashed_ref.at[0, tick, dynamic_rows(block)],
            out.at[pl.ds(flip * SHARD, SHARD)],
            sems.at[tick, flip],
        )
        for tick, out in enumerate(outs)
        for flip, block in enumerate((place_ref[0], place_ref[0] ^ RING))
    ]
    for copy in copies:
        copy.start()
    for copy in copies:
        copy.wait()


def setup_kernel(place_ref, table_ref, cos_ref, sin_ref, mask_ref, place_out_ref):
    lane = place_ref[0]
    tokens = mask_ref.shape[0]
    for first in range(0, tokens, SHARD):
        block = pl.ds(pl.multiple_of(place_of(first, lane), SHARD), SHARD)
        cos_ref[first : first + SHARD] = table_ref[block, :HEAD]
        sin_ref[first : first + SHARD] = table_ref[block, HEAD:]
    later = place_of(lax.broadcasted_iota(jnp.int32, mask_ref.shape, 0), lane)
    earlier = place_of(lax.broadcasted_iota(jnp.int32, mask_ref.shape, 1), lane)
    mask_ref[...] = jnp.where(later >= earlier, 1.0, 0.0)
    for index in range(place_ref.shape[0]):
        place_out_ref[index] = place_ref[index]


def ready_kernel(*refs):
    refs[-1][...] = refs[0][...]


def stacked(refs, part=slice(None)):
    return jnp.concatenate([ref[:, part] for ref in refs], axis=0)


def this_chunk():
    return pl.ds(pl.multiple_of(pl.program_id(0) * CHUNK, CHUNK), CHUNK)


def projection_gradient_kernel(*refs):
    normed = stacked(refs[:2], this_chunk())
    gq_ref, gk_ref, gv_ref = refs[-3:]
    gq_ref[...] = dot(normed, stacked(refs[2:4]), TN).astype(jnp.bfloat16)
    pair = jnp.concatenate([stacked(refs[4:6]), stacked(refs[6:8])], axis=1)
    both = dot(normed, pair, TN).astype(jnp.bfloat16)
    gk_ref[...] = both[:, :HEAD]
    gv_ref[...] = both[:, HEAD:]


def output_gradient_kernel(*refs):
    part = this_chunk()
    refs[-1][...] = dot(stacked(refs[4:6]), stacked(refs[:4], part), TN).astype(jnp.bfloat16)


def estimate(flops, moved):
    return pl.CostEstimate(flops=int(flops), bytes_accessed=int(moved), transcendentals=0)


def call(
    kernel, out_shape, operands, flops, moved, name, room, specs=None, scratch=(), last_scalar=False
):
    out_specs = jax.tree.map(lambda _: WHOLE, out_shape)
    if last_scalar:
        out_specs = out_specs[:-1] + (SCALAR,)
    return pl.pallas_call(
        kernel,
        out_shape=out_shape,
        in_specs=[(specs or {}).get(index, WHOLE) for index in range(len(operands))],
        out_specs=out_specs,
        scratch_shapes=list(scratch),
        compiler_params=pltpu.CompilerParams(vmem_limit_bytes=room),
        cost_estimate=estimate(flops, moved),
        name=name,
    )(*operands)


def shaped(shape, dtype=jnp.bfloat16):
    return jax.ShapeDtypeStruct(shape, dtype)


def layer_call(kernel, out_shape, before, weights, after, name, specs=None):
    tokens, size = 8 * SHARD, sum(w.size for w in weights)
    operands = (*before, *weights, *after)
    return call(kernel, out_shape, operands, 4 * tokens * size, 2 * size, name, LAYER_BYTES, specs)


def forward_term(pieces, gain, weights, tables, *after):
    half = shaped((tables[0].shape[0] // 2, pieces[0].shape[1]))
    count = len(pieces) + 1 + len(weights) + len(tables)
    return layer_call(
        forward_kernel,
        (half, half),
        (*pieces, gain),
        weights,
        (*tables, *after),
        "layer_term",
        {count + index: ANYWHERE for index in range(len(after))},
    )


def recomputed(pieces, first_row, gain, weights, tables):
    tokens, width = tables[0].shape[0], pieces[0].shape[1]
    heads = weights[0].shape[1]
    stacked_rows = tokens * heads // HEAD
    return layer_call(
        functools.partial(recompute_kernel, first_row),
        (
            shaped((tokens, width)),
            shaped((tokens, width)),
            shaped((tokens, HEAD), jnp.float32),
            shaped((stacked_rows, HEAD)),
            shaped((tokens, HEAD)),
            shaped((tokens, HEAD)),
            shaped((stacked_rows, HEAD), jnp.float32),
            shaped((tokens, heads)),
        ),
        (*pieces, gain),
        weights[:3],
        tables,
        "recompute",
    )


def backward_term(grads, saved, weights, tables, *earlier_gain):
    tokens, width = tables[0].shape[0], grads[0].shape[1]
    extra = 2 * width // (tokens // RING) if earlier_gain else 0
    out = layer_call(
        backward_kernel,
        (shaped((tokens // RING, width)),)
        + (shaped((tokens // RING, width + extra)),) * (RING - 1)
        + (
            shaped((width // CHUNK, CHUNK), jnp.float32),
            shaped((tokens, weights[0].shape[1])),
            shaped((tokens, HEAD)),
            shaped((tokens, HEAD)),
        ),
        (*grads, saved[0], *saved[2:7]),
        weights,
        (*tables[:2], *earlier_gain),
        "layer_gradient_term",
    )
    return out[:RING], out[RING:]


def small(kernel, out_shape, *operands, specs=None, scratch=()):
    size = sum(x.size for x in operands)
    return call(
        kernel, out_shape, operands, size, 2 * size, kernel.__name__, SMALL_BYTES, specs, scratch
    )


def joined(groups, *after):
    operands = [x for group in groups for x in group]
    outs = tuple(
        shaped((sum(x.shape[0] for x in group), group[0].shape[1])) for group in groups
    )
    size = sum(x.size for x in operands)
    return call(
        functools.partial(join_kernel, [len(group) for group in groups]),
        outs,
        (*operands, *after),
        size,
        2 * size,
        "joined",
        SMALL_BYTES,
        specs={len(operands) + index: ANYWHERE for index in range(len(after))},
    )


def weight_gradient(kernel, operands, out_shape, out_specs, after):
    chunks = max(out_shape[0].shape) // CHUNK
    size = sum(x.size for x in out_shape)
    return pl.pallas_call(
        kernel,
        grid=(chunks,),
        out_shape=out_shape,
        in_specs=[WHOLE] * len(operands) + [ANYWHERE],
        out_specs=out_specs,
        compiler_params=pltpu.CompilerParams(vmem_limit_bytes=GRADIENT_BYTES),
        cost_estimate=estimate(4 * 8 * SHARD * size, 2 * size),
        name=kernel.__name__,
    )(*operands, after)


def projection_gradients(normed, query_grads, key_grads, value_grads, after):
    width, heads = normed[0].shape[1], query_grads[0].shape[1]
    return weight_gradient(
        projection_gradient_kernel,
        (*normed, *query_grads, *key_grads, *value_grads),
        tuple(shaped((width, columns)) for columns in (heads, HEAD, HEAD)),
        tuple(pl.BlockSpec((CHUNK, columns), lambda i: (i, 0)) for columns in (heads, HEAD, HEAD)),
        after,
    )


def output_gradient(grads, attended, after):
    heads, width = attended[0].shape[1], grads[0].shape[1]
    return weight_gradient(
        output_gradient_kernel,
        (*grads, *attended),
        (shaped((heads, width)),),
        (pl.BlockSpec((heads, CHUNK), lambda i: (0, i)),),
        after,
    )[0]


def moved(x, route):
    count, lanes = lax.axis_size("pipe"), lax.axis_size("tensor")
    pairs = []
    for section in range(count):
        for lane in range(lanes):
            to_section, to_lane = route(section, lane)
            pairs.append((section * lanes + lane, to_section % count * lanes + to_lane))
    return lax.ppermute(x, ("pipe", "tensor"), pairs)


def around(lane, by):
    return lane // RING * RING + (lane + by) % RING


def across(x):
    return moved(x, lambda section, lane: (section, lane ^ RING))


def from_ahead(x):
    return [
        moved(x, lambda section, lane, by=by: (section, around(lane, -by)))
        for by in range(1, RING)
    ]


def to_ahead(xs):
    return [
        moved(x, lambda section, lane, by=by: (section, around(lane, by)))
        for by, x in enumerate(xs, 1)
    ]


def halve_shapes(near, riders):
    width = near.shape[1]
    piece = shaped((SHARD + riders, width))
    return (shaped((SHARD, width), jnp.float32),) + (piece,) * (RING - 1)


def quarter_shapes(terms):
    width, extra = terms[0].shape[1], terms[1].shape[1] - terms[0].shape[1]
    return shaped((SHARD, width), jnp.float32), shaped((SHARD, width + 2 * extra))


def sent_rows(place, stashed):
    _, _, _, width = stashed.shape
    return call(
        sent_rows_kernel,
        (shaped((2 * SHARD, width)),) * 2,
        (place, stashed),
        0,
        8 * SHARD * width,
        "sent_rows",
        SETUP_BYTES,
        specs={0: SCALAR, 1: AWAY},
        scratch=[pltpu.SemaphoreType.DMA((2, 2))],
    )


def set_up(place, tokens):
    table = shaped((tokens, HEAD), jnp.float32)
    out = call(
        setup_kernel,
        (table, table, shaped((tokens, tokens), jnp.float32), shaped(place.shape, jnp.int32)),
        (place, rope_tables(tokens)),
        tokens * HEAD,
        4 * tokens * HEAD,
        "setup",
        SMALL_BYTES,
        specs={0: SCALAR},
        last_scalar=True,
    )
    return out[:3], out[3]


def made_ready(table, weights):
    size = sum(w.size for w in weights)
    return call(
        ready_kernel, shaped(table.shape, jnp.float32), (table, *weights), 0, 2 * size,
        "weights_ready", LAYER_BYTES,
    )


def mirrored(rows):
    return moved(rows, lambda section, lane: (-1 - section, lane))


def per_device(
    forward_in,
    entering,
    backward_in,
    loss_grad,
    stashed,
    norm_gain,
    w_query,
    key_projection,
    value_projection,
    w_out,
):
    place = jnp.stack(
        [lax.axis_index("tensor"), lax.axis_index("pipe"), lax.axis_size("pipe") - 1]
    ).astype(jnp.int32)
    sent_pairs = sent_rows(place, stashed)
    tables, place = set_up(place, stashed.shape[2])
    weights = (w_query[0], key_projection[0], value_projection[0], w_out[0])
    tables = (made_ready(tables[0], weights), *tables[1:])
    gain = norm_gain
    own_in, own_grad = forward_in[0], backward_in[0]
    row = shaped(own_in.shape)
    both = shaped((2,) + row.shape)

    first_pair, second_pair = [mirrored(pair) for pair in sent_pairs]
    (in_pair,) = joined([(own_in, across(own_in))])
    in_pieces = (in_pair, *from_ahead(in_pair))
    grad_near, entering, loss_grad = joined(
        [(own_grad, *from_ahead(own_grad)), (entering,), (loss_grad,)], tables[0]
    )
    first_grads = (grad_near, across(grad_near))
    first_rows = (first_pair, *from_ahead(first_pair))
    first_terms = forward_term(in_pieces, gain, weights, tables)
    first_states = recomputed(first_rows, 0, gain, weights, tables)
    first_back_terms, first_grad_parts = backward_term(
        first_grads, first_states, weights, tables
    )
    own, *sent = small(
        halve_first_kernel, halve_shapes(first_terms[0], 2 * SHARD), first_terms[0],
        across(first_terms[1]), second_pair,
    )
    arrived = to_ahead(sent)
    second_rows = (second_pair, *arrived[::-1])
    first_out, handed_out = small(
        finish_forward_kernel, (row, row), in_pair, own, *arrived, place, entering,
        specs={5: SCALAR},
    )
    own, sent = small(
        quarter_first_kernel, quarter_shapes(first_back_terms),
        first_back_terms[0], *to_ahead(first_back_terms[1:]),
    )
    first_back, handed_back = small(
        finish_backward_kernel, (row, row), own, across(sent), first_states[0], grad_near, gain,
        place, loss_grad, specs={5: SCALAR},
    )

    next_pair, next_near = joined(
        [
            (
                moved(handed_out, lambda section, lane: (section + 1, lane)),
                moved(handed_out, lambda section, lane: (section + 1, lane ^ RING)),
            ),
            [
                moved(handed_back, lambda section, lane, by=by: (section - 1, around(lane, -by)))
                for by in range(RING)
            ],
        ]
    )
    next_pieces = (next_pair, *from_ahead(next_pair))
    second_grads = (next_near, across(next_near))
    second_states = recomputed(second_rows, SHARD, gain, weights, tables)
    second_terms = forward_term(next_pieces, gain, weights, tables, second_grads[1])
    second_back_terms, second_grad_parts = backward_term(
        second_grads, second_states, weights, tables, first_grad_parts[0]
    )
    grad_out = output_gradient(
        (*first_grads, *second_grads), (first_states[7], second_states[7]), second_grad_parts[0]
    )
    forward_own, *sent = small(
        halve_last_kernel, halve_shapes(second_terms[0], 0), second_terms[0],
        across(second_terms[1]), grad_out, specs={2: ANYWHERE},
    )
    arrived = to_ahead(sent)
    forward_out = small(
        finish_forward_kernel, both, next_pair, forward_own, *arrived, first_out
    )
    own, sent, gain_sum = small(
        quarter_last_kernel,
        (*quarter_shapes(second_back_terms), shaped(second_grad_parts[0].shape, jnp.float32)),
        second_back_terms[0], *to_ahead(second_back_terms[1:]), second_grad_parts[0],
        arrived[0], specs={RING + 1: ANYWHERE},
    )
    grad_query, key_weight_gradient, value_weight_gradient = projection_gradients(
        (first_states[1], second_states[1]),
        *[(first_grad_parts[index], second_grad_parts[index]) for index in (1, 2, 3)],
        own,
    )
    backward_out, grad_gain = small(
        finish_last_backward_kernel,
        (both, shaped(gain.shape, jnp.float32)),
        own, across(sent), second_states[0], next_near, gain, gain_sum, first_back,
    )
    return (
        forward_out[:, None],
        backward_out[:, None],
        grad_query[None],
        key_weight_gradient[None],
        value_weight_gradient[None],
        grad_out[None],
        grad_gain,
    )


def solution(mesh):
    in_specs = (
        P("pipe", "tensor", None),
        P("tensor", None),
        P("pipe", "tensor", None),
        P("tensor", None),
        P("pipe", None, None, None),
        P("pipe", None),
        P("pipe", None, "tensor"),
        P("pipe", None, "tensor"),
        P("pipe", None, "tensor"),
        P("pipe", "tensor", None),
    )
    out_specs = (
        P(None, "pipe", "tensor", None),
        P(None, "pipe", "tensor", None),
        P("pipe", None, "tensor"),
        P("pipe", None, "tensor"),
        P("pipe", None, "tensor"),
        P("pipe", "tensor", None),
        P("pipe", None),
    )
    return jax.shard_map(
        per_device, mesh=mesh, in_specs=in_specs, out_specs=out_specs, check_vma=False
    )
```

time: 169 us -> 159 us (0.941)
  starting transfers between devices: 85 us -> 62.7 us
  waiting for transfers between devices: 32 us -> 47.4 us
  Pallas kernels: 26.4 us -> 35.4 us
  local copies, waits for them, and re-layouts: 18.3 us -> 11.5 us
  other arithmetic: 5.3 us -> 0.59 us
    ppermute x50 -> x39, starting transfers between devices: 85 us -> 62.7 us  [moved(): return lax.ppermute(x, ('pipe', 'tensor'), pairs)]
    ppermute x50 -> x39, waiting for transfers between devices: 32 us -> 47.4 us  [moved(): return lax.ppermute(x, ('pipe', 'tensor'), pairs)]
    pallas_call x15 -> x22, Pallas kernels: 26.4 us -> 35.4 us  [the longest x20 25.1 us: call(): pl.pallas_call(kernel, out_shape=out_shape, in_specs=[(specs or {}).get(i...]
    slice x1 -> x0, local copies, waits for them, and re-layouts: 3.07 us -> none  [per_device(): pieces = [saved_pieces(stashed[0, tick], lane) for tick in range(2)]]
    concatenate x5 -> x0, other arithmetic: 2.5 us -> none  [the longest x2 1.44 us: saved_pieces(): jnp.concatenate(blocks)]
    select_n x2 -> x0, other arithmetic: 2.32 us -> none  [the longest x1 1.16 us: per_device(): next_pair = jnp.where(section_index == 0, enter_pair, next_in)]
    dynamic_slice x1 -> x0, local copies, waits for them, and re-layouts: 1.82 us -> none  [saved_pieces(): lax.dynamic_slice_in_dim(rows, block * SHARD, SHARD, 0)]
    unnamed x65 -> x30, local copies, waits for them, and re-layouts: 13.2 us -> 11.5 us
  transfers between devices with their start and end apart: 50 -> 39, of which waited for: 15 -> 20; matrix products, arithmetic and copies ran while one was open for 7% -> 0% of each run, Pallas kernels for 15% -> 20%
where the time goes in v3:
time: 159 us; the launch traced here: 158 us
  starting transfers between devices  62.7 us (39%)
  waiting for transfers between devices  47.4 us (30%)
  Pallas kernels  35.4 us (22%)
  local copies, waits for them, and re-layouts  11.5 us (7%)
    ppermute x39, starting transfers between devices, moved(): return lax.ppermute(x, ('pipe', 'tensor'), pairs)  62.7 us
    ppermute x39, waiting for transfers between devices, moved(): return lax.ppermute(x, ('pipe', 'tensor'), pairs)  47.4 us
    pallas_call x20, Pallas kernels, call(): pl.pallas_call(kernel, out_shape=out_shape, in_specs=[(specs or {}).get(i...  25.1 us
    unnamed x30, local copies, waits for them, and re-layouts  11.5 us
    pallas_call x2, Pallas kernels, weight_gradient(): pl.pallas_call(kernel, grid=(chunks,), out_shape=out_shape, in_specs=[WHO...  10.4 us
  transfers between devices with their start and end apart: 39, of which 20 were waited for; matrix products, arithmetic and copies ran while one was open for 0% of the time, Pallas kernels for 20%

profile of v3, /device:TPU:0, one launch (start us, length us, event | category | flops | bytes accessed | tf_op | source)
XLA Modules:
  0.0 158.5 jit_solution(10546641172503416524)
XLA Ops:
  0.6 3.4 %collective-permute-start = (bf16[16,4096]{1,0:T(8,128)(2,1)}, bf16[16,4096]{1,0:T(8,128)(2,1)S(1)}, u32[]{:S(2)}, u32[]{:S(2)}) collective-permute-start(bf16[16,4096]{1,0:T(8,128)(2,1)} %bitcast.45), channel_id=1, source_target_pairs={{0,4},{1,5},{2,6},{3,7},{4,0},{5,1},{6,2},{7,3},{8,12},{9,13},{10,... | collective-permute-start | bytes 393224 | tf_op jit(solution)/shard_map/ppermute | solution.py:579
  5.9 3.6 %collective-permute-start.10 = (bf16[16,4096]{1,0:T(8,128)(2,1)}, bf16[16,4096]{1,0:T(8,128)(2,1)S(1)}, u32[]{:S(2)}, u32[]{:S(2)}) collective-permute-start(bf16[16,4096]{1,0:T(8,128)(2,1)} %bitcast.48), channel_id=1, source_target_pairs={{0,2},{1,3},{2,0},{3,1},{4,6},{5,7},{6,4},{7,5},{8,10},{9,11},{10,... | collective-permute-start | bytes 393224 | tf_op jit(solution)/shard_map/ppermute | solution.py:579
  10.1 2.6 %sent_rows.1 = (bf16[32,4096]{1,0:T(8,128)(2,1)}, bf16[32,4096]{1,0:T(8,128)(2,1)}) custom-call(s32[3]{0:T(128)} %pad_add_fusion.place_ref, bf16[1,2,128,4096]{3,2,1,0:T(8,128)(2,1)} %stashed_ref.1), custom_call_target="tpu_custom_call" | custom-call | bytes 524288 | tf_op jit(solution)/shard_map/sent_rows/pallas_call | solution.py:430
  15.2 2.5 %collective-permute-start.2 = (bf16[32,4096]{1,0:T(8,128)(2,1)S(1)}, bf16[32,4096]{1,0:T(8,128)(2,1)S(1)}, u32[]{:S(2)}, u32[]{:S(2)}) collective-permute-start(bf16[32,4096]{1,0:T(8,128)(2,1)S(1)} %joined.3.refs_0_.x_ref), channel_id=1, source_target_pairs={{0,2},{1,3},{2,0},{3,1},{4,6},{5,7},{6,4},{7,5},{8,10},{9,11},{10,... | collective-permute-start | bytes 786440 | tf_op jit(solution)/shard_map/ppermute | solution.py:579
  22.1 2.2 %copy-done = bf16[1,4096,512]{2,1,0:T(8,128)(2,1)S(1)} copy-done((bf16[1,4096,512]{2,1,0:T(8,128)(2,1)S(1)}, bf16[1,4096,512]{2,1,0:T(8,128)(2,1)}, u32[]{:S(2)}) %copy-start) | copy-done | bytes 4194328
  24.3 2.2 %copy-done.2 = bf16[1,512,4096]{2,1,0:T(8,128)(2,1)S(1)} copy-done((bf16[1,512,4096]{2,1,0:T(8,128)(2,1)S(1)}, bf16[1,512,4096]{2,1,0:T(8,128)(2,1)}, u32[]{:S(2)}) %copy-start.2) | copy-done | bytes 4194328
  29.0 5.6 %collective-permute-done.9.refs_1_ = bf16[16,4096]{1,0:T(8,128)(2,1)S(1)} collective-permute-done((bf16[16,4096]{1,0:T(8,128)(2,1)}, bf16[16,4096]{1,0:T(8,128)(2,1)S(1)}, u32[]{:S(2)}, u32[]{:S(2)}) %collective-permute-start.9) | collective-permute-done | bytes 131104 | tf_op jit(solution)/shard_map/ppermute | solution.py:579
  36.9 3.6 %collective-permute-start.17 = (bf16[32,4096]{1,0:T(8,128)(2,1)S(1)}, bf16[32,4096]{1,0:T(8,128)(2,1)S(1)}, u32[]{:S(2)}, u32[]{:S(2)}) collective-permute-start(bf16[32,4096]{1,0:T(8,128)(2,1)S(1)} %collective-permute-done.15.refs_0_), channel_id=1, source_target_pairs={{0,2},{1,3},{2,0},{3,1},{4,6},{5,7},{6,4},{7,5},{8,10},{9,11},{10,... | collective-permute-start | bytes 786440 | tf_op jit(solution)/shard_map/ppermute | solution.py:579
  40.6 2.8 %layer_term.2 = (bf16[64,4096]{1,0:T(8,128)(2,1)S(1)}, bf16[64,4096]{1,0:T(8,128)(2,1)S(1)}) custom-call(bf16[32,4096]{1,0:T(8,128)(2,1)S(1)} %joined.3.refs_0_.x_ref, bf16[32,4096]{1,0:T(8,128)(2,1)S(1)} %collective-permute-done.1.refs_1_, bf16[32,4096]{1,0:T(8,128)(2,1)S(1)} %collective-permute-done.2.refs_2_, ...), custom_call_target="tpu_custom_call" | custom-call | flops 2684354560 | bytes 10485760 | tf_op jit(solution)/shard_map/layer_term/pallas_call | solution.py:430
  43.4 3.1 %collective-permute-done.18.refs_3_ = bf16[32,4096]{1,0:T(8,128)(2,1)S(1)} collective-permute-done((bf16[32,4096]{1,0:T(8,128)(2,1)S(1)}, bf16[32,4096]{1,0:T(8,128)(2,1)S(1)}, u32[]{:S(2)}, u32[]{:S(2)}) %collective-permute-start.18) | collective-permute-done | bytes 262176 | tf_op jit(solution)/shard_map/ppermute | solution.py:579
  48.2 3.9 %collective-permute-done.17.refs_2_ = bf16[32,4096]{1,0:T(8,128)(2,1)S(1)} collective-permute-done((bf16[32,4096]{1,0:T(8,128)(2,1)S(1)}, bf16[32,4096]{1,0:T(8,128)(2,1)S(1)}, u32[]{:S(2)}, u32[]{:S(2)}) %collective-permute-start.17) | collective-permute-done | bytes 262176 | tf_op jit(solution)/shard_map/ppermute | solution.py:579
  54.0 2.7 %collective-permute-done.14.refs_1_ = bf16[64,4096]{1,0:T(8,128)(2,1)S(1)} collective-permute-done((bf16[64,4096]{1,0:T(8,128)(2,1)S(1)}, bf16[64,4096]{1,0:T(8,128)(2,1)S(1)}, u32[]{:S(2)}, u32[]{:S(2)}) %collective-permute-start.14) | collective-permute-done | bytes 524320 | tf_op jit(solution)/shard_map/ppermute | solution.py:579
  56.7 4.2 %layer_gradient_term.2 = (bf16[32,4096]{1,0:T(8,128)(2,1)S(1)}, bf16[32,4096]{1,0:T(8,128)(2,1)S(1)}, bf16[32,4096]{1,0:T(8,128)(2,1)S(1)}, bf16[32,4096]{1,0:T(...) custom-call(bf16[64,4096]{1,0:T(8,128)(2,1)S(1)} %get-tuple-element., ...), custom_call_target="tpu_custom_call" | custom-call | flops 2684354560 | bytes 10485760 | tf_op jit(solution)/shard_map/layer_gradient_term/pallas_call | solution.py:430
  61.3 3.6 %collective-permute-start.20 = (bf16[32,4096]{1,0:T(8,128)(2,1)S(1)}, bf16[32,4096]{1,0:T(8,128)(2,1)S(1)}, u32[]{:S(2)}, u32[]{:S(2)}) collective-permute-start(bf16[32,4096]{1,0:T(8,128)(2,1)S(1)} %get-tuple-element.99), channel_id=1, source_target_pairs={{0,2},{1,3},{2,0},{3,1},{4,6},{5,7},{6,4},{7,5},{8,10},{9,11},{10,... | collective-permute-start | bytes 786440 | tf_op jit(solution)/shard_map/ppermute | solution.py:579
  64.8 2.3 %collective-permute-done.4.arrived_ref = bf16[64,4096]{1,0:T(8,128)(2,1)S(1)} collective-permute-done((bf16[64,4096]{1,0:T(8,128)(2,1)S(1)}, bf16[64,4096]{1,0:T(8,128)(2,1)S(1)}, u32[]{:S(2)}, u32[]{:S(2)}) %collective-permute-start.4) | collective-permute-done | bytes 524320 | tf_op jit(solution)/shard_map/ppermute | solution.py:579
  67.6 3.6 %collective-permute-start.7 = (bf16[48,4096]{1,0:T(8,128)(2,1)S(1)}, bf16[48,4096]{1,0:T(8,128)(2,1)S(1)}, u32[]{:S(2)}, u32[]{:S(2)}) collective-permute-start(bf16[48,4096]{1,0:T(8,128)(2,1)S(1)} %get-tuple-element.84), channel_id=1, source_target_pairs={{0,2},{1,3},{2,0},{3,1},{4,6},{5,7},{6,4},{7,5},{8,10},{9,11},{10,... | collective-permute-start | bytes 1179656 | tf_op jit(solution)/shard_map/ppermute | solution.py:579
  72.6 5.1 %collective-permute-done.20.two_ref = bf16[32,4096]{1,0:T(8,128)(2,1)S(1)} collective-permute-done((bf16[32,4096]{1,0:T(8,128)(2,1)S(1)}, bf16[32,4096]{1,0:T(8,128)(2,1)S(1)}, u32[]{:S(2)}, u32[]{:S(2)}) %collective-permute-start.20) | collective-permute-done | bytes 262176 | tf_op jit(solution)/shard_map/ppermute | solution.py:579
  80.0 4.6 %collective-permute-done.22.refs_1_ = bf16[16,4096]{1,0:T(8,128)(2,1)S(1)} collective-permute-done((bf16[16,4096]{1,0:T(8,128)(2,1)S(1)}, bf16[16,4096]{1,0:T(8,128)(2,1)S(1)}, u32[]{:S(2)}, u32[]{:S(2)}) %collective-permute-start.22) | collective-permute-done | bytes 131104 | tf_op jit(solution)/shard_map/ppermute | solution.py:579
  85.5 7.9 %collective-permute-start.25 = (bf16[16,4096]{1,0:T(8,128)(2,1)S(1)}, bf16[16,4096]{1,0:T(8,128)(2,1)S(1)}, u32[]{:S(2)}, u32[]{:S(2)}) collective-permute-start(bf16[16,4096]{1,0:T(8,128)(2,1)S(1)} %get-tuple-element.104), channel_id=1, source_target_pairs={{0,122},{1,123},{2,120},{3,121},{4,126},{5,127},{6,124},{7,125},{8... | collective-permute-start | bytes 393224 | tf_op jit(solution)/shard_map/ppermute | solution.py:579
  95.0 2.0 %collective-permute-start.13 = (bf16[16,4096]{1,0:T(8,128)(2,1)S(1)}, bf16[16,4096]{1,0:T(8,128)(2,1)S(1)}, u32[]{:S(2)}, u32[]{:S(2)}) collective-permute-start(bf16[16,4096]{1,0:T(8,128)(2,1)S(1)} %get-tuple-element.88), channel_id=1, source_target_pairs={{0,12},{1,13},{2,14},{3,15},{4,8},{5,9},{6,10},{7,11},{8,20},{9,21... | collective-permute-start | bytes 393224 | tf_op jit(solution)/shard_map/ppermute | solution.py:579
  99.8 3.3 %collective-permute-done.13.refs_1_ = bf16[16,4096]{1,0:T(8,128)(2,1)S(1)} collective-permute-done((bf16[16,4096]{1,0:T(8,128)(2,1)S(1)}, bf16[16,4096]{1,0:T(8,128)(2,1)S(1)}, u32[]{:S(2)}, u32[]{:S(2)}) %collective-permute-start.13) | collective-permute-done | bytes 131104 | tf_op jit(solution)/shard_map/ppermute | solution.py:579
  103.6 2.2 %collective-permute-start.30 = (bf16[64,4096]{1,0:T(8,128)(2,1)S(1)}, bf16[64,4096]{1,0:T(8,128)(2,1)S(1)}, u32[]{:S(2)}, u32[]{:S(2)}) collective-permute-start(bf16[64,4096]{1,0:T(8,128)(2,1)S(1)} %get-tuple-element.106.refs_0_.refs_2_.refs_3_), channel_id=1, source_target_pairs={{0,4},{1,5},{2,6},{3,7},{4,0},{5,1},{6,2},{7,3},{8,12},{9,13},{10,... | collective-permute-start | bytes 1572872 | tf_op jit(solution)/shard_map/ppermute | solution.py:579
  111.8 7.8 %collective-permute-done.29.refs_3_ = bf16[32,4096]{1,0:T(8,128)(2,1)S(1)} collective-permute-done((bf16[32,4096]{1,0:T(8,128)(2,1)S(1)}, bf16[32,4096]{1,0:T(8,128)(2,1)S(1)}, u32[]{:S(2)}, u32[]{:S(2)}) %collective-permute-start.29) | collective-permute-done | bytes 262176 | tf_op jit(solution)/shard_map/ppermute | solution.py:579
  120.2 2.8 %layer_term.3 = (bf16[64,4096]{1,0:T(8,128)(2,1)S(1)}, bf16[64,4096]{1,0:T(8,128)(2,1)S(1)}) custom-call(bf16[32,4096]{1,0:T(8,128)(2,1)S(1)} %get-tuple-element.105.refs_0_.x_ref, bf16[32,4096]{1,0:T(8,128)(2,1)S(1)} %collective-permute-done.27.refs_1_, bf16[32,4096]{1,0:T(8,128)(2,1)S(1)} %collective-permute-done.28.refs_2_, ...), custom_call_target="tpu_custom_call" | custom-call | flops 2684354560 | bytes 10485760 | tf_op jit(solution)/shard_map/layer_term/pallas_call | solution.py:430
  123.9 4.2 %layer_gradient_term.3 = (bf16[32,4096]{1,0:T(8,128)(2,1)S(1)}, bf16[32,4352]{1,0:T(8,128)(2,1)S(1)}, bf16[32,4352]{1,0:T(8,128)(2,1)S(1)}, bf16[32,4352]{1,0:T(...) custom-call(bf16[64,4096]{1,0:T(8,128)(2,1)S(1)} %get-tuple-element., ...), custom_call_target="tpu_custom_call" | custom-call | flops 2684354560 | bytes 10485760 | tf_op jit(solution)/shard_map/layer_gradient_term/pallas_call | solution.py:430
  128.5 3.6 %collective-permute-start.36 = (bf16[32,4352]{1,0:T(8,128)(2,1)S(1)}, bf16[32,4352]{1,0:T(8,128)(2,1)S(1)}, u32[]{:S(2)}, u32[]{:S(2)}) collective-permute-start(bf16[32,4352]{1,0:T(8,128)(2,1)S(1)} %get-tuple-element.126), channel_id=1, source_target_pairs={{0,2},{1,3},{2,0},{3,1},{4,6},{5,7},{6,4},{7,5},{8,10},{9,11},{10,... | collective-permute-start | bytes 835592 | tf_op jit(solution)/shard_map/ppermute | solution.py:579
  132.1 4.8 %output_gradient_kernel.1._ = bf16[512,4096]{1,0:T(8,128)(2,1)} custom-call(bf16[64,4096]{1,0:T(8,128)(2,1)S(1)} %get-tuple-element.89.refs_0_.refs_3_, bf16[64,4096]{1,0:T(8,128)(2,1)S(1)} %collective-permute-done.14.refs_1_, bf16[64,4096]{1,0:T(8,128)(2,1)S(1)} %get-tuple-element.106.refs_0_.refs_2_.refs_3_, ...), custom_call_target="tpu_custom_call" | custom-call | flops 1073741824 | bytes 4194304 | tf_op jit(solution)/shard_map/output_gradient_kernel/pallas_call | solution.py:538
  137.4 2.2 %copy-done.6 = bf16[512,4096]{1,0:T(8,128)(2,1)S(1)} copy-done((bf16[512,4096]{1,0:T(8,128)(2,1)S(1)}, bf16[512,4096]{1,0:T(8,128)(2,1)}, u32[]{:S(2)}) %copy-start.6) | copy-done | bytes 4194328
  141.3 3.1 %collective-permute-start.33 = (bf16[16,4096]{1,0:T(8,128)(2,1)S(1)}, bf16[16,4096]{1,0:T(8,128)(2,1)S(1)}, u32[]{:S(2)}, u32[]{:S(2)}) collective-permute-start(bf16[16,4096]{1,0:T(8,128)(2,1)S(1)} %get-tuple-element.121), channel_id=1, source_target_pairs={{0,2},{1,3},{2,0},{3,1},{4,6},{5,7},{6,4},{7,5},{8,10},{9,11},{10,... | collective-permute-start | bytes 393224 | tf_op jit(solution)/shard_map/ppermute | solution.py:579
  144.4 3.5 %collective-permute-done.32.one_ref.rest_0_ = bf16[16,4096]{1,0:T(8,128)(2,1)S(1)} collective-permute-done((bf16[16,4096]{1,0:T(8,128)(2,1)S(1)}, bf16[16,4096]{1,0:T(8,128)(2,1)S(1)}, u32[]{:S(2)}, u32[]{:S(2)}) %collective-permute-start.32) | collective-permute-done | bytes 131104 | tf_op jit(solution)/shard_map/ppermute | solution.py:579
  148.1 3.1 %collective-permute-start.38 = (bf16[16,4608]{1,0:T(8,128)(2,1)S(1)}, bf16[16,4608]{1,0:T(8,128)(2,1)S(1)}, u32[]{:S(2)}, u32[]{:S(2)}) collective-permute-start(bf16[16,4608]{1,0:T(8,128)(2,1)S(1)} %get-tuple-element.129), channel_id=1, source_target_pairs={{0,4},{1,5},{2,6},{3,7},{4,0},{5,1},{6,2},{7,3},{8,12},{9,13},{10,... | collective-permute-start | bytes 442376 | tf_op jit(solution)/shard_map/ppermute | solution.py:579
  152.0 5.6 %projection_gradient_kernel.1 = (bf16[4096,512]{1,0:T(8,128)(2,1)}, bf16[4096,128]{1,0:T(8,128)(2,1)}, bf16[4096,128]{1,0:T(8,128)(2,1)}) custom-call(bf16[128,4096]{1,0:T(8,128)(2,1)S(1)} %get-tuple-element.133.refs_0_, bf16[128,4096]{1,0:T(8,128)(2,1)S(1)} %get-tuple-element.134.refs_1_, bf16[128,512]{1,0:T(8,128)(2,1)S(1)} %get-tuple-element.135.refs_2_, ...), custom_call_target="tpu_custom_call" | custom-call | flops 1610612736 | bytes 6291456 | tf_op jit(solution)/shard_map/projection_gradient_kernel/pallas_call | solution.py:538
  (99 shorter events, 40.0 us)
Async XLA Ops:
  0.6 13.6 %collective-permute-start = (bf16[16,4096]{1,0:T(8,128)(2,1)}, bf16[16,4096]{1,0:T(8,128)(2,1)S(1)}, u32[]{:S(2)}, u32[]{:S(2)}) collective-permute-start(bf16[16,4096]{1,0:T(8,128)(2,1)} %bitcast.45), channel_id=1, source_target_pairs={{0,4},{1,5},{2,6},{3,7},{4,0},{5,1},{6,2},{7,3},{8,12},{9,13},{10,... | collective-permute-start | bytes 393224 | tf_op jit(solution)/shard_map/ppermute | solution.py:579
  4.0 13.7 %collective-permute-start.11 = (bf16[16,4096]{1,0:T(8,128)(2,1)}, bf16[16,4096]{1,0:T(8,128)(2,1)S(1)}, u32[]{:S(2)}, u32[]{:S(2)}) collective-permute-start(bf16[16,4096]{1,0:T(8,128)(2,1)} %bitcast.47), channel_id=1, source_target_pairs={{0,1},{1,2},{2,3},{3,0},{4,5},{5,6},{6,7},{7,4},{8,9},{9,10},{10,1... | collective-permute-start | bytes 393224 | tf_op jit(solution)/shard_map/ppermute | solution.py:579
  5.9 12.6 %collective-permute-start.10 = (bf16[16,4096]{1,0:T(8,128)(2,1)}, bf16[16,4096]{1,0:T(8,128)(2,1)S(1)}, u32[]{:S(2)}, u32[]{:S(2)}) collective-permute-start(bf16[16,4096]{1,0:T(8,128)(2,1)} %bitcast.48), channel_id=1, source_target_pairs={{0,2},{1,3},{2,0},{3,1},{4,6},{5,7},{6,4},{7,5},{8,10},{9,11},{10,... | collective-permute-start | bytes 393224 | tf_op jit(solution)/shard_map/ppermute | solution.py:579
  12.7 24.0 %collective-permute-start.15 = (bf16[32,4096]{1,0:T(8,128)(2,1)}, bf16[32,4096]{1,0:T(8,128)(2,1)S(1)}, u32[]{:S(2)}, u32[]{:S(2)}) collective-permute-start(bf16[32,4096]{1,0:T(8,128)(2,1)} %get-tuple-element.90), channel_id=1, source_target_pairs={{0,120},{1,121},{2,122},{3,123},{4,124},{5,125},{6,126},{7,127},{8... | collective-permute-start | bytes 786440 | tf_op jit(solution)/shard_map/ppermute | solution.py:579
  15.1 21.7 %collective-permute-start.3 = (bf16[32,4096]{1,0:T(8,128)(2,1)S(1)}, bf16[32,4096]{1,0:T(8,128)(2,1)S(1)}, u32[]{:S(2)}, u32[]{:S(2)}) collective-permute-start(bf16[32,4096]{1,0:T(8,128)(2,1)S(1)} %joined.3.refs_0_.x_ref), channel_id=1, source_target_pairs={{0,1},{1,2},{2,3},{3,0},{4,5},{5,6},{6,7},{7,4},{8,9},{9,10},{10,1... | collective-permute-start | bytes 786440 | tf_op jit(solution)/shard_map/ppermute | solution.py:579
  15.2 25.2 %collective-permute-start.2 = (bf16[32,4096]{1,0:T(8,128)(2,1)S(1)}, bf16[32,4096]{1,0:T(8,128)(2,1)S(1)}, u32[]{:S(2)}, u32[]{:S(2)}) collective-permute-start(bf16[32,4096]{1,0:T(8,128)(2,1)S(1)} %joined.3.refs_0_.x_ref), channel_id=1, source_target_pairs={{0,2},{1,3},{2,0},{3,1},{4,6},{5,7},{6,4},{7,5},{8,10},{9,11},{10,... | collective-permute-start | bytes 786440 | tf_op jit(solution)/shard_map/ppermute | solution.py:579
  17.7 22.8 %collective-permute-start.1 = (bf16[32,4096]{1,0:T(8,128)(2,1)S(1)}, bf16[32,4096]{1,0:T(8,128)(2,1)S(1)}, u32[]{:S(2)}, u32[]{:S(2)}) collective-permute-start(bf16[32,4096]{1,0:T(8,128)(2,1)S(1)} %joined.3.refs_0_.x_ref), channel_id=1, source_target_pairs={{0,3},{1,0},{2,1},{3,2},{4,7},{5,4},{6,5},{7,6},{8,11},{9,8},{10,9... | collective-permute-start | bytes 786440 | tf_op jit(solution)/shard_map/ppermute | solution.py:579
  18.5 16.2 %collective-permute-start.9 = (bf16[16,4096]{1,0:T(8,128)(2,1)}, bf16[16,4096]{1,0:T(8,128)(2,1)S(1)}, u32[]{:S(2)}, u32[]{:S(2)}) collective-permute-start(bf16[16,4096]{1,0:T(8,128)(2,1)} %bitcast.49), channel_id=1, source_target_pairs={{0,3},{1,0},{2,1},{3,2},{4,7},{5,4},{6,5},{7,6},{8,11},{9,8},{10,9... | collective-permute-start | bytes 393224 | tf_op jit(solution)/shard_map/ppermute | solution.py:579
  34.7 22.0 %collective-permute-start.14 = (bf16[64,4096]{1,0:T(8,128)(2,1)S(1)}, bf16[64,4096]{1,0:T(8,128)(2,1)S(1)}, u32[]{:S(2)}, u32[]{:S(2)}) collective-permute-start(bf16[64,4096]{1,0:T(8,128)(2,1)S(1)} %get-tuple-element.89.refs_0_.refs_3_), channel_id=1, source_target_pairs={{0,4},{1,5},{2,6},{3,7},{4,0},{5,1},{6,2},{7,3},{8,12},{9,13},{10,... | collective-permute-start | bytes 1572872 | tf_op jit(solution)/shard_map/ppermute | solution.py:579
  36.7 9.8 %collective-permute-start.18 = (bf16[32,4096]{1,0:T(8,128)(2,1)S(1)}, bf16[32,4096]{1,0:T(8,128)(2,1)S(1)}, u32[]{:S(2)}, u32[]{:S(2)}) collective-permute-start(bf16[32,4096]{1,0:T(8,128)(2,1)S(1)} %collective-permute-done.15.refs_0_), channel_id=1, source_target_pairs={{0,1},{1,2},{2,3},{3,0},{4,5},{5,6},{6,7},{7,4},{8,9},{9,10},{10,1... | collective-permute-start | bytes 786440 | tf_op jit(solution)/shard_map/ppermute | solution.py:579
  36.9 15.2 %collective-permute-start.17 = (bf16[32,4096]{1,0:T(8,128)(2,1)S(1)}, bf16[32,4096]{1,0:T(8,128)(2,1)S(1)}, u32[]{:S(2)}, u32[]{:S(2)}) collective-permute-start(bf16[32,4096]{1,0:T(8,128)(2,1)S(1)} %collective-permute-done.15.refs_0_), channel_id=1, source_target_pairs={{0,2},{1,3},{2,0},{3,1},{4,6},{5,7},{6,4},{7,5},{8,10},{9,11},{10,... | collective-permute-start | bytes 786440 | tf_op jit(solution)/shard_map/ppermute | solution.py:579
  40.5 11.7 %collective-permute-start.16 = (bf16[32,4096]{1,0:T(8,128)(2,1)S(1)}, bf16[32,4096]{1,0:T(8,128)(2,1)S(1)}, u32[]{:S(2)}, u32[]{:S(2)}) collective-permute-start(bf16[32,4096]{1,0:T(8,128)(2,1)S(1)} %collective-permute-done.15.refs_0_), channel_id=1, source_target_pairs={{0,3},{1,0},{2,1},{3,2},{4,7},{5,4},{6,5},{7,6},{8,11},{9,8},{10,9... | collective-permute-start | bytes 786440 | tf_op jit(solution)/shard_map/ppermute | solution.py:579
  40.5 24.3 %collective-permute-start.5 = (bf16[32,4096]{1,0:T(8,128)(2,1)S(1)}, bf16[32,4096]{1,0:T(8,128)(2,1)S(1)}, u32[]{:S(2)}, u32[]{:S(2)}) collective-permute-start(bf16[32,4096]{1,0:T(8,128)(2,1)S(1)} %copy-done.14), channel_id=1, source_target_pairs={{0,120},{1,121},{2,122},{3,123},{4,124},{5,125},{6,126},{7,127},{8... | collective-permute-start | bytes 786440 | tf_op jit(solution)/shard_map/ppermute | solution.py:579
  46.5 20.6 %collective-permute-start.4 = (bf16[64,4096]{1,0:T(8,128)(2,1)S(1)}, bf16[64,4096]{1,0:T(8,128)(2,1)S(1)}, u32[]{:S(2)}, u32[]{:S(2)}) collective-permute-start(bf16[64,4096]{1,0:T(8,128)(2,1)S(1)} %get-tuple-element.80), channel_id=1, source_target_pairs={{0,4},{1,5},{2,6},{3,7},{4,0},{5,1},{6,2},{7,3},{8,12},{9,13},{10,... | collective-permute-start | bytes 1572872 | tf_op jit(solution)/shard_map/ppermute | solution.py:579
  61.0 10.3 %collective-permute-start.19 = (bf16[32,4096]{1,0:T(8,128)(2,1)S(1)}, bf16[32,4096]{1,0:T(8,128)(2,1)S(1)}, u32[]{:S(2)}, u32[]{:S(2)}) collective-permute-start(bf16[32,4096]{1,0:T(8,128)(2,1)S(1)} %get-tuple-element.98), channel_id=1, source_target_pairs={{0,1},{1,2},{2,3},{3,0},{4,5},{5,6},{6,7},{7,4},{8,9},{9,10},{10,1... | collective-permute-start | bytes 786440 | tf_op jit(solution)/shard_map/ppermute | solution.py:579
  61.3 16.4 %collective-permute-start.20 = (bf16[32,4096]{1,0:T(8,128)(2,1)S(1)}, bf16[32,4096]{1,0:T(8,128)(2,1)S(1)}, u32[]{:S(2)}, u32[]{:S(2)}) collective-permute-start(bf16[32,4096]{1,0:T(8,128)(2,1)S(1)} %get-tuple-element.99), channel_id=1, source_target_pairs={{0,2},{1,3},{2,0},{3,1},{4,6},{5,7},{6,4},{7,5},{8,10},{9,11},{10,... | collective-permute-start | bytes 786440 | tf_op jit(solution)/shard_map/ppermute | solution.py:579
  64.8 13.1 %collective-permute-start.21 = (bf16[32,4096]{1,0:T(8,128)(2,1)S(1)}, bf16[32,4096]{1,0:T(8,128)(2,1)S(1)}, u32[]{:S(2)}, u32[]{:S(2)}) collective-permute-start(bf16[32,4096]{1,0:T(8,128)(2,1)S(1)} %get-tuple-element.100), channel_id=1, source_target_pairs={{0,3},{1,0},{2,1},{3,2},{4,7},{5,4},{6,5},{7,6},{8,11},{9,8},{10,9... | collective-permute-start | bytes 786440 | tf_op jit(solution)/shard_map/ppermute | solution.py:579
  67.3 26.1 %collective-permute-start.6 = (bf16[48,4096]{1,0:T(8,128)(2,1)S(1)}, bf16[48,4096]{1,0:T(8,128)(2,1)S(1)}, u32[]{:S(2)}, u32[]{:S(2)}) collective-permute-start(bf16[48,4096]{1,0:T(8,128)(2,1)S(1)} %get-tuple-element.83), channel_id=1, source_target_pairs={{0,1},{1,2},{2,3},{3,0},{4,5},{5,6},{6,7},{7,4},{8,9},{9,10},{10,1... | collective-permute-start | bytes 1179656 | tf_op jit(solution)/shard_map/ppermute | solution.py:579
  67.6 26.8 %collective-permute-start.7 = (bf16[48,4096]{1,0:T(8,128)(2,1)S(1)}, bf16[48,4096]{1,0:T(8,128)(2,1)S(1)}, u32[]{:S(2)}, u32[]{:S(2)}) collective-permute-start(bf16[48,4096]{1,0:T(8,128)(2,1)S(1)} %get-tuple-element.84), channel_id=1, source_target_pairs={{0,2},{1,3},{2,0},{3,1},{4,6},{5,7},{6,4},{7,5},{8,10},{9,11},{10,... | collective-permute-start | bytes 1179656 | tf_op jit(solution)/shard_map/ppermute | solution.py:579
  71.3 23.1 %collective-permute-start.8 = (bf16[48,4096]{1,0:T(8,128)(2,1)S(1)}, bf16[48,4096]{1,0:T(8,128)(2,1)S(1)}, u32[]{:S(2)}, u32[]{:S(2)}) collective-permute-start(bf16[48,4096]{1,0:T(8,128)(2,1)S(1)} %get-tuple-element.85), channel_id=1, source_target_pairs={{0,3},{1,0},{2,1},{3,2},{4,7},{5,4},{6,5},{7,6},{8,11},{9,8},{10,9... | collective-permute-start | bytes 1179656 | tf_op jit(solution)/shard_map/ppermute | solution.py:579
  85.4 11.6 %collective-permute-start.26 = (bf16[16,4096]{1,0:T(8,128)(2,1)S(1)}, bf16[16,4096]{1,0:T(8,128)(2,1)S(1)}, u32[]{:S(2)}, u32[]{:S(2)}) collective-permute-start(bf16[16,4096]{1,0:T(8,128)(2,1)S(1)} %get-tuple-element.104), channel_id=1, source_target_pairs={{0,121},{1,122},{2,123},{3,120},{4,125},{5,126},{6,127},{7,124},{8... | collective-permute-start | bytes 393224 | tf_op jit(solution)/shard_map/ppermute | solution.py:579
  85.5 12.3 %collective-permute-start.25 = (bf16[16,4096]{1,0:T(8,128)(2,1)S(1)}, bf16[16,4096]{1,0:T(8,128)(2,1)S(1)}, u32[]{:S(2)}, u32[]{:S(2)}) collective-permute-start(bf16[16,4096]{1,0:T(8,128)(2,1)S(1)} %get-tuple-element.104), channel_id=1, source_target_pairs={{0,122},{1,123},{2,120},{3,121},{4,126},{5,127},{6,124},{7,125},{8... | collective-permute-start | bytes 393224 | tf_op jit(solution)/shard_map/ppermute | solution.py:579
  103.6 16.6 %collective-permute-start.30 = (bf16[64,4096]{1,0:T(8,128)(2,1)S(1)}, bf16[64,4096]{1,0:T(8,128)(2,1)S(1)}, u32[]{:S(2)}, u32[]{:S(2)}) collective-permute-start(bf16[64,4096]{1,0:T(8,128)(2,1)S(1)} %get-tuple-element.106.refs_0_.refs_2_.refs_3_), channel_id=1, source_target_pairs={{0,4},{1,5},{2,6},{3,7},{4,0},{5,1},{6,2},{7,3},{8,12},{9,13},{10,... | collective-permute-start | bytes 1572872 | tf_op jit(solution)/shard_map/ppermute | solution.py:579
  105.8 13.8 %collective-permute-start.29 = (bf16[32,4096]{1,0:T(8,128)(2,1)S(1)}, bf16[32,4096]{1,0:T(8,128)(2,1)S(1)}, u32[]{:S(2)}, u32[]{:S(2)}) collective-permute-start(bf16[32,4096]{1,0:T(8,128)(2,1)S(1)} %get-tuple-element.105.refs_0_.x_ref), channel_id=1, source_target_pairs={{0,1},{1,2},{2,3},{3,0},{4,5},{5,6},{6,7},{7,4},{8,9},{9,10},{10,1... | collective-permute-start | bytes 786440 | tf_op jit(solution)/shard_map/ppermute | solution.py:579
  107.3 12.3 %collective-permute-start.28 = (bf16[32,4096]{1,0:T(8,128)(2,1)S(1)}, bf16[32,4096]{1,0:T(8,128)(2,1)S(1)}, u32[]{:S(2)}, u32[]{:S(2)}) collective-permute-start(bf16[32,4096]{1,0:T(8,128)(2,1)S(1)} %get-tuple-element.105.refs_0_.x_ref), channel_id=1, source_target_pairs={{0,2},{1,3},{2,0},{3,1},{4,6},{5,7},{6,4},{7,5},{8,10},{9,11},{10,... | collective-permute-start | bytes 786440 | tf_op jit(solution)/shard_map/ppermute | solution.py:579
  108.5 11.6 %collective-permute-start.27 = (bf16[32,4096]{1,0:T(8,128)(2,1)S(1)}, bf16[32,4096]{1,0:T(8,128)(2,1)S(1)}, u32[]{:S(2)}, u32[]{:S(2)}) collective-permute-start(bf16[32,4096]{1,0:T(8,128)(2,1)S(1)} %get-tuple-element.105.refs_0_.x_ref), channel_id=1, source_target_pairs={{0,3},{1,0},{2,1},{3,2},{4,7},{5,4},{6,5},{7,6},{8,11},{9,8},{10,9... | collective-permute-start | bytes 786440 | tf_op jit(solution)/shard_map/ppermute | solution.py:579
  122.9 14.4 %collective-permute-start.31 = (bf16[64,4096]{1,0:T(8,128)(2,1)S(1)}, bf16[64,4096]{1,0:T(8,128)(2,1)S(1)}, u32[]{:S(2)}, u32[]{:S(2)}) collective-permute-start(bf16[64,4096]{1,0:T(8,128)(2,1)S(1)} %get-tuple-element.108), channel_id=1, source_target_pairs={{0,4},{1,5},{2,6},{3,7},{4,0},{5,1},{6,2},{7,3},{8,12},{9,13},{10,... | collective-permute-start | bytes 1572872 | tf_op jit(solution)/shard_map/ppermute | solution.py:579
  128.2 16.3 %collective-permute-start.35 = (bf16[32,4352]{1,0:T(8,128)(2,1)S(1)}, bf16[32,4352]{1,0:T(8,128)(2,1)S(1)}, u32[]{:S(2)}, u32[]{:S(2)}) collective-permute-start(bf16[32,4352]{1,0:T(8,128)(2,1)S(1)} %get-tuple-element.125), channel_id=1, source_target_pairs={{0,1},{1,2},{2,3},{3,0},{4,5},{5,6},{6,7},{7,4},{8,9},{9,10},{10,1... | collective-permute-start | bytes 835592 | tf_op jit(solution)/shard_map/ppermute | solution.py:579
  128.5 15.9 %collective-permute-start.36 = (bf16[32,4352]{1,0:T(8,128)(2,1)S(1)}, bf16[32,4352]{1,0:T(8,128)(2,1)S(1)}, u32[]{:S(2)}, u32[]{:S(2)}) collective-permute-start(bf16[32,4352]{1,0:T(8,128)(2,1)S(1)} %get-tuple-element.126), channel_id=1, source_target_pairs={{0,2},{1,3},{2,0},{3,1},{4,6},{5,7},{6,4},{7,5},{8,10},{9,11},{10,... | collective-permute-start | bytes 835592 | tf_op jit(solution)/shard_map/ppermute | solution.py:579
  132.1 12.4 %collective-permute-start.37 = (bf16[32,4352]{1,0:T(8,128)(2,1)S(1)}, bf16[32,4352]{1,0:T(8,128)(2,1)S(1)}, u32[]{:S(2)}, u32[]{:S(2)}) collective-permute-start(bf16[32,4352]{1,0:T(8,128)(2,1)S(1)} %get-tuple-element.127), channel_id=1, source_target_pairs={{0,3},{1,0},{2,1},{3,2},{4,7},{5,4},{6,5},{7,6},{8,11},{9,8},{10,9... | collective-permute-start | bytes 835592 | tf_op jit(solution)/shard_map/ppermute | solution.py:579
  141.3 9.9 %collective-permute-start.33 = (bf16[16,4096]{1,0:T(8,128)(2,1)S(1)}, bf16[16,4096]{1,0:T(8,128)(2,1)S(1)}, u32[]{:S(2)}, u32[]{:S(2)}) collective-permute-start(bf16[16,4096]{1,0:T(8,128)(2,1)S(1)} %get-tuple-element.121), channel_id=1, source_target_pairs={{0,2},{1,3},{2,0},{3,1},{4,6},{5,7},{6,4},{7,5},{8,10},{9,11},{10,... | collective-permute-start | bytes 393224 | tf_op jit(solution)/shard_map/ppermute | solution.py:579
  148.1 9.5 %collective-permute-start.38 = (bf16[16,4608]{1,0:T(8,128)(2,1)S(1)}, bf16[16,4608]{1,0:T(8,128)(2,1)S(1)}, u32[]{:S(2)}, u32[]{:S(2)}) collective-permute-start(bf16[16,4608]{1,0:T(8,128)(2,1)S(1)} %get-tuple-element.129), channel_id=1, source_target_pairs={{0,4},{1,5},{2,6},{3,7},{4,0},{5,1},{6,2},{7,3},{8,12},{9,13},{10,... | collective-permute-start | bytes 442376 | tf_op jit(solution)/shard_map/ppermute | solution.py:579
  (22 other events, 121.8 us)

commit v4 on v3

--- a/solution.py
+++ b/solution.py
@@ -414,7 +414,8 @@
 
 def output_gradient_kernel(*refs):
     part = this_chunk()
-    refs[-1][...] = dot(stacked(refs[4:6]), stacked(refs[:4], part), TN).astype(jnp.bfloat16)
+    refs[-2][...] = dot(stacked(refs[4:6]), stacked(refs[:4], part), TN).astype(jnp.bfloat16)
+    refs[-1][...] = jnp.zeros(refs[-1].shape, jnp.float32)
 
 
 def estimate(flops, moved):
@@ -563,10 +564,13 @@
     return weight_gradient(
         output_gradient_kernel,
         (*grads, *attended),
-        (shaped((heads, width)),),
-        (pl.BlockSpec((heads, CHUNK), lambda i: (0, i)),),
+        (shaped((heads, width)), shaped((8, HEAD), jnp.float32)),
+        (
+            pl.BlockSpec((heads, CHUNK), lambda i: (0, i)),
+            pl.BlockSpec((8, HEAD), lambda i: (0, 0)),
+        ),
         after,
-    )[0]
+    )
 
 
 def moved(x, route):
@@ -730,12 +734,12 @@
     second_back_terms, second_grad_parts = backward_term(
         second_grads, second_states, weights, tables, first_grad_parts[0]
     )
-    grad_out = output_gradient(
+    grad_out, done = output_gradient(
         (*first_grads, *second_grads), (first_states[7], second_states[7]), second_grad_parts[0]
     )
     forward_own, *sent = small(
         halve_last_kernel, halve_shapes(second_terms[0], 0), second_terms[0],
-        across(second_terms[1]), grad_out, specs={2: ANYWHERE},
+        across(second_terms[1]), done, specs={2: ANYWHERE},
     )
     arrived = to_ahead(sent)
     forward_out = small(
@@ -745,7 +749,7 @@
         quarter_last_kernel,
         (*quarter_shapes(second_back_terms), shaped(second_grad_parts[0].shape, jnp.float32)),
         second_back_terms[0], *to_ahead(second_back_terms[1:]), second_grad_parts[0],
-        arrived[0], specs={RING + 1: ANYWHERE},
+        *arrived, specs={RING + 1 + index: ANYWHERE for index in range(len(arrived))},
     )
     grad_query, key_weight_gradient, value_weight_gradient = projection_gradients(
         (first_states[1], second_states[1]),

time: 159 us -> 160 us (level)
  waiting for transfers between devices: 47.4 us -> 51 us
  local copies, waits for them, and re-layouts: 11.5 us -> 9.31 us
    ppermute x39, waiting for transfers between devices: 47.4 us -> 51 us  [moved(): return lax.ppermute(x, ('pipe', 'tensor'), pairs)]
    unnamed x30 -> x28, local copies, waits for them, and re-layouts: 11.5 us -> 9.31 us
  transfers between devices with their start and end apart: 39 -> 39, of which waited for: 20 -> 22; matrix products, arithmetic and copies ran while one was open for 0% -> 0% of each run, Pallas kernels for 20% -> 20%
where the time goes in v4:
time: 160 us
  starting transfers between devices  62.7 us (39%)
  waiting for transfers between devices  51 us (32%)
  Pallas kernels  35.4 us (22%)
  local copies, waits for them, and re-layouts  9.31 us (6%)
    ppermute x39, starting transfers between devices, moved(): return lax.ppermute(x, ('pipe', 'tensor'), pairs)  62.7 us
    ppermute x39, waiting for transfers between devices, moved(): return lax.ppermute(x, ('pipe', 'tensor'), pairs)  51 us
    pallas_call x20, Pallas kernels, call(): pl.pallas_call(kernel, out_shape=out_shape, in_specs=[(specs or {}).get(i...  25.1 us
    pallas_call x2, Pallas kernels, weight_gradient(): pl.pallas_call(kernel, grid=(chunks,), out_shape=out_shape, in_specs=[WHO...  10.4 us
    unnamed x28, local copies, waits for them, and re-layouts  9.31 us
  transfers between devices with their start and end apart: 39, of which 22 were waited for; matrix products, arithmetic and copies ran while one was open for 0% of the time, Pallas kernels for 20%

profile of v4, /device:TPU:0, one launch (start us, length us, event | category | flops | bytes accessed | tf_op | source)
XLA Modules:
  0.0 159.9 jit_solution(5847543696068457795)
XLA Ops:
  0.6 3.4 %collective-permute-start = (bf16[16,4096]{1,0:T(8,128)(2,1)}, bf16[16,4096]{1,0:T(8,128)(2,1)S(1)}, u32[]{:S(2)}, u32[]{:S(2)}) collective-permute-start(bf16[16,4096]{1,0:T(8,128)(2,1)} %bitcast.44), channel_id=1, source_target_pairs={{0,4},{1,5},{2,6},{3,7},{4,0},{5,1},{6,2},{7,3},{8,12},{9,13},{10,... | collective-permute-start | bytes 393224 | tf_op jit(solution)/shard_map/ppermute | solution.py:583
  5.9 3.6 %collective-permute-start.10 = (bf16[16,4096]{1,0:T(8,128)(2,1)}, bf16[16,4096]{1,0:T(8,128)(2,1)S(1)}, u32[]{:S(2)}, u32[]{:S(2)}) collective-permute-start(bf16[16,4096]{1,0:T(8,128)(2,1)} %bitcast.47), channel_id=1, source_target_pairs={{0,2},{1,3},{2,0},{3,1},{4,6},{5,7},{6,4},{7,5},{8,10},{9,11},{10,... | collective-permute-start | bytes 393224 | tf_op jit(solution)/shard_map/ppermute | solution.py:583
  10.1 2.6 %sent_rows.1 = (bf16[32,4096]{1,0:T(8,128)(2,1)}, bf16[32,4096]{1,0:T(8,128)(2,1)}) custom-call(s32[3]{0:T(128)} %pad_add_fusion.place_ref, bf16[1,2,128,4096]{3,2,1,0:T(8,128)(2,1)} %stashed_ref.1), custom_call_target="tpu_custom_call" | custom-call | bytes 524288 | tf_op jit(solution)/shard_map/sent_rows/pallas_call | solution.py:431
  15.2 2.5 %collective-permute-start.2 = (bf16[32,4096]{1,0:T(8,128)(2,1)S(1)}, bf16[32,4096]{1,0:T(8,128)(2,1)S(1)}, u32[]{:S(2)}, u32[]{:S(2)}) collective-permute-start(bf16[32,4096]{1,0:T(8,128)(2,1)S(1)} %joined.3.refs_0_.x_ref), channel_id=1, source_target_pairs={{0,2},{1,3},{2,0},{3,1},{4,6},{5,7},{6,4},{7,5},{8,10},{9,11},{10,... | collective-permute-start | bytes 786440 | tf_op jit(solution)/shard_map/ppermute | solution.py:583
  22.1 2.2 %copy-done = bf16[1,4096,512]{2,1,0:T(8,128)(2,1)S(1)} copy-done((bf16[1,4096,512]{2,1,0:T(8,128)(2,1)S(1)}, bf16[1,4096,512]{2,1,0:T(8,128)(2,1)}, u32[]{:S(2)}) %copy-start) | copy-done | bytes 4194328
  24.3 2.2 %copy-done.2 = bf16[1,512,4096]{2,1,0:T(8,128)(2,1)S(1)} copy-done((bf16[1,512,4096]{2,1,0:T(8,128)(2,1)S(1)}, bf16[1,512,4096]{2,1,0:T(8,128)(2,1)}, u32[]{:S(2)}) %copy-start.2) | copy-done | bytes 4194328
  29.0 5.6 %collective-permute-done.9.refs_1_ = bf16[16,4096]{1,0:T(8,128)(2,1)S(1)} collective-permute-done((bf16[16,4096]{1,0:T(8,128)(2,1)}, bf16[16,4096]{1,0:T(8,128)(2,1)S(1)}, u32[]{:S(2)}, u32[]{:S(2)}) %collective-permute-start.9) | collective-permute-done | bytes 131104 | tf_op jit(solution)/shard_map/ppermute | solution.py:583
  36.9 3.6 %collective-permute-start.17 = (bf16[32,4096]{1,0:T(8,128)(2,1)S(1)}, bf16[32,4096]{1,0:T(8,128)(2,1)S(1)}, u32[]{:S(2)}, u32[]{:S(2)}) collective-permute-start(bf16[32,4096]{1,0:T(8,128)(2,1)S(1)} %collective-permute-done.15.refs_0_), channel_id=1, source_target_pairs={{0,2},{1,3},{2,0},{3,1},{4,6},{5,7},{6,4},{7,5},{8,10},{9,11},{10,... | collective-permute-start | bytes 786440 | tf_op jit(solution)/shard_map/ppermute | solution.py:583
  40.6 2.8 %layer_term.2 = (bf16[64,4096]{1,0:T(8,128)(2,1)S(1)}, bf16[64,4096]{1,0:T(8,128)(2,1)S(1)}) custom-call(bf16[32,4096]{1,0:T(8,128)(2,1)S(1)} %joined.3.refs_0_.x_ref, bf16[32,4096]{1,0:T(8,128)(2,1)S(1)} %collective-permute-done.1.refs_1_, bf16[32,4096]{1,0:T(8,128)(2,1)S(1)} %collective-permute-done.2.refs_2_, ...), custom_call_target="tpu_custom_call" | custom-call | flops 2684354560 | bytes 10485760 | tf_op jit(solution)/shard_map/layer_term/pallas_call | solution.py:431
  43.4 3.1 %collective-permute-done.18.refs_3_ = bf16[32,4096]{1,0:T(8,128)(2,1)S(1)} collective-permute-done((bf16[32,4096]{1,0:T(8,128)(2,1)S(1)}, bf16[32,4096]{1,0:T(8,128)(2,1)S(1)}, u32[]{:S(2)}, u32[]{:S(2)}) %collective-permute-start.18) | collective-permute-done | bytes 262176 | tf_op jit(solution)/shard_map/ppermute | solution.py:583
  48.2 3.9 %collective-permute-done.17.refs_2_ = bf16[32,4096]{1,0:T(8,128)(2,1)S(1)} collective-permute-done((bf16[32,4096]{1,0:T(8,128)(2,1)S(1)}, bf16[32,4096]{1,0:T(8,128)(2,1)S(1)}, u32[]{:S(2)}, u32[]{:S(2)}) %collective-permute-start.17) | collective-permute-done | bytes 262176 | tf_op jit(solution)/shard_map/ppermute | solution.py:583
  54.0 2.7 %collective-permute-done.14.refs_1_ = bf16[64,4096]{1,0:T(8,128)(2,1)S(1)} collective-permute-done((bf16[64,4096]{1,0:T(8,128)(2,1)S(1)}, bf16[64,4096]{1,0:T(8,128)(2,1)S(1)}, u32[]{:S(2)}, u32[]{:S(2)}) %collective-permute-start.14) | collective-permute-done | bytes 524320 | tf_op jit(solution)/shard_map/ppermute | solution.py:583
  56.7 4.2 %layer_gradient_term.2 = (bf16[32,4096]{1,0:T(8,128)(2,1)S(1)}, bf16[32,4096]{1,0:T(8,128)(2,1)S(1)}, bf16[32,4096]{1,0:T(8,128)(2,1)S(1)}, bf16[32,4096]{1,0:T(...) custom-call(bf16[64,4096]{1,0:T(8,128)(2,1)S(1)} %get-tuple-element., ...), custom_call_target="tpu_custom_call" | custom-call | flops 2684354560 | bytes 10485760 | tf_op jit(solution)/shard_map/layer_gradient_term/pallas_call | solution.py:431
  61.3 3.6 %collective-permute-start.20 = (bf16[32,4096]{1,0:T(8,128)(2,1)S(1)}, bf16[32,4096]{1,0:T(8,128)(2,1)S(1)}, u32[]{:S(2)}, u32[]{:S(2)}) collective-permute-start(bf16[32,4096]{1,0:T(8,128)(2,1)S(1)} %get-tuple-element.101), channel_id=1, source_target_pairs={{0,2},{1,3},{2,0},{3,1},{4,6},{5,7},{6,4},{7,5},{8,10},{9,11},{10,... | collective-permute-start | bytes 786440 | tf_op jit(solution)/shard_map/ppermute | solution.py:583
  64.8 2.3 %collective-permute-done.4.arrived_ref = bf16[64,4096]{1,0:T(8,128)(2,1)S(1)} collective-permute-done((bf16[64,4096]{1,0:T(8,128)(2,1)S(1)}, bf16[64,4096]{1,0:T(8,128)(2,1)S(1)}, u32[]{:S(2)}, u32[]{:S(2)}) %collective-permute-start.4) | collective-permute-done | bytes 524320 | tf_op jit(solution)/shard_map/ppermute | solution.py:583
  67.6 3.6 %collective-permute-start.7 = (bf16[48,4096]{1,0:T(8,128)(2,1)S(1)}, bf16[48,4096]{1,0:T(8,128)(2,1)S(1)}, u32[]{:S(2)}, u32[]{:S(2)}) collective-permute-start(bf16[48,4096]{1,0:T(8,128)(2,1)S(1)} %get-tuple-element.86), channel_id=1, source_target_pairs={{0,2},{1,3},{2,0},{3,1},{4,6},{5,7},{6,4},{7,5},{8,10},{9,11},{10,... | collective-permute-start | bytes 1179656 | tf_op jit(solution)/shard_map/ppermute | solution.py:583
  72.6 5.1 %collective-permute-done.20.two_ref = bf16[32,4096]{1,0:T(8,128)(2,1)S(1)} collective-permute-done((bf16[32,4096]{1,0:T(8,128)(2,1)S(1)}, bf16[32,4096]{1,0:T(8,128)(2,1)S(1)}, u32[]{:S(2)}, u32[]{:S(2)}) %collective-permute-start.20) | collective-permute-done | bytes 262176 | tf_op jit(solution)/shard_map/ppermute | solution.py:583
  80.0 4.6 %collective-permute-done.22.refs_1_ = bf16[16,4096]{1,0:T(8,128)(2,1)S(1)} collective-permute-done((bf16[16,4096]{1,0:T(8,128)(2,1)S(1)}, bf16[16,4096]{1,0:T(8,128)(2,1)S(1)}, u32[]{:S(2)}, u32[]{:S(2)}) %collective-permute-start.22) | collective-permute-done | bytes 131104 | tf_op jit(solution)/shard_map/ppermute | solution.py:583
  85.5 7.9 %collective-permute-start.25 = (bf16[16,4096]{1,0:T(8,128)(2,1)S(1)}, bf16[16,4096]{1,0:T(8,128)(2,1)S(1)}, u32[]{:S(2)}, u32[]{:S(2)}) collective-permute-start(bf16[16,4096]{1,0:T(8,128)(2,1)S(1)} %get-tuple-element.106), channel_id=1, source_target_pairs={{0,122},{1,123},{2,120},{3,121},{4,126},{5,127},{6,124},{7,125},{8... | collective-permute-start | bytes 393224 | tf_op jit(solution)/shard_map/ppermute | solution.py:583
  95.0 2.0 %collective-permute-start.13 = (bf16[16,4096]{1,0:T(8,128)(2,1)S(1)}, bf16[16,4096]{1,0:T(8,128)(2,1)S(1)}, u32[]{:S(2)}, u32[]{:S(2)}) collective-permute-start(bf16[16,4096]{1,0:T(8,128)(2,1)S(1)} %get-tuple-element.90), channel_id=1, source_target_pairs={{0,12},{1,13},{2,14},{3,15},{4,8},{5,9},{6,10},{7,11},{8,20},{9,21... | collective-permute-start | bytes 393224 | tf_op jit(solution)/shard_map/ppermute | solution.py:583
  99.8 3.3 %collective-permute-done.13.refs_1_ = bf16[16,4096]{1,0:T(8,128)(2,1)S(1)} collective-permute-done((bf16[16,4096]{1,0:T(8,128)(2,1)S(1)}, bf16[16,4096]{1,0:T(8,128)(2,1)S(1)}, u32[]{:S(2)}, u32[]{:S(2)}) %collective-permute-start.13) | collective-permute-done | bytes 131104 | tf_op jit(solution)/shard_map/ppermute | solution.py:583
  103.6 2.2 %collective-permute-start.30 = (bf16[64,4096]{1,0:T(8,128)(2,1)S(1)}, bf16[64,4096]{1,0:T(8,128)(2,1)S(1)}, u32[]{:S(2)}, u32[]{:S(2)}) collective-permute-start(bf16[64,4096]{1,0:T(8,128)(2,1)S(1)} %get-tuple-element.108.refs_0_.refs_2_.refs_3_), channel_id=1, source_target_pairs={{0,4},{1,5},{2,6},{3,7},{4,0},{5,1},{6,2},{7,3},{8,12},{9,13},{10,... | collective-permute-start | bytes 1572872 | tf_op jit(solution)/shard_map/ppermute | solution.py:583
  111.8 7.8 %collective-permute-done.29.refs_3_ = bf16[32,4096]{1,0:T(8,128)(2,1)S(1)} collective-permute-done((bf16[32,4096]{1,0:T(8,128)(2,1)S(1)}, bf16[32,4096]{1,0:T(8,128)(2,1)S(1)}, u32[]{:S(2)}, u32[]{:S(2)}) %collective-permute-start.29) | collective-permute-done | bytes 262176 | tf_op jit(solution)/shard_map/ppermute | solution.py:583
  120.2 2.8 %layer_term.3 = (bf16[64,4096]{1,0:T(8,128)(2,1)S(1)}, bf16[64,4096]{1,0:T(8,128)(2,1)S(1)}) custom-call(bf16[32,4096]{1,0:T(8,128)(2,1)S(1)} %get-tuple-element.107.refs_0_.x_ref, bf16[32,4096]{1,0:T(8,128)(2,1)S(1)} %collective-permute-done.27.refs_1_, bf16[32,4096]{1,0:T(8,128)(2,1)S(1)} %collective-permute-done.28.refs_2_, ...), custom_call_target="tpu_custom_call" | custom-call | flops 2684354560 | bytes 10485760 | tf_op jit(solution)/shard_map/layer_term/pallas_call | solution.py:431
  123.9 4.2 %layer_gradient_term.3 = (bf16[32,4096]{1,0:T(8,128)(2,1)S(1)}, bf16[32,4352]{1,0:T(8,128)(2,1)S(1)}, bf16[32,4352]{1,0:T(8,128)(2,1)S(1)}, bf16[32,4352]{1,0:T(...) custom-call(bf16[64,4096]{1,0:T(8,128)(2,1)S(1)} %get-tuple-element., ...), custom_call_target="tpu_custom_call" | custom-call | flops 2684354560 | bytes 10485760 | tf_op jit(solution)/shard_map/layer_gradient_term/pallas_call | solution.py:431
  128.5 3.6 %collective-permute-start.36 = (bf16[32,4352]{1,0:T(8,128)(2,1)S(1)}, bf16[32,4352]{1,0:T(8,128)(2,1)S(1)}, u32[]{:S(2)}, u32[]{:S(2)}) collective-permute-start(bf16[32,4352]{1,0:T(8,128)(2,1)S(1)} %get-tuple-element.129), channel_id=1, source_target_pairs={{0,2},{1,3},{2,0},{3,1},{4,6},{5,7},{6,4},{7,5},{8,10},{9,11},{10,... | collective-permute-start | bytes 835592 | tf_op jit(solution)/shard_map/ppermute | solution.py:583
  132.1 4.8 %output_gradient_kernel.1 = (bf16[512,4096]{1,0:T(8,128)(2,1)}, f32[8,128]{1,0:T(8,128)S(1)}) custom-call(bf16[64,4096]{1,0:T(8,128)(2,1)S(1)} %get-tuple-element.91.refs_0_.refs_3_, bf16[64,4096]{1,0:T(8,128)(2,1)S(1)} %collective-permute-done.14.refs_1_, bf16[64,4096]{1,0:T(8,128)(2,1)S(1)} %get-tuple-element.108.refs_0_.refs_2_.refs_3_, ...), custom_call_target="tpu_custom_call" | custom-call | flops 1074266112 | bytes 4196352 | tf_op jit(solution)/shard_map/output_gradient_kernel/pallas_call | solution.py:539
  139.1 3.1 %collective-permute-start.33 = (bf16[16,4096]{1,0:T(8,128)(2,1)S(1)}, bf16[16,4096]{1,0:T(8,128)(2,1)S(1)}, u32[]{:S(2)}, u32[]{:S(2)}) collective-permute-start(bf16[16,4096]{1,0:T(8,128)(2,1)S(1)} %get-tuple-element.124), channel_id=1, source_target_pairs={{0,2},{1,3},{2,0},{3,1},{4,6},{5,7},{6,4},{7,5},{8,10},{9,11},{10,... | collective-permute-start | bytes 393224 | tf_op jit(solution)/shard_map/ppermute | solution.py:583
  142.2 3.4 %collective-permute-done.36.two_ref = bf16[32,4352]{1,0:T(8,128)(2,1)S(1)} collective-permute-done((bf16[32,4352]{1,0:T(8,128)(2,1)S(1)}, bf16[32,4352]{1,0:T(8,128)(2,1)S(1)}, u32[]{:S(2)}, u32[]{:S(2)}) %collective-permute-start.36) | collective-permute-done | bytes 278560 | tf_op jit(solution)/shard_map/ppermute | solution.py:583
  145.7 2.3 %collective-permute-done.32.one_ref.rest_0_ = bf16[16,4096]{1,0:T(8,128)(2,1)S(1)} collective-permute-done((bf16[16,4096]{1,0:T(8,128)(2,1)S(1)}, bf16[16,4096]{1,0:T(8,128)(2,1)S(1)}, u32[]{:S(2)}, u32[]{:S(2)}) %collective-permute-start.32) | collective-permute-done | bytes 131104 | tf_op jit(solution)/shard_map/ppermute | solution.py:583
  149.5 3.2 %collective-permute-start.38 = (bf16[16,4608]{1,0:T(8,128)(2,1)S(1)}, bf16[16,4608]{1,0:T(8,128)(2,1)S(1)}, u32[]{:S(2)}, u32[]{:S(2)}) collective-permute-start(bf16[16,4608]{1,0:T(8,128)(2,1)S(1)} %get-tuple-element.132), channel_id=1, source_target_pairs={{0,4},{1,5},{2,6},{3,7},{4,0},{5,1},{6,2},{7,3},{8,12},{9,13},{10,... | collective-permute-start | bytes 442376 | tf_op jit(solution)/shard_map/ppermute | solution.py:583
  153.5 5.6 %projection_gradient_kernel.1 = (bf16[4096,512]{1,0:T(8,128)(2,1)}, bf16[4096,128]{1,0:T(8,128)(2,1)}, bf16[4096,128]{1,0:T(8,128)(2,1)}) custom-call(bf16[128,4096]{1,0:T(8,128)(2,1)S(1)} %get-tuple-element.136.refs_0_, bf16[128,4096]{1,0:T(8,128)(2,1)S(1)} %get-tuple-element.137.refs_1_, bf16[128,512]{1,0:T(8,128)(2,1)S(1)} %get-tuple-element.138.refs_2_, ...), custom_call_target="tpu_custom_call" | custom-call | flops 1610612736 | bytes 6291456 | tf_op jit(solution)/shard_map/projection_gradient_kernel/pallas_call | solution.py:539
  (97 shorter events, 41.4 us)
Async XLA Ops:
  0.6 13.6 %collective-permute-start = (bf16[16,4096]{1,0:T(8,128)(2,1)}, bf16[16,4096]{1,0:T(8,128)(2,1)S(1)}, u32[]{:S(2)}, u32[]{:S(2)}) collective-permute-start(bf16[16,4096]{1,0:T(8,128)(2,1)} %bitcast.44), channel_id=1, source_target_pairs={{0,4},{1,5},{2,6},{3,7},{4,0},{5,1},{6,2},{7,3},{8,12},{9,13},{10,... | collective-permute-start | bytes 393224 | tf_op jit(solution)/shard_map/ppermute | solution.py:583
  4.0 13.7 %collective-permute-start.11 = (bf16[16,4096]{1,0:T(8,128)(2,1)}, bf16[16,4096]{1,0:T(8,128)(2,1)S(1)}, u32[]{:S(2)}, u32[]{:S(2)}) collective-permute-start(bf16[16,4096]{1,0:T(8,128)(2,1)} %bitcast.46), channel_id=1, source_target_pairs={{0,1},{1,2},{2,3},{3,0},{4,5},{5,6},{6,7},{7,4},{8,9},{9,10},{10,1... | collective-permute-start | bytes 393224 | tf_op jit(solution)/shard_map/ppermute | solution.py:583
  5.9 12.6 %collective-permute-start.10 = (bf16[16,4096]{1,0:T(8,128)(2,1)}, bf16[16,4096]{1,0:T(8,128)(2,1)S(1)}, u32[]{:S(2)}, u32[]{:S(2)}) collective-permute-start(bf16[16,4096]{1,0:T(8,128)(2,1)} %bitcast.47), channel_id=1, source_target_pairs={{0,2},{1,3},{2,0},{3,1},{4,6},{5,7},{6,4},{7,5},{8,10},{9,11},{10,... | collective-permute-start | bytes 393224 | tf_op jit(solution)/shard_map/ppermute | solution.py:583
  12.7 24.0 %collective-permute-start.15 = (bf16[32,4096]{1,0:T(8,128)(2,1)}, bf16[32,4096]{1,0:T(8,128)(2,1)S(1)}, u32[]{:S(2)}, u32[]{:S(2)}) collective-permute-start(bf16[32,4096]{1,0:T(8,128)(2,1)} %get-tuple-element.92), channel_id=1, source_target_pairs={{0,120},{1,121},{2,122},{3,123},{4,124},{5,125},{6,126},{7,127},{8... | collective-permute-start | bytes 786440 | tf_op jit(solution)/shard_map/ppermute | solution.py:583
  15.1 21.7 %collective-permute-start.3 = (bf16[32,4096]{1,0:T(8,128)(2,1)S(1)}, bf16[32,4096]{1,0:T(8,128)(2,1)S(1)}, u32[]{:S(2)}, u32[]{:S(2)}) collective-permute-start(bf16[32,4096]{1,0:T(8,128)(2,1)S(1)} %joined.3.refs_0_.x_ref), channel_id=1, source_target_pairs={{0,1},{1,2},{2,3},{3,0},{4,5},{5,6},{6,7},{7,4},{8,9},{9,10},{10,1... | collective-permute-start | bytes 786440 | tf_op jit(solution)/shard_map/ppermute | solution.py:583
  15.2 25.2 %collective-permute-start.2 = (bf16[32,4096]{1,0:T(8,128)(2,1)S(1)}, bf16[32,4096]{1,0:T(8,128)(2,1)S(1)}, u32[]{:S(2)}, u32[]{:S(2)}) collective-permute-start(bf16[32,4096]{1,0:T(8,128)(2,1)S(1)} %joined.3.refs_0_.x_ref), channel_id=1, source_target_pairs={{0,2},{1,3},{2,0},{3,1},{4,6},{5,7},{6,4},{7,5},{8,10},{9,11},{10,... | collective-permute-start | bytes 786440 | tf_op jit(solution)/shard_map/ppermute | solution.py:583
  17.7 22.8 %collective-permute-start.1 = (bf16[32,4096]{1,0:T(8,128)(2,1)S(1)}, bf16[32,4096]{1,0:T(8,128)(2,1)S(1)}, u32[]{:S(2)}, u32[]{:S(2)}) collective-permute-start(bf16[32,4096]{1,0:T(8,128)(2,1)S(1)} %joined.3.refs_0_.x_ref), channel_id=1, source_target_pairs={{0,3},{1,0},{2,1},{3,2},{4,7},{5,4},{6,5},{7,6},{8,11},{9,8},{10,9... | collective-permute-start | bytes 786440 | tf_op jit(solution)/shard_map/ppermute | solution.py:583
  18.5 16.2 %collective-permute-start.9 = (bf16[16,4096]{1,0:T(8,128)(2,1)}, bf16[16,4096]{1,0:T(8,128)(2,1)S(1)}, u32[]{:S(2)}, u32[]{:S(2)}) collective-permute-start(bf16[16,4096]{1,0:T(8,128)(2,1)} %bitcast.48), channel_id=1, source_target_pairs={{0,3},{1,0},{2,1},{3,2},{4,7},{5,4},{6,5},{7,6},{8,11},{9,8},{10,9... | collective-permute-start | bytes 393224 | tf_op jit(solution)/shard_map/ppermute | solution.py:583
  34.7 22.0 %collective-permute-start.14 = (bf16[64,4096]{1,0:T(8,128)(2,1)S(1)}, bf16[64,4096]{1,0:T(8,128)(2,1)S(1)}, u32[]{:S(2)}, u32[]{:S(2)}) collective-permute-start(bf16[64,4096]{1,0:T(8,128)(2,1)S(1)} %get-tuple-element.91.refs_0_.refs_3_), channel_id=1, source_target_pairs={{0,4},{1,5},{2,6},{3,7},{4,0},{5,1},{6,2},{7,3},{8,12},{9,13},{10,... | collective-permute-start | bytes 1572872 | tf_op jit(solution)/shard_map/ppermute | solution.py:583
  36.7 9.8 %collective-permute-start.18 = (bf16[32,4096]{1,0:T(8,128)(2,1)S(1)}, bf16[32,4096]{1,0:T(8,128)(2,1)S(1)}, u32[]{:S(2)}, u32[]{:S(2)}) collective-permute-start(bf16[32,4096]{1,0:T(8,128)(2,1)S(1)} %collective-permute-done.15.refs_0_), channel_id=1, source_target_pairs={{0,1},{1,2},{2,3},{3,0},{4,5},{5,6},{6,7},{7,4},{8,9},{9,10},{10,1... | collective-permute-start | bytes 786440 | tf_op jit(solution)/shard_map/ppermute | solution.py:583
  36.9 15.2 %collective-permute-start.17 = (bf16[32,4096]{1,0:T(8,128)(2,1)S(1)}, bf16[32,4096]{1,0:T(8,128)(2,1)S(1)}, u32[]{:S(2)}, u32[]{:S(2)}) collective-permute-start(bf16[32,4096]{1,0:T(8,128)(2,1)S(1)} %collective-permute-done.15.refs_0_), channel_id=1, source_target_pairs={{0,2},{1,3},{2,0},{3,1},{4,6},{5,7},{6,4},{7,5},{8,10},{9,11},{10,... | collective-permute-start | bytes 786440 | tf_op jit(solution)/shard_map/ppermute | solution.py:583
  40.5 11.7 %collective-permute-start.16 = (bf16[32,4096]{1,0:T(8,128)(2,1)S(1)}, bf16[32,4096]{1,0:T(8,128)(2,1)S(1)}, u32[]{:S(2)}, u32[]{:S(2)}) collective-permute-start(bf16[32,4096]{1,0:T(8,128)(2,1)S(1)} %collective-permute-done.15.refs_0_), channel_id=1, source_target_pairs={{0,3},{1,0},{2,1},{3,2},{4,7},{5,4},{6,5},{7,6},{8,11},{9,8},{10,9... | collective-permute-start | bytes 786440 | tf_op jit(solution)/shard_map/ppermute | solution.py:583
  40.5 24.3 %collective-permute-start.5 = (bf16[32,4096]{1,0:T(8,128)(2,1)S(1)}, bf16[32,4096]{1,0:T(8,128)(2,1)S(1)}, u32[]{:S(2)}, u32[]{:S(2)}) collective-permute-start(bf16[32,4096]{1,0:T(8,128)(2,1)S(1)} %copy-done.13), channel_id=1, source_target_pairs={{0,120},{1,121},{2,122},{3,123},{4,124},{5,125},{6,126},{7,127},{8... | collective-permute-start | bytes 786440 | tf_op jit(solution)/shard_map/ppermute | solution.py:583
  46.5 20.6 %collective-permute-start.4 = (bf16[64,4096]{1,0:T(8,128)(2,1)S(1)}, bf16[64,4096]{1,0:T(8,128)(2,1)S(1)}, u32[]{:S(2)}, u32[]{:S(2)}) collective-permute-start(bf16[64,4096]{1,0:T(8,128)(2,1)S(1)} %get-tuple-element.82), channel_id=1, source_target_pairs={{0,4},{1,5},{2,6},{3,7},{4,0},{5,1},{6,2},{7,3},{8,12},{9,13},{10,... | collective-permute-start | bytes 1572872 | tf_op jit(solution)/shard_map/ppermute | solution.py:583
  61.0 10.3 %collective-permute-start.19 = (bf16[32,4096]{1,0:T(8,128)(2,1)S(1)}, bf16[32,4096]{1,0:T(8,128)(2,1)S(1)}, u32[]{:S(2)}, u32[]{:S(2)}) collective-permute-start(bf16[32,4096]{1,0:T(8,128)(2,1)S(1)} %get-tuple-element.100), channel_id=1, source_target_pairs={{0,1},{1,2},{2,3},{3,0},{4,5},{5,6},{6,7},{7,4},{8,9},{9,10},{10,1... | collective-permute-start | bytes 786440 | tf_op jit(solution)/shard_map/ppermute | solution.py:583
  61.3 16.4 %collective-permute-start.20 = (bf16[32,4096]{1,0:T(8,128)(2,1)S(1)}, bf16[32,4096]{1,0:T(8,128)(2,1)S(1)}, u32[]{:S(2)}, u32[]{:S(2)}) collective-permute-start(bf16[32,4096]{1,0:T(8,128)(2,1)S(1)} %get-tuple-element.101), channel_id=1, source_target_pairs={{0,2},{1,3},{2,0},{3,1},{4,6},{5,7},{6,4},{7,5},{8,10},{9,11},{10,... | collective-permute-start | bytes 786440 | tf_op jit(solution)/shard_map/ppermute | solution.py:583
  64.8 13.1 %collective-permute-start.21 = (bf16[32,4096]{1,0:T(8,128)(2,1)S(1)}, bf16[32,4096]{1,0:T(8,128)(2,1)S(1)}, u32[]{:S(2)}, u32[]{:S(2)}) collective-permute-start(bf16[32,4096]{1,0:T(8,128)(2,1)S(1)} %get-tuple-element.102), channel_id=1, source_target_pairs={{0,3},{1,0},{2,1},{3,2},{4,7},{5,4},{6,5},{7,6},{8,11},{9,8},{10,9... | collective-permute-start | bytes 786440 | tf_op jit(solution)/shard_map/ppermute | solution.py:583
  67.3 26.1 %collective-permute-start.6 = (bf16[48,4096]{1,0:T(8,128)(2,1)S(1)}, bf16[48,4096]{1,0:T(8,128)(2,1)S(1)}, u32[]{:S(2)}, u32[]{:S(2)}) collective-permute-start(bf16[48,4096]{1,0:T(8,128)(2,1)S(1)} %get-tuple-element.85), channel_id=1, source_target_pairs={{0,1},{1,2},{2,3},{3,0},{4,5},{5,6},{6,7},{7,4},{8,9},{9,10},{10,1... | collective-permute-start | bytes 1179656 | tf_op jit(solution)/shard_map/ppermute | solution.py:583
  67.6 26.8 %collective-permute-start.7 = (bf16[48,4096]{1,0:T(8,128)(2,1)S(1)}, bf16[48,4096]{1,0:T(8,128)(2,1)S(1)}, u32[]{:S(2)}, u32[]{:S(2)}) collective-permute-start(bf16[48,4096]{1,0:T(8,128)(2,1)S(1)} %get-tuple-element.86), channel_id=1, source_target_pairs={{0,2},{1,3},{2,0},{3,1},{4,6},{5,7},{6,4},{7,5},{8,10},{9,11},{10,... | collective-permute-start | bytes 1179656 | tf_op jit(solution)/shard_map/ppermute | solution.py:583
  71.3 23.1 %collective-permute-start.8 = (bf16[48,4096]{1,0:T(8,128)(2,1)S(1)}, bf16[48,4096]{1,0:T(8,128)(2,1)S(1)}, u32[]{:S(2)}, u32[]{:S(2)}) collective-permute-start(bf16[48,4096]{1,0:T(8,128)(2,1)S(1)} %get-tuple-element.87), channel_id=1, source_target_pairs={{0,3},{1,0},{2,1},{3,2},{4,7},{5,4},{6,5},{7,6},{8,11},{9,8},{10,9... | collective-permute-start | bytes 1179656 | tf_op jit(solution)/shard_map/ppermute | solution.py:583
  85.4 11.6 %collective-permute-start.26 = (bf16[16,4096]{1,0:T(8,128)(2,1)S(1)}, bf16[16,4096]{1,0:T(8,128)(2,1)S(1)}, u32[]{:S(2)}, u32[]{:S(2)}) collective-permute-start(bf16[16,4096]{1,0:T(8,128)(2,1)S(1)} %get-tuple-element.106), channel_id=1, source_target_pairs={{0,121},{1,122},{2,123},{3,120},{4,125},{5,126},{6,127},{7,124},{8... | collective-permute-start | bytes 393224 | tf_op jit(solution)/shard_map/ppermute | solution.py:583
  85.5 12.3 %collective-permute-start.25 = (bf16[16,4096]{1,0:T(8,128)(2,1)S(1)}, bf16[16,4096]{1,0:T(8,128)(2,1)S(1)}, u32[]{:S(2)}, u32[]{:S(2)}) collective-permute-start(bf16[16,4096]{1,0:T(8,128)(2,1)S(1)} %get-tuple-element.106), channel_id=1, source_target_pairs={{0,122},{1,123},{2,120},{3,121},{4,126},{5,127},{6,124},{7,125},{8... | collective-permute-start | bytes 393224 | tf_op jit(solution)/shard_map/ppermute | solution.py:583
  103.6 16.6 %collective-permute-start.30 = (bf16[64,4096]{1,0:T(8,128)(2,1)S(1)}, bf16[64,4096]{1,0:T(8,128)(2,1)S(1)}, u32[]{:S(2)}, u32[]{:S(2)}) collective-permute-start(bf16[64,4096]{1,0:T(8,128)(2,1)S(1)} %get-tuple-element.108.refs_0_.refs_2_.refs_3_), channel_id=1, source_target_pairs={{0,4},{1,5},{2,6},{3,7},{4,0},{5,1},{6,2},{7,3},{8,12},{9,13},{10,... | collective-permute-start | bytes 1572872 | tf_op jit(solution)/shard_map/ppermute | solution.py:583
  105.8 13.8 %collective-permute-start.29 = (bf16[32,4096]{1,0:T(8,128)(2,1)S(1)}, bf16[32,4096]{1,0:T(8,128)(2,1)S(1)}, u32[]{:S(2)}, u32[]{:S(2)}) collective-permute-start(bf16[32,4096]{1,0:T(8,128)(2,1)S(1)} %get-tuple-element.107.refs_0_.x_ref), channel_id=1, source_target_pairs={{0,1},{1,2},{2,3},{3,0},{4,5},{5,6},{6,7},{7,4},{8,9},{9,10},{10,1... | collective-permute-start | bytes 786440 | tf_op jit(solution)/shard_map/ppermute | solution.py:583
  107.3 12.3 %collective-permute-start.28 = (bf16[32,4096]{1,0:T(8,128)(2,1)S(1)}, bf16[32,4096]{1,0:T(8,128)(2,1)S(1)}, u32[]{:S(2)}, u32[]{:S(2)}) collective-permute-start(bf16[32,4096]{1,0:T(8,128)(2,1)S(1)} %get-tuple-element.107.refs_0_.x_ref), channel_id=1, source_target_pairs={{0,2},{1,3},{2,0},{3,1},{4,6},{5,7},{6,4},{7,5},{8,10},{9,11},{10,... | collective-permute-start | bytes 786440 | tf_op jit(solution)/shard_map/ppermute | solution.py:583
  108.5 11.6 %collective-permute-start.27 = (bf16[32,4096]{1,0:T(8,128)(2,1)S(1)}, bf16[32,4096]{1,0:T(8,128)(2,1)S(1)}, u32[]{:S(2)}, u32[]{:S(2)}) collective-permute-start(bf16[32,4096]{1,0:T(8,128)(2,1)S(1)} %get-tuple-element.107.refs_0_.x_ref), channel_id=1, source_target_pairs={{0,3},{1,0},{2,1},{3,2},{4,7},{5,4},{6,5},{7,6},{8,11},{9,8},{10,9... | collective-permute-start | bytes 786440 | tf_op jit(solution)/shard_map/ppermute | solution.py:583
  122.9 14.4 %collective-permute-start.31 = (bf16[64,4096]{1,0:T(8,128)(2,1)S(1)}, bf16[64,4096]{1,0:T(8,128)(2,1)S(1)}, u32[]{:S(2)}, u32[]{:S(2)}) collective-permute-start(bf16[64,4096]{1,0:T(8,128)(2,1)S(1)} %get-tuple-element.110), channel_id=1, source_target_pairs={{0,4},{1,5},{2,6},{3,7},{4,0},{5,1},{6,2},{7,3},{8,12},{9,13},{10,... | collective-permute-start | bytes 1572872 | tf_op jit(solution)/shard_map/ppermute | solution.py:583
  128.2 14.1 %collective-permute-start.35 = (bf16[32,4352]{1,0:T(8,128)(2,1)S(1)}, bf16[32,4352]{1,0:T(8,128)(2,1)S(1)}, u32[]{:S(2)}, u32[]{:S(2)}) collective-permute-start(bf16[32,4352]{1,0:T(8,128)(2,1)S(1)} %get-tuple-element.128), channel_id=1, source_target_pairs={{0,1},{1,2},{2,3},{3,0},{4,5},{5,6},{6,7},{7,4},{8,9},{9,10},{10,1... | collective-permute-start | bytes 835592 | tf_op jit(solution)/shard_map/ppermute | solution.py:583
  128.5 17.2 %collective-permute-start.36 = (bf16[32,4352]{1,0:T(8,128)(2,1)S(1)}, bf16[32,4352]{1,0:T(8,128)(2,1)S(1)}, u32[]{:S(2)}, u32[]{:S(2)}) collective-permute-start(bf16[32,4352]{1,0:T(8,128)(2,1)S(1)} %get-tuple-element.129), channel_id=1, source_target_pairs={{0,2},{1,3},{2,0},{3,1},{4,6},{5,7},{6,4},{7,5},{8,10},{9,11},{10,... | collective-permute-start | bytes 835592 | tf_op jit(solution)/shard_map/ppermute | solution.py:583
  132.1 13.6 %collective-permute-start.37 = (bf16[32,4352]{1,0:T(8,128)(2,1)S(1)}, bf16[32,4352]{1,0:T(8,128)(2,1)S(1)}, u32[]{:S(2)}, u32[]{:S(2)}) collective-permute-start(bf16[32,4352]{1,0:T(8,128)(2,1)S(1)} %get-tuple-element.130), channel_id=1, source_target_pairs={{0,3},{1,0},{2,1},{3,2},{4,7},{5,4},{6,5},{7,6},{8,11},{9,8},{10,9... | collective-permute-start | bytes 835592 | tf_op jit(solution)/shard_map/ppermute | solution.py:583
  137.5 10.4 %collective-permute-start.32 = (bf16[16,4096]{1,0:T(8,128)(2,1)S(1)}, bf16[16,4096]{1,0:T(8,128)(2,1)S(1)}, u32[]{:S(2)}, u32[]{:S(2)}) collective-permute-start(bf16[16,4096]{1,0:T(8,128)(2,1)S(1)} %get-tuple-element.123), channel_id=1, source_target_pairs={{0,1},{1,2},{2,3},{3,0},{4,5},{5,6},{6,7},{7,4},{8,9},{9,10},{10,1... | collective-permute-start | bytes 393224 | tf_op jit(solution)/shard_map/ppermute | solution.py:583
  139.1 10.3 %collective-permute-start.33 = (bf16[16,4096]{1,0:T(8,128)(2,1)S(1)}, bf16[16,4096]{1,0:T(8,128)(2,1)S(1)}, u32[]{:S(2)}, u32[]{:S(2)}) collective-permute-start(bf16[16,4096]{1,0:T(8,128)(2,1)S(1)} %get-tuple-element.124), channel_id=1, source_target_pairs={{0,2},{1,3},{2,0},{3,1},{4,6},{5,7},{6,4},{7,5},{8,10},{9,11},{10,... | collective-permute-start | bytes 393224 | tf_op jit(solution)/shard_map/ppermute | solution.py:583
  (21 other events, 121.2 us)
